TPU v7x, 256 devices: a whole 4x4x8 slice. The times are simulated.
256 devices in a mesh: ctx: 64 (over z, y, x_hi), tp: 4 (over x_lo, core).
Axes of the slice: x: 4 (x_hi: 2, x_lo: 2; x = x_hi * 2 + x_lo), y: 4, z: 8, core: 2. Of those that a mesh axis runs over, the one named last changes fastest.
Arguments:
- inputs: bfloat16 [8192, 4096], P('ctx', 'tp'), may hold values from -6 to 6
- out_grad: bfloat16 [8192, 4096], P('ctx', 'tp'), may hold values from -6 to 6
- w_query: bfloat16 [4096, 2048], P(None, 'tp'), may hold values from -0.09375 to 0.09375
- key_weight: bfloat16 [4096, 512], P(None, 'tp'), may hold values from -0.09375 to 0.09375
- value_weight: bfloat16 [4096, 512], P(None, 'tp'), may hold values from -0.09375 to 0.09375
- w_output: bfloat16 [2048, 4096], P('tp'), may hold values from -0.09375 to 0.09375
- times: int32 [8192], replicated, may hold values from 0 to 8191, as said below
Outputs:
- input_grad: bfloat16 [8192, 4096], P('ctx', 'tp')
- gradient_keys: bfloat16 [8192, 512], P('ctx', 'tp')
- gradient_values: bfloat16 [8192, 512], P('ctx', 'tp')
Inputs may be any that keep to these rules, and one draw needn't show every extreme that they name: Each event's time is its position in the sequence or one less (the first and last events have exactly their positions), so times are nondecreasing and rise by at most 2 from one event to the next; equal times see each other.
All inputs are finite; a program needn't handle non-finite values.
Results may differ from a plain program's by a relative error of at most 0.02.
Values may be sent and summed in bfloat16 or wider, within the bound.
No kernel may reach another device: no remote copies, remote signals or barrier semaphores. Data moves between devices by JAX's collectives and lax.ppermute only.
A program may use at most 128 MiB of HBM per device.

v0:
```python
import math

import jax
import jax.numpy as jnp
from jax import lax
from jax.sharding import PartitionSpec as P

HEAD_SIZE = 128


NEG_FILL = -1e30


def contract_last(left, right):
    return lax.dot_general(
        left, right, (((1,), (1,)), ((), ())), preferred_element_type=jnp.float32
    )


def contract_first(left, right):
    return lax.dot_general(
        left, right, (((0,), (0,)), ((), ())), preferred_element_type=jnp.float32
    )


def block_terms(
    query_rows,
    grad_rows,
    lse_rows,
    delta_rows,
    row_times,
    key_block,
    value_block,
    key_times,
    factor,
):
    scores = contract_last(query_rows, key_block) * factor
    visible = key_times[None, :] <= row_times[:, None]
    prob = jnp.where(visible, jnp.exp(scores - lse_rows[:, None]), 0.0)
    prob_low = prob.astype(jnp.bfloat16)
    prob_grad = contract_last(grad_rows, value_block)
    score_grad = (prob * (prob_grad - delta_rows[:, None])).astype(jnp.bfloat16)
    return (prob_low, score_grad)


def local(inputs, out_grad, w_query, key_weight, value_weight, w_output, times):
    factor = HEAD_SIZE ** (-0.5)
    tok_dev = inputs.shape[0]
    full_inputs, full_grad = (
        lax.all_gather(inputs, "tp", axis=1, tiled=True),
        lax.all_gather(out_grad, "tp", axis=1, tiled=True),
    )
    ctx_rank = lax.axis_index("ctx")
    my_times = lax.dynamic_slice_in_dim(times, ctx_rank * tok_dev, tok_dev, 0)
    queries = jnp.dot(full_inputs, w_query, preferred_element_type=jnp.float32).astype(jnp.bfloat16)
    keys_own = jnp.dot(full_inputs, key_weight, preferred_element_type=jnp.float32).astype(
        jnp.bfloat16
    )
    values_own = jnp.dot(full_inputs, value_weight, preferred_element_type=jnp.float32).astype(
        jnp.bfloat16
    )
    attn_grad = contract_last(full_grad, w_output).astype(jnp.bfloat16)
    heads_dev = queries.shape[1] // HEAD_SIZE
    row_count = tok_dev * heads_dev
    query_rows = queries.reshape(row_count, HEAD_SIZE)
    grad_rows = attn_grad.reshape(row_count, HEAD_SIZE)
    row_times = jnp.repeat(my_times, heads_dev)
    keys_all, values_all = (
        lax.all_gather(keys_own, "ctx", axis=0, tiled=True),
        lax.all_gather(values_own, "ctx", axis=0, tiled=True),
    )
    seq_total = keys_all.shape[0]
    key_span = math.gcd(512, seq_total)
    block_ids = jnp.arange(seq_total // key_span, dtype=jnp.int32)

    def key_slices(block_index):
        first_row = block_index * key_span
        key_block = lax.dynamic_slice_in_dim(keys_all, first_row, key_span, 0)
        value_block = lax.dynamic_slice_in_dim(values_all, first_row, key_span, 0)
        key_times = lax.dynamic_slice_in_dim(times, first_row, key_span, 0)
        return (key_block, value_block, key_times)

    count = query_rows.shape[0]

    def stats_step(state_pair, block_index):
        key_block, value_block, key_times = key_slices(block_index)
        row_top, row_norm = state_pair
        scores = contract_last(query_rows, key_block) * factor
        visible = key_times[None, :] <= row_times[:, None]
        new_top = jnp.maximum(row_top, jnp.max(jnp.where(visible, scores, NEG_FILL), axis=1))
        fresh = jnp.sum(jnp.where(visible, jnp.exp(scores - new_top[:, None]), 0.0), axis=1)
        return ((new_top, row_norm * jnp.exp(row_top - new_top) + fresh), None)

    start_pair = (jnp.full((count,), NEG_FILL, jnp.float32), jnp.zeros((count,), jnp.float32))
    (row_top, row_norm), unused = lax.scan(stats_step, start_pair, block_ids)
    rows_lse = row_top + jnp.log(row_norm)

    def out_step(out_total, block_index):
        key_block, value_block, key_times = key_slices(block_index)
        scores = contract_last(query_rows, key_block) * factor
        visible = key_times[None, :] <= row_times[:, None]
        prob_low = jnp.where(visible, jnp.exp(scores - rows_lse[:, None]), 0.0).astype(jnp.bfloat16)
        return (
            out_total + jnp.dot(prob_low, value_block, preferred_element_type=jnp.float32),
            None,
        )

    out_total, unused = lax.scan(out_step, jnp.zeros((count, HEAD_SIZE), jnp.float32), block_ids)
    attn_out = out_total.astype(jnp.bfloat16)
    rows_delta = jnp.sum(grad_rows.astype(jnp.float32) * attn_out.astype(jnp.float32), axis=1)

    def grad_step(query_sum, block_index):
        key_block, value_block, key_times = key_slices(block_index)
        prob_low, score_grad = block_terms(
            query_rows,
            grad_rows,
            rows_lse,
            rows_delta,
            row_times,
            key_block,
            value_block,
            key_times,
            factor,
        )
        new_sum = query_sum + jnp.dot(score_grad, key_block, preferred_element_type=jnp.float32)
        stacked = jnp.concatenate(
            [contract_first(score_grad, query_rows), contract_first(prob_low, grad_rows)], axis=1
        )
        return (new_sum, stacked)

    query_sum, key_terms = lax.scan(
        grad_step, jnp.zeros((count, HEAD_SIZE), jnp.float32), block_ids
    )
    lse_rows, delta_rows, query_sum, key_terms = (rows_lse, rows_delta, query_sum, key_terms)
    key_terms = key_terms.reshape(seq_total, 2 * HEAD_SIZE)
    own_grads = lax.psum_scatter(key_terms, "ctx", scatter_dimension=0, tiled=True)
    gradient_keys = (own_grads[:, :HEAD_SIZE] * factor).astype(jnp.bfloat16)
    gradient_values = own_grads[:, HEAD_SIZE:].astype(jnp.bfloat16)
    gradient_queries = (
        (query_sum * factor).astype(jnp.bfloat16).reshape(tok_dev, heads_dev * HEAD_SIZE)
    )
    partial_value = (
        contract_last(gradient_queries, w_query)
        + contract_last(gradient_keys, key_weight)
        + contract_last(gradient_values, value_weight)
    )
    input_grad = lax.psum_scatter(
        partial_value.astype(jnp.bfloat16), "tp", scatter_dimension=1, tiled=True
    )
    return (input_grad, gradient_keys, gradient_values)


def solution(mesh):
    in_specs = (
        P("ctx", "tp"),
        P("ctx", "tp"),
        P(None, "tp"),
        P(None, "tp"),
        P(None, "tp"),
        P("tp", None),
        P(),
    )
    out_specs = (P("ctx", "tp"), P("ctx", "tp"), P("ctx", "tp"))
    return jax.shard_map(local, mesh=mesh, in_specs=in_specs, out_specs=out_specs, check_vma=False)
```

profile of v0, /device:TPU:1, one launch (start us, length us, event | category | flops | bytes accessed | tf_op | source)
XLA Modules:
  0.0 894.9 jit_solution(3803903503441947136)
XLA Ops:
  8.7 28.6 %all-gather.5.cloned.1.call-done = bf16[128,4096]{1,0:T(8,128)(2,1)} async-done(((bf16[128,1024]{1,0:T(8,128)(2,1)}), bf16[128,4096]{1,0:T(8,128)(2,1)}) %all-gather.5.cloned.1.call-update) | async-done | bytes 1048592 | tf_op jit(solution)/shard_map/all_gather | solution.py:50
  37.3 2.3 convolution_convert_fusion.3
  40.5 22.9 %all-gather.11.cloned.1.call-done = bf16[128,4096]{1,0:T(8,128)(2,1)} async-done(((bf16[128,1024]{1,0:T(8,128)(2,1)}), bf16[128,4096]{1,0:T(8,128)(2,1)}) %all-gather.11.cloned.1.call-update) | async-done | bytes 1048592 | tf_op jit(solution)/shard_map/all_gather | solution.py:51
  63.4 4.0 convolution_convert_fusion
  67.5 2.9 convolution_convert_fusion.1
  70.5 2.3 convolution_convert_fusion.2
  72.9 110.6 %all-gather.7.cloned.1.call-done = bf16[8192,128]{1,0:T(8,128)(2,1)} async-done(((bf16[128,128]{1,0:T(8,128)(2,1)}), bf16[8192,128]{1,0:T(8,128)(2,1)}) %all-gather.7.cloned.1.call-update) | async-done | bytes 2097168 | tf_op jit(solution)/shard_map/all_gather | solution.py:69
  183.4 59.6 %while.37 = (s32[]{:T(128)}, f32[512]{0:T(512)S(1)}, f32[512]{0:T(512)S(1)}, s32[16]{0:T(128)S(1)}, s32[8192]{0:T(1024)}, /*index=5*/bf16[8192,128]{1,0:T(8,128)...) while((s32[]{:T(128)}, f32[512]{0:T(512)S(1)}, ...), condition=%wide.region_3.4_spmd.clone, body=%wide.region_0.3_spmd.clone.sunk | while | flops 69208584 | bytes 2405066 | solution.py:95
  243.1 59.8 %all-gather.9.cloned.1.call-done = bf16[8192,128]{1,0:T(8,128)(2,1)} async-done(((bf16[128,128]{1,0:T(8,128)(2,1)}), bf16[8192,128]{1,0:T(8,128)(2,1)}) %all-gather.9.cloned.1.call-update) | async-done | bytes 2097168 | tf_op jit(solution)/shard_map/all_gather | solution.py:70
  302.9 59.3 %while.38 = (s32[]{:T(128)}, f32[512,128]{1,0:T(8,128)S(1)}, s32[16]{0:T(128)S(1)}, s32[8192]{0:T(1024)}, bf16[8192,128]{1,0:T(8,128)(2,1)}, /*index=5*/bf16[512...) while((s32[]{:T(128)}, f32[512,128]{1,0:T(8,128)S(1)}, ...), condition=%wide.region_5.6_spmd.clone, body=%wide.region_4.5_spmd.clone.sunk | while | flops 135659520 | bytes 936140 | solution.py:108
  305.1 1.5 fusion.102
  308.8 1.5 fusion.102
  312.5 1.5 fusion.102
  316.2 1.5 fusion.102
  319.9 1.5 fusion.102
  323.6 1.5 fusion.102
  327.3 1.5 fusion.102
  331.1 1.5 fusion.102
  334.8 1.5 fusion.102
  338.5 1.5 fusion.102
  342.2 1.5 fusion.102
  345.9 1.5 fusion.102
  349.6 1.5 fusion.102
  353.3 1.5 fusion.102
  357.0 1.5 fusion.102
  360.7 1.5 fusion.102
  362.4 123.5 %while.39 = (s32[]{:T(128)}, f32[512,128]{1,0:T(8,128)S(1)}, f32[16,512,256]{2,1,0:T(8,128)}, s32[16]{0:T(128)S(1)}, s32[8192]{0:T(1024)}, /*index=5*/bf16[8192,...) while((s32[]{:T(128)}, f32[512,128]{1,0:T(8,128)S(1)}, ...), condition=%wide.region_8.9_spmd.clone, body=%wide.region_7.8_spmd.clone.sunk | while | flops 337903616 | bytes 9849589 | solution.py:131
  364.6 1.3 fusion.113
  372.3 1.3 fusion.113
  380.0 1.3 fusion.113
  382.9 1.3 convolution_add_fusion.4
  387.8 1.3 fusion.113
  395.5 1.3 fusion.113
  403.2 1.3 fusion.113
  410.9 1.3 fusion.113
  418.6 1.3 fusion.113
  426.4 1.3 fusion.113
  434.1 1.3 fusion.113
  441.8 1.3 fusion.113
  449.5 1.3 fusion.113
  457.2 1.3 fusion.113
  464.9 1.3 fusion.113
  472.6 1.3 fusion.113
  480.3 1.3 fusion.113
  486.1 3.7 fusion.50
  489.8 328.4 %reduce-scatter.3.cloned.1.call-done = f32[128,256]{1,0:T(8,128)} async-done(((f32[8192,256]{1,0:T(8,128)}), f32[128,256]{1,0:T(8,128)}) %reduce-scatter.3.cloned.1.call-update) | async-done | bytes 131088 | tf_op jit(solution)/shard_map/reduce_scatter | solution.py:136
  820.5 1.4 fusion.47
  821.9 66.1 %reduce-scatter.5.cloned.1.call-done = bf16[128,1024]{1,0:T(8,128)(2,1)} async-done(((bf16[128,4096]{1,0:T(8,128)(2,1)}), bf16[128,1024]{1,0:T(8,128)(2,1)}) %reduce-scatter.5.cloned.1.call-update) | async-done | bytes 262160 | tf_op jit(solution)/shard_map/reduce_scatter | solution.py:147
  (423 shorter events, 168.5 us)
Async XLA Ops:
  7.2 30.1 %copy-start = (bf16[4096,128]{1,0:T(8,128)(2,1)S(1)}, bf16[4096,128]{1,0:T(8,128)(2,1)}, u32[]{:S(2)}) copy-start(bf16[4096,128]{1,0:T(8,128)(2,1)} %param.16) | copy-start | bytes 3145732
  7.2 30.1 %all-gather.5.cloned.1.call-start = ((), (), s32[]{:S(2)}) async-start(), calls=%async_computation.2 | async-start | bytes 1310720 | tf_op jit(solution)/shard_map/all_gather | solution.py:50
  7.9 55.4 %all-gather.11.cloned.1.call-start = ((), (), s32[]{:S(2)}) async-start(), calls=%async_computation.5 | async-start | bytes 1310720 | tf_op jit(solution)/shard_map/all_gather | solution.py:51
  8.7 174.7 %all-gather.7.cloned.1.call-start = ((), (), s32[]{:S(2)}) async-start(), calls=%async_computation.3 | async-start | bytes 2129920 | tf_op jit(solution)/shard_map/all_gather | solution.py:69
  39.6 263.3 %all-gather.9.cloned.1.call-start = ((), (), s32[]{:S(2)}) async-start(), calls=%async_computation.4 | async-start | bytes 2129920 | tf_op jit(solution)/shard_map/all_gather | solution.py:70
  40.5 27.0 %copy-start.1 = (bf16[128,4096]{1,0:T(8,128)(2,1)S(1)}, bf16[128,4096]{1,0:T(8,128)(2,1)}, u32[]{:S(2)}) copy-start(bf16[128,4096]{1,0:T(8,128)(2,1)} %all-gather.5.cloned.1.call-done) | copy-start | bytes 3145732
  72.8 745.4 %reduce-scatter.3.cloned.1.call-start = ((), (), s32[]{:S(2)}) async-start(), calls=%async_computation.6 | async-start | bytes 8519680 | tf_op jit(solution)/shard_map/reduce_scatter | solution.py:136
  485.9 402.1 %reduce-scatter.5.cloned.1.call-start = ((), (), s32[]{:S(2)}) async-start(), calls=%async_computation.7 | async-start | bytes 1310720 | tf_op jit(solution)/shard_map/reduce_scatter | solution.py:147
  819.0 0.6 copy-start.3
  819.0 1.5 copy-start.2
  820.5 1.4 copy-start.4
Sparse Core Ops, SparseCore 0:
  9.8 27.4 all-gather.4
  39.1 24.2 all-gather.10
  67.5 115.8 all-gather.6
  187.4 115.4 all-gather.8
  486.1 332.0 reduce-scatter.2
  822.0 65.9 reduce-scatter.4
where the time goes:
time: 899 us; the launch traced here: 895 us
  waiting for transfers between devices  618 us (69%)
  matrix products  131 us (15%)
  local copies, waits for them, and re-layouts  92.5 us (10%)
  loops' own time  33.5 us (4%)
  between operations  14.3 us (2%)
    reduce_scatter x1, waiting for transfers between devices, local(): lax.psum_scatter(key_terms, 'ctx', scatter_dimension=0, tiled=True)  328 us
    all_gather x1, waiting for transfers between devices, local(): lax.all_gather(keys_own, 'ctx', axis=0, tiled=True)  111 us
    dot_general x52, matrix products, contract_last(): lax.dot_general(left, right, (((1,), (1,)), ((), ())), preferred_element_...  69.1 us
    reduce_scatter x1, waiting for transfers between devices, local(): lax.psum_scatter(partial_value.astype(jnp.bfloat16), 'tp', scatter_dimens...  66.1 us
    all_gather x1, waiting for transfers between devices, local(): lax.all_gather(values_own, 'ctx', axis=0, tiled=True)  59.8 us
    dynamic_slice x48, local copies, waits for them, and re-layouts, key_slices(): key_times = lax.dynamic_slice_in_dim(times, first_row, key_span, 0)  36.7 us
    all_gather x1, waiting for transfers between devices, local(): lax.all_gather(inputs, 'tp', axis=1, tiled=True)  28.6 us
    dynamic_slice x48, local copies, waits for them, and re-layouts, local(): (row_top, row_norm), unused = lax.scan(stats_step, start_pair, block_ids)  28.1 us
  transfers between devices with their start and end apart: 6, of which 6 were waited for; matrix products, arithmetic and copies ran while one was open for 7% of the time, Pallas kernels for 0%

commit v1 on v0

v1 whole, which is shorter than its diff:
```python
import functools

import jax
import jax.numpy as jnp
from jax import lax
from jax.experimental import pallas as pl
from jax.experimental.pallas import tpu as pltpu
from jax.sharding import Mesh
from jax.sharding import PartitionSpec as P

HEAD = 128
FACTOR = HEAD**-0.5
LOG2E = 1.4426950408889634
SCALE2 = FACTOR * LOG2E
NEG_FILL = -1e30
BLOCK = 128
HEADS = 4
ROWS = HEADS * BLOCK
CHUNK = 2 * BLOCK
VMEM_LIMIT = 24 * 1024 * 1024
BF16 = jnp.bfloat16
F32 = jnp.float32


def shifted(size, step):
    return [(i, (i + step) % size) for i in range(size)]


def contract_last(left, right):
    return lax.dot_general(
        left, right, (((1,), (1,)), ((), ())), preferred_element_type=F32
    )


def matmul(left, right):
    return jnp.dot(left, right, preferred_element_type=F32)


def project_kernel(first, rank, x0, x1, g0, g1, wq, wk, wv, wo, *rest):
    if first:
        sum_ref, acc = rest
    else:
        before, kv_ref, qd_ref, acc = rest
    step = pl.program_id(0)

    def add(x_ref, g_ref, start):
        x, g = x_ref[...], g_ref[...]
        parts = (
            (0, 128, matmul(x, wk[...])),
            (128, 256, matmul(x, wv[...])),
            (256, 768, matmul(x, wq[...])),
            (768, 1280, contract_last(g, wo[...])),
        )
        for low, high, part in parts:
            if start is None:
                acc[:, low:high] = part
            else:
                acc[:, low:high] = start[:, low:high] + part

    @pl.when(step == 0)
    def _():
        add(x0, g0, None if first else before)

    @pl.when(step == 1)
    def _():
        add(x1, g1, acc)
        if first:
            sum_ref[...] = acc[...]
        else:
            kv_ref[...] = acc[:, :256].astype(BF16)
            qd_ref[...] = acc[:, 256:].astype(BF16)


def project(first, rank, offset, x0, x1, g0, g1, weights, before=None):
    wq, wk, wv, wo = weights
    whole = pl.BlockSpec((BLOCK, 1024), lambda i, r: (0, 0))

    def rows(width):
        return pl.BlockSpec((1024, width), lambda i, r: (r[0] ^ (offset + i), 0))

    in_specs = [whole] * 4 + [
        rows(512),
        rows(128),
        rows(128),
        pl.BlockSpec((512, 1024), lambda i, r: (0, r[0] ^ (offset + i))),
    ]
    operands = [x0, x1, g0, g1, wq, wk, wv, wo]
    if first:
        out_shape = [jax.ShapeDtypeStruct((BLOCK, 1280), F32)]
        out_specs = [pl.BlockSpec((BLOCK, 1280), lambda i, r: (0, 0))]
    else:
        in_specs.append(pl.BlockSpec((BLOCK, 1280), lambda i, r: (0, 0)))
        operands.append(before)
        out_shape = [
            jax.ShapeDtypeStruct((BLOCK, 256), BF16),
            jax.ShapeDtypeStruct((BLOCK, 1024), BF16),
        ]
        out_specs = [
            pl.BlockSpec((BLOCK, 256), lambda i, r: (0, 0)),
            pl.BlockSpec((BLOCK, 1024), lambda i, r: (0, 0)),
        ]
    return pl.pallas_call(
        functools.partial(project_kernel, first),
        grid_spec=pltpu.PrefetchScalarGridSpec(
            num_scalar_prefetch=1,
            grid=(2,),
            in_specs=in_specs,
            out_specs=out_specs,
            scratch_shapes=[pltpu.VMEM((BLOCK, 1280), F32)],
        ),
        out_shape=out_shape,
        compiler_params=pltpu.CompilerParams(vmem_limit_bytes=VMEM_LIMIT),
        cost_estimate=pl.CostEstimate(
            flops=2 * 128 * 2048 * 1280, bytes_accessed=6 << 20, transcendentals=0
        ),
    )(rank, *operands)


def stack_heads(ref, first):
    return jnp.concatenate(
        [ref[:, first + h * HEAD : first + (h + 1) * HEAD] for h in range(HEADS)], axis=0
    )


def visible_tile(times, key_block, query_block):
    key_row = jnp.broadcast_to(times[pl.ds(key_block, 1), :], (BLOCK, BLOCK))
    seen = key_row.T <= times[pl.ds(query_block, 1), :]
    return jnp.concatenate([seen] * HEADS, axis=1)


def for_chunks(place, query_y, full, masked):
    z, y, xh = place[0], place[1], place[2]
    lax.fori_loop(0, z, lambda i, carry: (full(i), carry)[1], 0)
    masked(z)

    @pl.when((z < 7) & (y == 0) & (xh == 1) & (query_y == 3))
    def _():
        masked(z + 1)


def chunk_mask(times, place, chunk, query_y):
    z, y, xh = place[0], place[1], place[2]
    query_block = 8 * z + 2 * query_y + xh
    return jnp.concatenate(
        [visible_tile(times, 8 * chunk + 2 * y + h, query_block) for h in range(2)], axis=0
    )


def stats_kernel(place, times, kv, qd0, qd1, qd2, qd3, out, q_rows, g_rows):
    for s, qd in enumerate((qd0, qd1, qd2, qd3)):
        query_y = (place[1] - s + 4) % 4
        q_rows[...] = stack_heads(qd, 0)
        g_rows[...] = stack_heads(qd, 512)
        base = 4 * s
        out[base : base + 1, :] = jnp.full((1, ROWS), NEG_FILL, F32)
        out[base + 1 : base + 4, :] = jnp.zeros((3, ROWS), F32)

        def chunk_stats(chunk, with_mask):
            first = pl.multiple_of(chunk * CHUNK, CHUNK)
            keys = kv[pl.ds(first, CHUNK), :HEAD]
            values = kv[pl.ds(first, CHUNK), HEAD:]
            scores = contract_last(keys, q_rows[...]) * SCALE2
            if with_mask:
                seen = chunk_mask(times, place, chunk, query_y)
                scores = jnp.where(seen, scores, NEG_FILL)
            old = out[base : base + 1, :]
            top = jnp.maximum(old, jnp.max(scores, axis=0, keepdims=True))
            prob = jnp.exp2(scores - top)
            if with_mask:
                prob = jnp.where(seen, prob, 0.0)
            prob_grad = contract_last(values, g_rows[...])
            shrink = jnp.exp2(old - top)
            out[base : base + 1, :] = top
            out[base + 1 : base + 2, :] = out[base + 1 : base + 2, :] * shrink + jnp.sum(
                prob, axis=0, keepdims=True
            )
            out[base + 2 : base + 3, :] = out[base + 2 : base + 3, :] * shrink + jnp.sum(
                prob * prob_grad, axis=0, keepdims=True
            )

        for_chunks(
            place,
            query_y,
            functools.partial(chunk_stats, with_mask=False),
            functools.partial(chunk_stats, with_mask=True),
        )


def whole_specs(count):
    return [pl.BlockSpec(memory_space=pltpu.SMEM)] + [
        pl.BlockSpec(memory_space=pltpu.VMEM) for _ in range(count - 1)
    ]


def stats(place, times, kv, blocks):
    return pl.pallas_call(
        stats_kernel,
        in_specs=whole_specs(7),
        out_specs=pl.BlockSpec(memory_space=pltpu.VMEM),
        out_shape=jax.ShapeDtypeStruct((16, ROWS), F32),
        scratch_shapes=[pltpu.VMEM((ROWS, HEAD), BF16), pltpu.VMEM((ROWS, HEAD), BF16)],
        compiler_params=pltpu.CompilerParams(vmem_limit_bytes=VMEM_LIMIT),
        cost_estimate=pl.CostEstimate(
            flops=4 * 2048 * 2048 * 128, bytes_accessed=2 << 20, transcendentals=2048 * 2048
        ),
    )(place, times, kv, *blocks)


def grads_kernel(
    place, times, kv, qd0, qd1, qd2, qd3, st0, st1, st2, st3,
    dkv, dq0, dq1, dq2, dq3, sums, q_rows, g_rows, q_sum,
):
    sums[...] = jnp.zeros_like(sums)
    gathered = (st0, st1, st2, st3)
    for s, (qd, dq) in enumerate(zip((qd0, qd1, qd2, qd3), (dq0, dq1, dq2, dq3))):
        query_y = (place[1] - s + 4) % 4
        q_rows[...] = stack_heads(qd, 0)
        g_rows[...] = stack_heads(qd, 512)
        q_sum[...] = jnp.zeros_like(q_sum)
        tops, norms, dots = [], [], []
        for k, st in enumerate(gathered):
            base = 4 * ((s - k) % 4)
            tops.append(st[base : base + 1, :])
            norms.append(st[base + 1 : base + 2, :])
            dots.append(st[base + 2 : base + 3, :])
        top = functools.reduce(jnp.maximum, tops)
        scales = [jnp.exp2(t - top) for t in tops]
        norm = sum(n * f for n, f in zip(norms, scales))
        delta = sum(d * f for d, f in zip(dots, scales)) / norm
        lse = top + jnp.log2(norm)

        def chunk_grads(chunk, with_mask):
            first = pl.multiple_of(chunk * CHUNK, CHUNK)
            keys = kv[pl.ds(first, CHUNK), :HEAD]
            values = kv[pl.ds(first, CHUNK), HEAD:]
            q, g = q_rows[...], g_rows[...]
            prob = jnp.exp2(contract_last(keys, q) * SCALE2 - lse)
            if with_mask:
                prob = jnp.where(chunk_mask(times, place, chunk, query_y), prob, 0.0)
            prob_grad = contract_last(values, g)
            score_grad = (prob * (prob_grad - delta)).astype(BF16)
            sums[pl.ds(first, CHUNK), :HEAD] += matmul(score_grad, q)
            sums[pl.ds(first, CHUNK), HEAD:] += matmul(prob.astype(BF16), g)
            q_sum[...] += lax.dot_general(
                keys, score_grad, (((0,), (0,)), ((), ())), preferred_element_type=F32
            )

        for_chunks(
            place,
            query_y,
            functools.partial(chunk_grads, with_mask=False),
            functools.partial(chunk_grads, with_mask=True),
        )
        for h in range(HEADS):
            cols = slice(h * HEAD, (h + 1) * HEAD)
            dq[:, cols] = (q_sum[:, cols].T * FACTOR).astype(BF16)
    dkv[...] = sums[...].astype(BF16)


def grads(place, times, kv, blocks, gathered):
    return pl.pallas_call(
        grads_kernel,
        in_specs=whole_specs(11),
        out_specs=[pl.BlockSpec(memory_space=pltpu.VMEM)] * 5,
        out_shape=[jax.ShapeDtypeStruct((16 * BLOCK, 2 * HEAD), BF16)]
        + [jax.ShapeDtypeStruct((BLOCK, ROWS), BF16)] * 4,
        scratch_shapes=[
            pltpu.VMEM((16 * BLOCK, 2 * HEAD), F32),
            pltpu.VMEM((ROWS, HEAD), BF16),
            pltpu.VMEM((ROWS, HEAD), BF16),
            pltpu.VMEM((HEAD, ROWS), F32),
        ],
        compiler_params=pltpu.CompilerParams(vmem_limit_bytes=VMEM_LIMIT),
        cost_estimate=pl.CostEstimate(
            flops=10 * 2048 * 2048 * 128, bytes_accessed=4 << 20, transcendentals=2048 * 2048
        ),
    )(place, times, kv, *blocks, *gathered)


def back_kernel(rank, dq, dkv, wq, wk, wv, out):
    out[...] = (
        contract_last(dq[...], wq[...])
        + contract_last(dkv[:, :HEAD], wk[...])
        + contract_last(dkv[:, HEAD:], wv[...])
    ).astype(BF16)


def back(rank, first, dq, dkv, weights):
    wq, wk, wv = weights

    def rows(width):
        return pl.BlockSpec((1024, width), lambda i, r: (r[0] ^ (first - i), 0))

    return pl.pallas_call(
        back_kernel,
        grid_spec=pltpu.PrefetchScalarGridSpec(
            num_scalar_prefetch=1,
            grid=(2,),
            in_specs=[
                pl.BlockSpec((BLOCK, 512), lambda i, r: (0, 0)),
                pl.BlockSpec((BLOCK, 256), lambda i, r: (0, 0)),
                rows(512),
                rows(128),
                rows(128),
            ],
            out_specs=pl.BlockSpec((None, BLOCK, 1024), lambda i, r: (i, 0, 0)),
        ),
        out_shape=jax.ShapeDtypeStruct((2, BLOCK, 1024), BF16),
        compiler_params=pltpu.CompilerParams(vmem_limit_bytes=VMEM_LIMIT),
        cost_estimate=pl.CostEstimate(
            flops=2 * 128 * 2048 * 768, bytes_accessed=4 << 20, transcendentals=0
        ),
    )(rank, dq, dkv, wq, wk, wv)


def local(inputs, out_grad, w_query, key_weight, value_weight, w_output, times):
    z, y, xh = lax.axis_index("z"), lax.axis_index("y"), lax.axis_index("xh")
    xl, core = lax.axis_index("xl"), lax.axis_index("core")
    rank = (2 * xl + core).astype(jnp.int32).reshape(1)
    place = jnp.stack([z, y, xh]).astype(jnp.int32)
    times2d = times.reshape(64, BLOCK)
    swap = shifted(2, 1)

    def to_core(value):
        return lax.ppermute(value, "core", swap)

    def to_xl(value):
        return lax.ppermute(value, "xl", swap)

    x2, g2 = to_xl(inputs), to_xl(out_grad)
    x1, g1 = to_core(inputs), to_core(out_grad)
    weights = (w_query, key_weight, value_weight, w_output)
    (half,) = project(True, rank, 0, inputs, x1, out_grad, g1, weights)
    x3, g3 = to_core(x2), to_core(g2)
    kv_own, qd_own = project(False, rank, 2, x2, x3, g2, g3, weights, half)

    blocks = [qd_own] + [lax.ppermute(qd_own, "y", shifted(4, s)) for s in (1, 2, 3)]
    kv = lax.all_to_all(
        jnp.broadcast_to(kv_own, (16,) + kv_own.shape), ("z", "xh"), 0, 0, tiled=True
    ).reshape(16 * BLOCK, 2 * HEAD)

    own_stats = stats(place, times2d, kv, blocks)
    gathered = [own_stats] + [lax.ppermute(own_stats, "y", shifted(4, s)) for s in (1, 2, 3)]
    dkv, *dqs = grads(place, times2d, kv, blocks, gathered)

    dq_parts = [dqs[0]] + [lax.ppermute(dqs[s], "y", shifted(4, -s)) for s in (1, 2, 3)]
    dkv_parts = lax.all_to_all(
        dkv.reshape(16, BLOCK, 2 * HEAD), ("z", "xh"), 0, 0, tiled=True
    )
    dq = sum(part.astype(F32) for part in dq_parts).astype(BF16)
    dkv_sum = jnp.sum(dkv_parts.astype(F32), axis=0)
    dk = (dkv_sum[:, :HEAD] * FACTOR).astype(BF16)
    dv = dkv_sum[:, HEAD:].astype(BF16)
    dkv_own = jnp.concatenate([dk, dv], axis=1)

    back_weights = (w_query, key_weight, value_weight)
    far = back(rank, 3, dq, dkv_own, back_weights)
    far_sum = (far[1].astype(F32) + to_core(far[0]).astype(F32)).astype(BF16)
    from_far = to_xl(far_sum)
    near = back(rank, 1, dq, dkv_own, back_weights)
    input_grad = (
        near[1].astype(F32) + to_core(near[0]).astype(F32) + from_far.astype(F32)
    ).astype(BF16)
    return input_grad, dk, dv


def solution(mesh):
    split = Mesh(mesh.devices.reshape(8, 4, 2, 2, 2), ("z", "y", "xh", "xl", "core"))
    ctx, tp = ("z", "y", "xh"), ("xl", "core")
    in_specs = (
        P(ctx, tp),
        P(ctx, tp),
        P(None, tp),
        P(None, tp),
        P(None, tp),
        P(tp, None),
        P(),
    )
    out_specs = (P(ctx, tp), P(ctx, tp), P(ctx, tp))
    return jax.shard_map(
        local, mesh=split, in_specs=in_specs, out_specs=out_specs, check_vma=False
    )
```

time: 899 us -> 160 us (0.18)
  waiting for transfers between devices: 618 us -> 60.6 us
  matrix products: 131 us -> 0 us
  local copies, waits for them, and re-layouts: 92.5 us -> 15.3 us
  starting transfers between devices: 0.24 us -> 67.3 us
  loops' own time: 33.5 us -> 0 us
  between operations: 14.3 us -> 0.84 us
  Pallas kernels: 0 us -> 12.9 us
    reduce_scatter x2 -> x0, waiting for transfers between devices: 395 us -> none  [the longest x1 328 us: local(): lax.psum_scatter(key_terms, 'ctx', scatter_dimension=0, tiled=True)]
    all_gather x4 -> x0, waiting for transfers between devices: 222 us -> none  [the longest x1 111 us: local(): lax.all_gather(keys_own, 'ctx', axis=0, tiled=True)]
    dot_general x119 -> x0, matrix products: 131 us -> none  [the longest x52 69.1 us: contract_last(): lax.dot_general(left, right, (((1,), (1,)), ((), ())), preferred_element_...]
    dynamic_slice x97 -> x0, local copies, waits for them, and re-layouts: 65.5 us -> none  [the longest x48 36.7 us: key_slices(): key_times = lax.dynamic_slice_in_dim(times, first_row, key_span, 0)]
    all_to_all x0 -> x2, starting transfers between devices: none -> 39.4 us  [the longest x1 28.4 us: local(): lax.all_to_all(dkv.reshape(16, BLOCK, 2 * HEAD), ('z', 'xh'), 0, 0, tiled...]
    another operation x3 -> x0, loops' own time: 33.5 us -> none  [the longest x1 11.5 us: local(): lax.scan(grad_step, jnp.zeros((count, HEAD_SIZE), jnp.float32), block_ids)]
    ppermute x0 -> x18, waiting for transfers between devices: none -> 32.3 us  [the longest x3 14.2 us: local(): lax.ppermute(qd_own, 'y', shifted(4, s))]
    all_to_all x0 -> x2, waiting for transfers between devices: none -> 28.3 us  [the longest x1 18.7 us: local(): lax.all_to_all(dkv.reshape(16, BLOCK, 2 * HEAD), ('z', 'xh'), 0, 0, tiled...]
  transfers between devices with their start and end apart: 6 -> 20, of which waited for: 6 -> 13; matrix products, arithmetic and copies ran while one was open for 7% -> 0% of each run, Pallas kernels for 0% -> 2%
where the time goes in v1:
time: 160 us; the launch traced here: 159 us
  starting transfers between devices  67.3 us (42%)
  waiting for transfers between devices  60.6 us (38%)
  local copies, waits for them, and re-layouts  15.3 us (10%)
  Pallas kernels  12.9 us (8%)
  other arithmetic  2.43 us (2%)
    all_to_all x1, starting transfers between devices, local(): lax.all_to_all(dkv.reshape(16, BLOCK, 2 * HEAD), ('z', 'xh'), 0, 0, tiled...  28.4 us
    all_to_all x1, waiting for transfers between devices, local(): lax.all_to_all(dkv.reshape(16, BLOCK, 2 * HEAD), ('z', 'xh'), 0, 0, tiled...  18.7 us
    ppermute x6, starting transfers between devices, to_core(): return lax.ppermute(value, 'core', swap)  15.4 us
    ppermute x3, waiting for transfers between devices, local(): lax.ppermute(qd_own, 'y', shifted(4, s))  14.2 us
    unnamed x32, local copies, waits for them, and re-layouts  14.2 us
    all_to_all x1, starting transfers between devices, local(): lax.all_to_all(jnp.broadcast_to(kv_own, (16,) + kv_own.shape), ('z', 'xh'...  11 us
    all_to_all x1, waiting for transfers between devices, local(): lax.all_to_all(jnp.broadcast_to(kv_own, (16,) + kv_own.shape), ('z', 'xh'...  9.64 us
    ppermute x3, waiting for transfers between devices, to_xl(): return lax.ppermute(value, 'xl', swap)  8.19 us
  transfers between devices with their start and end apart: 20, of which 13 were waited for; matrix products, arithmetic and copies ran while one was open for 0% of the time, Pallas kernels for 2%

profile of v1, /device:TPU:1, one launch (start us, length us, event | category | flops | bytes accessed | tf_op | source)
XLA Modules:
  0.0 159.3 jit_solution(6168816468530282127)
XLA Ops:
  0.6 2.1 %collective-permute-start = (bf16[128,1024]{1,0:T(8,128)(2,1)}, bf16[128,1024]{1,0:T(8,128)(2,1)S(1)}, u32[]{:S(2)}, u32[]{:S(2)}) collective-permute-start(bf16[128,1024]{1,0:T(8,128)(2,1)} %x0.1), channel_id=1, source_target_pairs={{0,2},{2,0},{1,3},{3,1},{4,6},{6,4},{5,7},{7,5},{8,10},{10,8},{9,1... | collective-permute-start | bytes 786440 | tf_op jit(solution)/shard_map/ppermute | solution.py:328
  2.9 3.1 %collective-permute-start.4 = (bf16[128,1024]{1,0:T(8,128)(2,1)}, bf16[128,1024]{1,0:T(8,128)(2,1)S(1)}, u32[]{:S(2)}, u32[]{:S(2)}) collective-permute-start(bf16[128,1024]{1,0:T(8,128)(2,1)} %x0.1), channel_id=1, source_target_pairs={{0,1},{1,0},{2,3},{3,2},{4,5},{5,4},{6,7},{7,6},{8,9},{9,8},{10,11... | collective-permute-start | bytes 786440 | tf_op jit(solution)/shard_map/ppermute | solution.py:325
  6.0 1.8 %collective-permute-done.x0 = bf16[128,1024]{1,0:T(8,128)(2,1)S(1)} collective-permute-done((bf16[128,1024]{1,0:T(8,128)(2,1)}, bf16[128,1024]{1,0:T(8,128)(2,1)S(1)}, u32[]{:S(2)}, u32[]{:S(2)}) %collective-permute-start) | collective-permute-done | bytes 262176 | tf_op jit(solution)/shard_map/ppermute | solution.py:328
  7.8 5.3 %collective-permute-start.1 = (bf16[128,1024]{1,0:T(8,128)(2,1)S(1)}, bf16[128,1024]{1,0:T(8,128)(2,1)S(1)}, u32[]{:S(2)}, u32[]{:S(2)}) collective-permute-start(bf16[128,1024]{1,0:T(8,128)(2,1)S(1)} %collective-permute-done.x0), channel_id=1, source_target_pairs={{0,1},{1,0},{2,3},{3,2},{4,5},{5,4},{6,7},{7,6},{8,9},{9,8},{10,11... | collective-permute-start | bytes 786440 | tf_op jit(solution)/shard_map/ppermute | solution.py:325
  13.0 0.3 collective-permute-done.2.g0
  13.4 2.5 %collective-permute-start.3 = (bf16[128,1024]{1,0:T(8,128)(2,1)S(1)}, bf16[128,1024]{1,0:T(8,128)(2,1)S(1)}, u32[]{:S(2)}, u32[]{:S(2)}) collective-permute-start(bf16[128,1024]{1,0:T(8,128)(2,1)S(1)} %collective-permute-done.2.g0), channel_id=1, source_target_pairs={{0,1},{1,0},{2,3},{3,2},{4,5},{5,4},{6,7},{7,6},{8,9},{9,8},{10,11... | collective-permute-start | bytes 786440 | tf_op jit(solution)/shard_map/ppermute | solution.py:325
  15.9 2.2 %copy-done = bf16[4096,512]{1,0:T(8,128)(2,1)S(1)} copy-done((bf16[4096,512]{1,0:T(8,128)(2,1)S(1)}, bf16[4096,512]{1,0:T(8,128)(2,1)}, u32[]{:S(2)}) %copy-start) | copy-done | bytes 4194328
  18.0 2.2 %copy-done.3 = bf16[512,4096]{1,0:T(8,128)(2,1)S(1)} copy-done((bf16[512,4096]{1,0:T(8,128)(2,1)S(1)}, bf16[512,4096]{1,0:T(8,128)(2,1)}, u32[]{:S(2)}) %copy-start.3) | copy-done | bytes 4194328
  20.2 1.2 copy-done.5
  21.5 1.2 copy-done.7
  22.7 0.9 copy-done.9
  23.6 0.9 copy-done.10
  24.6 1.7 %shard_map.94.rest_0_ = f32[128,1280]{1,0:T(8,128)S(1)} custom-call(s32[1]{0:T(128)} %bitcast.rank, bf16[128,1024]{1,0:T(8,128)(2,1)S(1)} %copy-done.9, bf16[128,1024]{1,0:T(8,128)(2,1)S(1)} %collective-permute-done.4.x1, bf16[128,1024]{1,0:T(8,128)(2,1)S(1)} %copy-done.10, bf16[128,1024]{1,0:T(8,128)(2,1)S(1)} %collective-permute-done.5.g1, ...), custom_call_target="tpu_custom_call" | custom-call | flops 671088640 | bytes 6291456 | tf_op jit(solution)/shard_map/pallas_call | solution.py:102
  26.3 0.4 copy-done.1
  26.8 1.3 copy-done.4
  28.3 1.7 %shard_map.95 = (bf16[128,256]{1,0:T(8,128)(2,1)S(1)}, bf16[128,1024]{1,0:T(8,128)(2,1)S(1)}) custom-call(s32[1]{0:T(128)} %bitcast.rank, bf16[128,1024]{1,0:T(8,128)(2,1)S(1)} %collective-permute-done.x0, bf16[128,1024]{1,0:T(8,128)(2,1)S(1)} %collective-permute-done.1.x1, bf16[128,1024]{1,0:T(8,128)(2,1)S(1)} %collective-permute-done.2.g0, ...), custom_call_target="tpu_custom_call" | custom-call | flops 671088640 | bytes 6291456 | tf_op jit(solution)/shard_map/pallas_call | solution.py:102
  30.0 1.1 broadcast_in_dim.3
  31.1 11.0 %all-to-all-start = ((bf16[16,128,256]{2,1,0:T(8,128)(2,1)}), bf16[16,128,256]{2,1,0:T(8,128)(2,1)S(1)}, u32[]{:S(2)}, u32[]{:S(2)}) async-start(bf16[16,128,256]{2,1,0:T(8,128)(2,1)} %broadcast_in_dim.3), calls=%async_computation | async-start | bytes 2097152 | tf_op jit(solution)/shard_map/all_to_all | solution.py:338
  42.1 2.8 %collective-permute-start.8 = (bf16[128,1024]{1,0:T(8,128)(2,1)S(1)}, bf16[128,1024]{1,0:T(8,128)(2,1)S(1)}, u32[]{:S(2)}, u32[]{:S(2)}) collective-permute-start(bf16[128,1024]{1,0:T(8,128)(2,1)S(1)} %get-tuple-element.11.qd0), channel_id=1, source_target_pairs={{0,24},{8,0},{16,8},{24,16},{1,25},{9,1},{17,9},{25,17},{2,26},{10... | collective-permute-start | bytes 786440 | tf_op jit(solution)/shard_map/ppermute | solution.py:337
  44.9 0.3 collective-permute-start.7
  45.3 0.7 collective-permute-start.6
  46.0 9.8 %collective-permute-done.8.qd3 = bf16[128,1024]{1,0:T(8,128)(2,1)S(1)} collective-permute-done((bf16[128,1024]{1,0:T(8,128)(2,1)S(1)}, bf16[128,1024]{1,0:T(8,128)(2,1)S(1)}, u32[]{:S(2)}, u32[]{:S(2)}) %collective-permute-start.8) | collective-permute-done | bytes 262176 | tf_op jit(solution)/shard_map/ppermute | solution.py:337
  55.8 4.5 %collective-permute-done.6.qd1 = bf16[128,1024]{1,0:T(8,128)(2,1)S(1)} collective-permute-done((bf16[128,1024]{1,0:T(8,128)(2,1)S(1)}, bf16[128,1024]{1,0:T(8,128)(2,1)S(1)}, u32[]{:S(2)}, u32[]{:S(2)}) %collective-permute-start.6) | collective-permute-done | bytes 262176 | tf_op jit(solution)/shard_map/ppermute | solution.py:337
  60.3 9.6 %all-to-all-done = bf16[16,128,256]{2,1,0:T(8,128)(2,1)S(1)} async-done(((bf16[16,128,256]{2,1,0:T(8,128)(2,1)}), bf16[16,128,256]{2,1,0:T(8,128)(2,1)S(1)}, u32[]{:S(2)}, u32[]{:S(2)}) %all-to-all-start) | async-done | bytes 1048608 | tf_op jit(solution)/shard_map/all_to_all | solution.py:338
  69.9 2.3 %shard_map.96.st0 = f32[16,512]{1,0:T(8,128)S(1)} custom-call(s32[3]{0:T(128)S(1)} %pad_add_fusion.place, s32[64,128]{1,0:T(8,128)S(1)} %bitcast.23, bf16[2048,256]{1,0:T(8,128)(2,1)S(1)} %bitcast.21, bf16[128,1024]{1,0:T(8,128)(2,1)S(1)} %get-tuple-element.11.qd0, bf16[128,1024]{1,0:T(8,128)(2,1)S(1)} %collective-permute-done.6.qd1, ...), custom_call_target="tpu_custom_call" | custom-call | flops 2147483648 | bytes 2097152 | tf_op jit(solution)/shard_map/pallas_call | solution.py:196
  72.2 3.0 %collective-permute-start.11 = (f32[16,512]{1,0:T(8,128)S(1)}, f32[16,512]{1,0:T(8,128)S(1)}, u32[]{:S(2)}, u32[]{:S(2)}) collective-permute-start(f32[16,512]{1,0:T(8,128)S(1)} %shard_map.96.st0), channel_id=1, source_target_pairs={{0,24},{8,0},{16,8},{24,16},{1,25},{9,1},{17,9},{25,17},{2,26},{10... | collective-permute-start | bytes 98312 | tf_op jit(solution)/shard_map/ppermute | solution.py:343
  75.2 0.3 collective-permute-start.10
  75.5 0.7 collective-permute-start.9
  76.2 3.3 %collective-permute-done.10.st2 = f32[16,512]{1,0:T(8,128)S(1)} collective-permute-done((f32[16,512]{1,0:T(8,128)S(1)}, f32[16,512]{1,0:T(8,128)S(1)}, u32[]{:S(2)}, u32[]{:S(2)}) %collective-permute-start.10) | collective-permute-done | bytes 32800 | tf_op jit(solution)/shard_map/ppermute | solution.py:343
  79.8 4.5 %shard_map.97 = (bf16[2048,256]{1,0:T(8,128)(2,1)}, bf16[128,512]{1,0:T(8,128)(2,1)S(1)}, bf16[128,512]{1,0:T(8,128)(2,1)S(1)}, bf16[128,512]{1,0:T(8,128)(2,1)S(1)}, bf16[128,512]{1,0:T(8,128)(2,1)S(1)}) custom-call(s32[3]{0:T(128)S(1)} %pad_add_fusion.place, s32[64,128]{1,0:T(8,128)S(1)} %bitcast.24, bf16[2048,256]{1,0:T(8,128)(2,1)S(1)} %bitcast.22, ...), custom_call_target="tpu_custom_call" | custom-call | flops 5368709120 | bytes 4194304 | tf_op jit(solution)/shard_map/pallas_call | solution.py:261
  84.4 0.7 copy-done.11
  85.0 0.6 copy-done.12
  85.7 28.4 %all-to-all-start.1 = ((bf16[16,128,256]{2,1,0:T(8,128)(2,1)}), bf16[16,128,256]{2,1,0:T(8,128)(2,1)}, u32[]{:S(2)}, u32[]{:S(2)}) async-start(bf16[16,128,256]{2,1,0:T(8,128)(2,1)} %bitcast.6), calls=%async_computation.1 | async-start | bytes 2097152 | tf_op jit(solution)/shard_map/all_to_all | solution.py:347
  114.4 0.9 collective-permute-start.13
  115.3 0.8 collective-permute-start.14
  116.1 2.1 %collective-permute-done.12 = bf16[128,512]{1,0:T(8,128)(2,1)S(1)} collective-permute-done((bf16[128,512]{1,0:T(8,128)(2,1)}, bf16[128,512]{1,0:T(8,128)(2,1)S(1)}, u32[]{:S(2)}, u32[]{:S(2)}) %collective-permute-start.12) | collective-permute-done | bytes 131104 | tf_op jit(solution)/shard_map/ppermute | solution.py:346
  118.2 1.9 %collective-permute-done.13 = bf16[128,512]{1,0:T(8,128)(2,1)S(1)} collective-permute-done((bf16[128,512]{1,0:T(8,128)(2,1)}, bf16[128,512]{1,0:T(8,128)(2,1)S(1)}, u32[]{:S(2)}, u32[]{:S(2)}) %collective-permute-start.13) | collective-permute-done | bytes 131104 | tf_op jit(solution)/shard_map/ppermute | solution.py:346
  120.0 1.3 collective-permute-done.14
  121.4 18.7 %all-to-all-done.1 = bf16[16,128,256]{2,1,0:T(8,128)(2,1)} async-done(((bf16[16,128,256]{2,1,0:T(8,128)(2,1)}), bf16[16,128,256]{2,1,0:T(8,128)(2,1)}, u32[]{:S(2)}, u32[]{:S(2)}) %all-to-all-start.1) | async-done | bytes 1048608 | tf_op jit(solution)/shard_map/all_to_all | solution.py:347
  140.1 1.4 convert_reduce_fusion
  141.6 2.2 %copy-done.2 = bf16[4096,512]{1,0:T(8,128)(2,1)S(1)} copy-done((bf16[4096,512]{1,0:T(8,128)(2,1)S(1)}, bf16[4096,512]{1,0:T(8,128)(2,1)}, u32[]{:S(2)}) %copy-start.2) | copy-done | bytes 4194328
  143.7 1.3 shard_map.99
  145.1 4.4 %collective-permute-start.16 = (bf16[128,1024]{1,0:T(8,128)(2,1)S(1)}, bf16[128,1024]{1,0:T(8,128)(2,1)S(1)}, u32[]{:S(2)}, u32[]{:S(2)}) collective-permute-start(bf16[128,1024]{1,0:T(8,128)(2,1)S(1)} %slice_bitcast_fusion), channel_id=1, source_target_pairs={{0,1},{1,0},{2,3},{3,2},{4,5},{5,4},{6,7},{7,6},{8,9},{9,8},{10,11... | collective-permute-start | bytes 786440 | tf_op jit(solution)/shard_map/ppermute | solution.py:325
  149.4 1.3 shard_map.98
  151.0 0.4 collective-permute-start.17
  151.4 1.0 collective-permute-done.15
  152.4 6.1 %collective-permute-done.17 = bf16[128,1024]{1,0:T(8,128)(2,1)S(1)} collective-permute-done((bf16[128,1024]{1,0:T(8,128)(2,1)S(1)}, bf16[128,1024]{1,0:T(8,128)(2,1)S(1)}, u32[]{:S(2)}, u32[]{:S(2)}) %collective-permute-start.17) | collective-permute-done | bytes 262176 | tf_op jit(solution)/shard_map/ppermute | solution.py:328
  158.5 0.8 fusion.2
  (41 shorter events, 1.4 us)
Async XLA Ops:
  0.6 7.1 %collective-permute-start = (bf16[128,1024]{1,0:T(8,128)(2,1)}, bf16[128,1024]{1,0:T(8,128)(2,1)S(1)}, u32[]{:S(2)}, u32[]{:S(2)}) collective-permute-start(bf16[128,1024]{1,0:T(8,128)(2,1)} %x0.1), channel_id=1, source_target_pairs={{0,2},{2,0},{1,3},{3,1},{4,6},{6,4},{5,7},{7,5},{8,10},{10,8},{9,1... | collective-permute-start | bytes 786440 | tf_op jit(solution)/shard_map/ppermute | solution.py:328
  2.8 10.6 %collective-permute-start.2 = (bf16[128,1024]{1,0:T(8,128)(2,1)}, bf16[128,1024]{1,0:T(8,128)(2,1)S(1)}, u32[]{:S(2)}, u32[]{:S(2)}) collective-permute-start(bf16[128,1024]{1,0:T(8,128)(2,1)} %g0.1), channel_id=1, source_target_pairs={{0,2},{2,0},{1,3},{3,1},{4,6},{6,4},{5,7},{7,5},{8,10},{10,8},{9,1... | collective-permute-start | bytes 786440 | tf_op jit(solution)/shard_map/ppermute | solution.py:328
  2.9 13.0 %collective-permute-start.4 = (bf16[128,1024]{1,0:T(8,128)(2,1)}, bf16[128,1024]{1,0:T(8,128)(2,1)S(1)}, u32[]{:S(2)}, u32[]{:S(2)}) collective-permute-start(bf16[128,1024]{1,0:T(8,128)(2,1)} %x0.1), channel_id=1, source_target_pairs={{0,1},{1,0},{2,3},{3,2},{4,5},{5,4},{6,7},{7,6},{8,9},{9,8},{10,11... | collective-permute-start | bytes 786440 | tf_op jit(solution)/shard_map/ppermute | solution.py:325
  6.0 9.9 %collective-permute-start.5 = (bf16[128,1024]{1,0:T(8,128)(2,1)}, bf16[128,1024]{1,0:T(8,128)(2,1)S(1)}, u32[]{:S(2)}, u32[]{:S(2)}) collective-permute-start(bf16[128,1024]{1,0:T(8,128)(2,1)} %g0.1), channel_id=1, source_target_pairs={{0,1},{1,0},{2,3},{3,2},{4,5},{5,4},{6,7},{7,6},{8,9},{9,8},{10,11... | collective-permute-start | bytes 786440 | tf_op jit(solution)/shard_map/ppermute | solution.py:325
  7.8 18.6 %collective-permute-start.1 = (bf16[128,1024]{1,0:T(8,128)(2,1)S(1)}, bf16[128,1024]{1,0:T(8,128)(2,1)S(1)}, u32[]{:S(2)}, u32[]{:S(2)}) collective-permute-start(bf16[128,1024]{1,0:T(8,128)(2,1)S(1)} %collective-permute-done.x0), channel_id=1, source_target_pairs={{0,1},{1,0},{2,3},{3,2},{4,5},{5,4},{6,7},{7,6},{8,9},{9,8},{10,11... | collective-permute-start | bytes 786440 | tf_op jit(solution)/shard_map/ppermute | solution.py:325
  13.4 13.0 %collective-permute-start.3 = (bf16[128,1024]{1,0:T(8,128)(2,1)S(1)}, bf16[128,1024]{1,0:T(8,128)(2,1)S(1)}, u32[]{:S(2)}, u32[]{:S(2)}) collective-permute-start(bf16[128,1024]{1,0:T(8,128)(2,1)S(1)} %collective-permute-done.2.g0), channel_id=1, source_target_pairs={{0,1},{1,0},{2,3},{3,2},{4,5},{5,4},{6,7},{7,6},{8,9},{9,8},{10,11... | collective-permute-start | bytes 786440 | tf_op jit(solution)/shard_map/ppermute | solution.py:325
  15.9 2.2 %copy-start = (bf16[4096,512]{1,0:T(8,128)(2,1)S(1)}, bf16[4096,512]{1,0:T(8,128)(2,1)}, u32[]{:S(2)}) copy-start(bf16[4096,512]{1,0:T(8,128)(2,1)} %wq.7) | copy-start | bytes 12582916
  18.0 2.2 %copy-start.3 = (bf16[512,4096]{1,0:T(8,128)(2,1)S(1)}, bf16[512,4096]{1,0:T(8,128)(2,1)}, u32[]{:S(2)}) copy-start(bf16[512,4096]{1,0:T(8,128)(2,1)} %wo.3) | copy-start | bytes 12582916
  20.2 1.2 copy-start.5
  21.5 1.2 copy-start.7
  22.7 0.9 copy-start.9
  23.6 0.9 copy-start.10
  24.6 2.2 %copy-start.1 = (bf16[4096,512]{1,0:T(8,128)(2,1)S(1)}, bf16[4096,512]{1,0:T(8,128)(2,1)}, u32[]{:S(2)}) copy-start(bf16[4096,512]{1,0:T(8,128)(2,1)} %wq.7) | copy-start | bytes 12582916
  24.6 3.5 %copy-start.4 = (bf16[512,4096]{1,0:T(8,128)(2,1)S(1)}, bf16[512,4096]{1,0:T(8,128)(2,1)}, u32[]{:S(2)}) copy-start(bf16[512,4096]{1,0:T(8,128)(2,1)} %wo.3) | copy-start | bytes 12582916
  24.6 3.7 %copy-start.6 = (bf16[4096,128]{1,0:T(8,128)(2,1)S(1)}, bf16[4096,128]{1,0:T(8,128)(2,1)}, u32[]{:S(2)}) copy-start(bf16[4096,128]{1,0:T(8,128)(2,1)} %wk.7) | copy-start | bytes 3145732
  26.3 43.6 %copy-start.13 = (s32[8192]{0:T(1024)S(1)}, s32[8192]{0:T(1024)}, u32[]{:S(2)}) copy-start(s32[8192]{0:T(1024)} %param.13) | copy-start | bytes 98308
  31.1 38.8 %all-to-all-start = ((bf16[16,128,256]{2,1,0:T(8,128)(2,1)}), bf16[16,128,256]{2,1,0:T(8,128)(2,1)S(1)}, u32[]{:S(2)}, u32[]{:S(2)}) async-start(bf16[16,128,256]{2,1,0:T(8,128)(2,1)} %broadcast_in_dim.3), calls=%async_computation | async-start | bytes 2097152 | tf_op jit(solution)/shard_map/all_to_all | solution.py:338
  42.1 13.7 %collective-permute-start.8 = (bf16[128,1024]{1,0:T(8,128)(2,1)S(1)}, bf16[128,1024]{1,0:T(8,128)(2,1)S(1)}, u32[]{:S(2)}, u32[]{:S(2)}) collective-permute-start(bf16[128,1024]{1,0:T(8,128)(2,1)S(1)} %get-tuple-element.11.qd0), channel_id=1, source_target_pairs={{0,24},{8,0},{16,8},{24,16},{1,25},{9,1},{17,9},{25,17},{2,26},{10... | collective-permute-start | bytes 786440 | tf_op jit(solution)/shard_map/ppermute | solution.py:337
  44.9 10.9 %collective-permute-start.7 = (bf16[128,1024]{1,0:T(8,128)(2,1)S(1)}, bf16[128,1024]{1,0:T(8,128)(2,1)S(1)}, u32[]{:S(2)}, u32[]{:S(2)}) collective-permute-start(bf16[128,1024]{1,0:T(8,128)(2,1)S(1)} %get-tuple-element.11.qd0), channel_id=1, source_target_pairs={{0,16},{8,24},{16,0},{24,8},{1,17},{9,25},{17,1},{25,9},{2,18},{10... | collective-permute-start | bytes 786440 | tf_op jit(solution)/shard_map/ppermute | solution.py:337
  45.3 15.0 %collective-permute-start.6 = (bf16[128,1024]{1,0:T(8,128)(2,1)S(1)}, bf16[128,1024]{1,0:T(8,128)(2,1)S(1)}, u32[]{:S(2)}, u32[]{:S(2)}) collective-permute-start(bf16[128,1024]{1,0:T(8,128)(2,1)S(1)} %get-tuple-element.11.qd0), channel_id=1, source_target_pairs={{0,8},{8,16},{16,24},{24,0},{1,9},{9,17},{17,25},{25,1},{2,10},{10... | collective-permute-start | bytes 786440 | tf_op jit(solution)/shard_map/ppermute | solution.py:337
  72.2 4.0 %collective-permute-start.11 = (f32[16,512]{1,0:T(8,128)S(1)}, f32[16,512]{1,0:T(8,128)S(1)}, u32[]{:S(2)}, u32[]{:S(2)}) collective-permute-start(f32[16,512]{1,0:T(8,128)S(1)} %shard_map.96.st0), channel_id=1, source_target_pairs={{0,24},{8,0},{16,8},{24,16},{1,25},{9,1},{17,9},{25,17},{2,26},{10... | collective-permute-start | bytes 98312 | tf_op jit(solution)/shard_map/ppermute | solution.py:343
  75.2 4.3 %collective-permute-start.10 = (f32[16,512]{1,0:T(8,128)S(1)}, f32[16,512]{1,0:T(8,128)S(1)}, u32[]{:S(2)}, u32[]{:S(2)}) collective-permute-start(f32[16,512]{1,0:T(8,128)S(1)} %shard_map.96.st0), channel_id=1, source_target_pairs={{0,16},{8,24},{16,0},{24,8},{1,17},{9,25},{17,1},{25,9},{2,18},{10... | collective-permute-start | bytes 98312 | tf_op jit(solution)/shard_map/ppermute | solution.py:343
  75.5 4.3 %collective-permute-start.9 = (f32[16,512]{1,0:T(8,128)S(1)}, f32[16,512]{1,0:T(8,128)S(1)}, u32[]{:S(2)}, u32[]{:S(2)}) collective-permute-start(f32[16,512]{1,0:T(8,128)S(1)} %shard_map.96.st0), channel_id=1, source_target_pairs={{0,8},{8,16},{16,24},{24,0},{1,9},{9,17},{17,25},{25,1},{2,10},{10... | collective-permute-start | bytes 98312 | tf_op jit(solution)/shard_map/ppermute | solution.py:343
  84.4 0.7 copy-start.11
  85.0 0.6 copy-start.12
  85.7 55.9 %copy-start.8 = (bf16[4096,128]{1,0:T(8,128)(2,1)S(1)}, bf16[4096,128]{1,0:T(8,128)(2,1)}, u32[]{:S(2)}) copy-start(bf16[4096,128]{1,0:T(8,128)(2,1)} %wv.7) | copy-start | bytes 3145732
  85.7 54.4 %all-to-all-start.1 = ((bf16[16,128,256]{2,1,0:T(8,128)(2,1)}), bf16[16,128,256]{2,1,0:T(8,128)(2,1)}, u32[]{:S(2)}, u32[]{:S(2)}) async-start(bf16[16,128,256]{2,1,0:T(8,128)(2,1)} %bitcast.6), calls=%async_computation.1 | async-start | bytes 2097152 | tf_op jit(solution)/shard_map/all_to_all | solution.py:347
  114.0 4.1 %collective-permute-start.12 = (bf16[128,512]{1,0:T(8,128)(2,1)}, bf16[128,512]{1,0:T(8,128)(2,1)S(1)}, u32[]{:S(2)}, u32[]{:S(2)}) collective-permute-start(bf16[128,512]{1,0:T(8,128)(2,1)} %copy-done.12), channel_id=1, source_target_pairs={{0,24},{8,0},{16,8},{24,16},{1,25},{9,1},{17,9},{25,17},{2,26},{10... | collective-permute-start | bytes 393224 | tf_op jit(solution)/shard_map/ppermute | solution.py:346
  114.4 5.6 %collective-permute-start.13 = (bf16[128,512]{1,0:T(8,128)(2,1)}, bf16[128,512]{1,0:T(8,128)(2,1)S(1)}, u32[]{:S(2)}, u32[]{:S(2)}) collective-permute-start(bf16[128,512]{1,0:T(8,128)(2,1)} %copy-done.11), channel_id=1, source_target_pairs={{0,16},{8,24},{16,0},{24,8},{1,17},{9,25},{17,1},{25,9},{2,18},{10... | collective-permute-start | bytes 393224 | tf_op jit(solution)/shard_map/ppermute | solution.py:346
  115.3 6.0 %collective-permute-start.14 = (bf16[128,512]{1,0:T(8,128)(2,1)S(1)}, bf16[128,512]{1,0:T(8,128)(2,1)S(1)}, u32[]{:S(2)}, u32[]{:S(2)}) collective-permute-start(bf16[128,512]{1,0:T(8,128)(2,1)S(1)} %get-tuple-element.15), channel_id=1, source_target_pairs={{0,8},{8,16},{16,24},{24,0},{1,9},{9,17},{17,25},{25,1},{2,10},{10... | collective-permute-start | bytes 393224 | tf_op jit(solution)/shard_map/ppermute | solution.py:346
  141.5 9.3 %copy-start.15 = (bf16[128,128]{1,0:T(8,128)(2,1)}, bf16[128,128]{1,0:T(8,128)(2,1)S(1)}, u32[]{:S(2)}) copy-start(bf16[128,128]{1,0:T(8,128)(2,1)S(1)} %slice.43) | copy-start | bytes 98308
  141.5 9.2 %copy-start.14 = (bf16[128,128]{1,0:T(8,128)(2,1)}, bf16[128,128]{1,0:T(8,128)(2,1)S(1)}, u32[]{:S(2)}) copy-start(bf16[128,128]{1,0:T(8,128)(2,1)S(1)} %fusion.3) | copy-start | bytes 98308
  141.5 2.2 %copy-start.2 = (bf16[4096,512]{1,0:T(8,128)(2,1)S(1)}, bf16[4096,512]{1,0:T(8,128)(2,1)}, u32[]{:S(2)}) copy-start(bf16[4096,512]{1,0:T(8,128)(2,1)} %wq.7) | copy-start | bytes 12582916
  145.1 5.8 %collective-permute-start.16 = (bf16[128,1024]{1,0:T(8,128)(2,1)S(1)}, bf16[128,1024]{1,0:T(8,128)(2,1)S(1)}, u32[]{:S(2)}, u32[]{:S(2)}) collective-permute-start(bf16[128,1024]{1,0:T(8,128)(2,1)S(1)} %slice_bitcast_fusion), channel_id=1, source_target_pairs={{0,1},{1,0},{2,3},{3,2},{4,5},{5,4},{6,7},{7,6},{8,9},{9,8},{10,11... | collective-permute-start | bytes 786440 | tf_op jit(solution)/shard_map/ppermute | solution.py:325
  150.8 1.6 %collective-permute-start.15 = (bf16[128,1024]{1,0:T(8,128)(2,1)S(1)}, bf16[128,1024]{1,0:T(8,128)(2,1)S(1)}, u32[]{:S(2)}, u32[]{:S(2)}) collective-permute-start(bf16[128,1024]{1,0:T(8,128)(2,1)S(1)} %slice_bitcast_fusion.2), channel_id=1, source_target_pairs={{0,1},{1,0},{2,3},{3,2},{4,5},{5,4},{6,7},{7,6},{8,9},{9,8},{10,11... | collective-permute-start | bytes 786440 | tf_op jit(solution)/shard_map/ppermute | solution.py:325
  151.0 7.5 %collective-permute-start.17 = (bf16[128,1024]{1,0:T(8,128)(2,1)S(1)}, bf16[128,1024]{1,0:T(8,128)(2,1)S(1)}, u32[]{:S(2)}, u32[]{:S(2)}) collective-permute-start(bf16[128,1024]{1,0:T(8,128)(2,1)S(1)} %fusion), channel_id=1, source_target_pairs={{0,2},{2,0},{1,3},{3,1},{4,6},{6,4},{5,7},{7,5},{8,10},{10,8},{9,1... | collective-permute-start | bytes 786440 | tf_op jit(solution)/shard_map/ppermute | solution.py:328

commit v2 on v0

v2 whole, which is shorter than its diff:
```python
import functools

import jax
import jax.numpy as jnp
from jax import lax
from jax.experimental import pallas as pl
from jax.experimental.pallas import tpu as pltpu
from jax.sharding import Mesh
from jax.sharding import PartitionSpec as P

HEAD = 128
FACTOR = HEAD**-0.5
LOG2E = 1.4426950408889634
SCALE2 = FACTOR * LOG2E
NEG_FILL = -1e30
BLOCK = 128
HEADS = 4
ROWS = HEADS * BLOCK
CHUNK = 2 * BLOCK
FAR_FLOPS = 15_000_000_000
PARTS = 4
PART = 2048 // PARTS
STEP = 512
VMEM_LIMIT = 20 * 1024 * 1024
BF16 = jnp.bfloat16
F32 = jnp.float32


def shifted(size, step):
    return [(i, (i + step) % size) for i in range(size)]


def contract_last(left, right):
    return lax.dot_general(
        left, right, (((1,), (1,)), ((), ())), preferred_element_type=F32
    )


def matmul(left, right):
    return jnp.dot(left, right, preferred_element_type=F32)


PAIR = 2048


def near_kernel(
    place, x0, x1, g0, g1, wq, wk, wv, wo,
    x_half, g_half, far_q, far_k, far_v, far_o,
    near_q, near_k, near_v, near_o, g_buf, sems,
):
    xl, core = place[3], place[4]
    near = pl.ds(pl.multiple_of(xl * PAIR, PAIR), PAIR)
    far = pl.ds(pl.multiple_of((1 - xl) * PAIR, PAIR), PAIR)
    copies = []
    for rows, targets in (
        (near, (near_q, near_k, near_v, near_o)),
        (far, (far_q, far_k, far_v, far_o)),
    ):
        for source, target in zip((wq, wk, wv, wo), targets):
            part = source.at[:, rows] if source is wo else source.at[rows, :]
            copies.append(pltpu.make_async_copy(part, target, sems.at[len(copies)]))
    for copy in copies:
        copy.start()
    own, other = core_halves(core)
    for copy, weight, low, high in (
        (copies[0], near_q, 256, 768),
        (copies[1], near_k, 0, 128),
        (copies[2], near_v, 128, 256),
    ):
        copy.wait()
        x_half[:, low:high] = matmul(x0[...], weight[own, :]) + matmul(x1[...], weight[other, :])
    copies[3].wait()
    g_buf[...] = contract_last(g0[...], near_o[:, own]) + contract_last(g1[...], near_o[:, other])
    copies.append(pltpu.make_async_copy(g_buf, g_half, sems.at[8]))
    copies[8].start()
    for copy in copies[4:]:
        copy.wait()


def core_halves(core):
    return [pl.ds(pl.multiple_of(c * 1024, 1024), 1024) for c in (core, 1 - core)]


def far_inputs_kernel(place, x2, x3, wq, wk, wv, x_half, kv, q, kv_buf, q_buf, sems):
    own, other = core_halves(place[4])

    def product(weight, low, high):
        return (
            x_half[:, low:high]
            + matmul(x2[...], weight[own, :])
            + matmul(x3[...], weight[other, :])
        ).astype(BF16)

    kv_buf[:, :HEAD] = product(wk, 0, 128)
    kv_buf[:, HEAD:] = product(wv, 128, 256)
    copies = [pltpu.make_async_copy(kv_buf, kv.at[i], sems.at[i]) for i in range(16)]
    for copy in copies:
        copy.start()
    q_buf[...] = product(wq, 256, 768)
    copies.append(pltpu.make_async_copy(q_buf, q, sems.at[16]))
    copies[16].start()
    for copy in copies:
        copy.wait()


def far_grads_kernel(place, g2, g3, wo, g_half, q, out, g_buf, out_buf, sems):
    own, other = core_halves(place[4])
    fetch_g = pltpu.make_async_copy(g_half, g_buf, sems.at[0])
    fetch_q = pltpu.make_async_copy(q, out_buf.at[:, :ROWS], sems.at[1])
    fetch_g.start()
    fetch_q.start()
    far = contract_last(g2[...], wo[:, own]) + contract_last(g3[...], wo[:, other])
    fetch_g.wait()
    out_buf[:, ROWS:] = (g_buf[...] + far).astype(BF16)
    fetch_q.wait()
    store = pltpu.make_async_copy(out_buf, out, sems.at[2])
    store.start()
    store.wait()


def whole_call(
    kernel, operands, outs, scratch=(), hbm=(), hbm_outs=(), flops=0, traffic=0, exps=0
):
    vmem = pl.BlockSpec(memory_space=pltpu.VMEM)
    operands = list(operands)
    in_specs = [vmem] * len(operands)
    in_specs[0] = pl.BlockSpec(memory_space=pltpu.SMEM)
    for i in hbm:
        in_specs[i] = pl.BlockSpec(memory_space=pltpu.HBM)
        operands[i] = pltpu.with_memory_space_constraint(operands[i], pltpu.HBM)
    return pl.pallas_call(
        kernel,
        in_specs=in_specs,
        out_specs=[
            pl.BlockSpec(memory_space=pltpu.HBM) if i in hbm_outs else vmem
            for i in range(len(outs))
        ],
        out_shape=outs,
        scratch_shapes=list(scratch),
        compiler_params=pltpu.CompilerParams(vmem_limit_bytes=VMEM_LIMIT),
        cost_estimate=pl.CostEstimate(flops=flops, bytes_accessed=traffic, transcendentals=exps),
    )(*operands)


def stack_heads(ref, first):
    return jnp.concatenate(
        [ref[:, first + h * HEAD : first + (h + 1) * HEAD] for h in range(HEADS)], axis=0
    )


def visible_tile(times, key_block, query_block):
    key_row = jnp.broadcast_to(times[pl.ds(key_block, 1), :], (BLOCK, BLOCK))
    seen = key_row.T <= times[pl.ds(query_block, 1), :]
    return jnp.concatenate([seen] * HEADS, axis=1)


def for_tiles(place, times, tile):
    z, y, xh = place[0], place[1], place[2]

    def past(first, keys):
        for part in range(PARTS):
            tile(pl.multiple_of(first, CHUNK), keys, part * PART, PART, None)

    def some(i, carry):
        past(i * STEP, STEP)
        return carry

    lax.fori_loop(0, z * CHUNK // STEP, some, 0)
    if STEP > CHUNK:

        @pl.when(z % 2 == 1)
        def _():
            past((z - 1) * CHUNK, CHUNK)

    for s in range(4):
        query_block = 8 * z + 2 * ((y - s + 4) % 4) + xh
        mask = jnp.concatenate(
            [visible_tile(times, 8 * z + 2 * y + h, query_block) for h in range(2)], axis=0
        )
        tile(pl.multiple_of(z * CHUNK, CHUNK), CHUNK, s * ROWS, ROWS, mask)

    @pl.when((z < 7) & (y == 0) & (xh == 1))
    def _():
        mask = visible_tile(times, 8 * (z + 1), 8 * z + 7)
        tile(pl.multiple_of((z + 1) * CHUNK, CHUNK), BLOCK, ROWS, ROWS, mask)


def fetch(times, own, times_buf, own_buf, sems):
    copies = [
        pltpu.make_async_copy(own, own_buf, sems.at[0]),
        pltpu.make_async_copy(times, times_buf, sems.at[1]),
    ]
    for copy in copies:
        copy.start()
    return copies


FETCHED = [
    pltpu.VMEM((64, BLOCK), jnp.int32),
    pltpu.VMEM((BLOCK, 1024), BF16),
    pltpu.SemaphoreType.DMA((2,)),
]


def stack_blocks(blocks, copies, q_rows, g_rows):
    for s in (1, 2, 3, 0):
        if s == 0:
            for copy in copies:
                copy.wait()
        q_rows[s * ROWS : (s + 1) * ROWS, :] = stack_heads(blocks[s], 0)
        g_rows[s * ROWS : (s + 1) * ROWS, :] = stack_heads(blocks[s], 512)


def stats_kernel(
    place, times_hbm, kv, qd0, qd1, qd2, qd3, out, times, own, sems, q_rows, g_rows
):
    copies = fetch(times_hbm, qd0, times, own, sems)
    stack_blocks((own, qd1, qd2, qd3), copies, q_rows, g_rows)
    out[0:1, :] = jnp.full((1, 4 * ROWS), NEG_FILL, F32)
    out[1:4, :] = jnp.zeros((3, 4 * ROWS), F32)

    def tile(first, count, row, rows, seen):
        cols = slice(row, row + rows)
        keys = kv[pl.ds(first, count), :HEAD]
        values = kv[pl.ds(first, count), HEAD:]
        scores = contract_last(keys, q_rows[cols, :]) * SCALE2
        if seen is not None:
            scores = jnp.where(seen, scores, NEG_FILL)
        old = out[0:1, cols]
        top = jnp.maximum(old, jnp.max(scores, axis=0, keepdims=True))
        prob = jnp.exp2(scores - top)
        if seen is not None:
            prob = jnp.where(seen, prob, 0.0)
        prob_grad = contract_last(values, g_rows[cols, :])
        shrink = jnp.exp2(old - top)
        out[0:1, cols] = top
        out[1:2, cols] = out[1:2, cols] * shrink + jnp.sum(prob, axis=0, keepdims=True)
        out[2:3, cols] = out[2:3, cols] * shrink + jnp.sum(
            prob * prob_grad, axis=0, keepdims=True
        )

    for_tiles(place, times, tile)


def stats(place, times, kv, blocks):
    (out,) = whole_call(
        stats_kernel,
        (place, times, kv, *blocks),
        [jax.ShapeDtypeStruct((4, 4 * ROWS), F32)],
        FETCHED + [pltpu.VMEM((4 * ROWS, HEAD), BF16)] * 2,
        hbm=(1, 3),
        flops=4 * 2048 * 2048 * 128,
        traffic=2 << 20,
        exps=2048 * 2048,
    )
    return out


def grads_kernel(
    place, times_hbm, kv, qd0, qd1, qd2, qd3, st0, st1, st2, st3,
    dkv, dq0, dq1, dq2, dq3,
    times, own, sems, sums, q_rows, g_rows, q_sum, row_stats, dkv_buf, dq_buf, out_sems,
):
    copies = fetch(times_hbm, qd0, times, own, sems)
    sums[...] = jnp.zeros_like(sums)
    q_sum[...] = jnp.zeros_like(q_sum)
    for s in range(4):
        cols = slice(s * ROWS, (s + 1) * ROWS)
        tops, norms, dots = [], [], []
        for k, st in enumerate((st0, st1, st2, st3)):
            first = ((s - k) % 4) * ROWS
            tops.append(st[0:1, first : first + ROWS])
            norms.append(st[1:2, first : first + ROWS])
            dots.append(st[2:3, first : first + ROWS])
        top = functools.reduce(jnp.maximum, tops)
        scales = [jnp.exp2(t - top) for t in tops]
        norm = sum(n * f for n, f in zip(norms, scales))
        row_stats[0:1, cols] = top + jnp.log2(norm)
        row_stats[1:2, cols] = sum(d * f for d, f in zip(dots, scales)) / norm
    stack_blocks((own, qd1, qd2, qd3), copies, q_rows, g_rows)

    def tile(first, count, row, rows, seen):
        cols = slice(row, row + rows)
        keys = kv[pl.ds(first, count), :HEAD]
        values = kv[pl.ds(first, count), HEAD:]
        q, g = q_rows[cols, :], g_rows[cols, :]
        prob = jnp.exp2(contract_last(keys, q) * SCALE2 - row_stats[0:1, cols])
        if seen is not None:
            prob = jnp.where(seen, prob, 0.0)
        prob_grad = contract_last(values, g)
        score_grad = (prob * (prob_grad - row_stats[1:2, cols])).astype(BF16)
        sums[pl.ds(first, count), :HEAD] += matmul(score_grad, q)
        sums[pl.ds(first, count), HEAD:] += matmul(prob.astype(BF16), g)
        q_sum[:, cols] += lax.dot_general(
            keys, score_grad, (((0,), (0,)), ((), ())), preferred_element_type=F32
        )

    for_tiles(place, times, tile)
    outs = []
    for i in range(16):
        dkv_buf[i] = sums[i * BLOCK : (i + 1) * BLOCK, :].astype(BF16)
        if i % 4 == 3:
            part = pl.ds(i - 3, 4)
            outs.append(
                pltpu.make_async_copy(dkv_buf.at[part], dkv.at[part], out_sems.at[i // 4])
            )
            outs[-1].start()
    for s, dq in enumerate((dq0, dq1, dq2, dq3)):
        for h in range(HEADS):
            part = q_sum[:, s * ROWS + h * HEAD : s * ROWS + (h + 1) * HEAD]
            dq_buf[s, :, h * HEAD : (h + 1) * HEAD] = (part.T * FACTOR).astype(BF16)
        outs.append(pltpu.make_async_copy(dq_buf.at[s], dq, out_sems.at[4 + s]))
        outs[-1].start()
    for copy in outs:
        copy.wait()


def grads(place, times, kv, blocks, gathered):
    return whole_call(
        grads_kernel,
        (place, times, kv, *blocks, *gathered),
        [jax.ShapeDtypeStruct((16, BLOCK, 2 * HEAD), BF16)]
        + [jax.ShapeDtypeStruct((BLOCK, ROWS), BF16)] * 4,
        FETCHED
        + [
            pltpu.VMEM((16 * BLOCK, 2 * HEAD), F32),
            pltpu.VMEM((4 * ROWS, HEAD), BF16),
            pltpu.VMEM((4 * ROWS, HEAD), BF16),
            pltpu.VMEM((HEAD, 4 * ROWS), F32),
            pltpu.VMEM((8, 4 * ROWS), F32),
            pltpu.VMEM((16, BLOCK, 2 * HEAD), BF16),
            pltpu.VMEM((4, BLOCK, ROWS), BF16),
            pltpu.SemaphoreType.DMA((8,)),
        ],
        hbm=(1, 3),
        hbm_outs=(0, 1, 2, 3, 4),
        flops=10 * 2048 * 2048 * 128,
        traffic=4 << 20,
        exps=2048 * 2048,
    )


def feature_rows(place, flip):
    first = (2 * place[3] + place[4]) ^ flip
    return pl.ds(pl.multiple_of(first * 1024, 1024), 1024)


def query_back_kernel(
    place, dq0, dq1, dq2, dq3, wq, wk, wv, far0, far1, near1, near0, out_k, out_v, held, sems
):
    copies = [
        pltpu.make_async_copy(wq.at[feature_rows(place, flip), :], held.at[i], sems.at[i])
        for i, flip in enumerate((3, 2, 1, 0))
    ]
    copies.append(pltpu.make_async_copy(wk, out_k, sems.at[4]))
    copies.append(pltpu.make_async_copy(wv, out_v, sems.at[5]))
    for copy in copies:
        copy.start()
    parts = [d[...].astype(F32) for d in (dq0, dq1, dq2, dq3)]
    total = (parts[0] + parts[1] + parts[2] + parts[3]).astype(BF16)
    for i, out in enumerate((far0, far1, near1, near0)):
        copies[i].wait()
        out[...] = contract_last(total, held[i]).astype(out.dtype)
    copies[4].wait()
    copies[5].wait()


def key_terms(place, flip, dk, dv, wk, wv):
    rows = feature_rows(place, flip)
    return contract_last(dk, wk[rows, :]) + contract_last(dv, wv[rows, :])


def key_far_kernel(place, parts, wk, wv, queries, far0, far1, dk, dv, dkv):
    total = parts[0].astype(F32)
    for i in range(1, 16):
        total = total + parts[i].astype(F32)
    dk[...] = (total[:, :HEAD] * FACTOR).astype(BF16)
    dv[...] = total[:, HEAD:].astype(BF16)
    dkv[:, :HEAD] = dk[...]
    dkv[:, HEAD:] = dv[...]
    far0[...] = key_terms(place, 3, dk[...], dv[...], wk, wv).astype(BF16)
    far1[...] = queries[...].astype(F32) + key_terms(place, 2, dk[...], dv[...], wk, wv)


def key_near_kernel(place, dkv, wk, wv, queries, near1, near0):
    dk, dv = dkv[:, :HEAD], dkv[:, HEAD:]
    near1[...] = key_terms(place, 1, dk, dv, wk, wv).astype(BF16)
    near0[...] = queries[...].astype(F32) + key_terms(place, 0, dk, dv, wk, wv)


def local(inputs, out_grad, w_query, key_weight, value_weight, w_output, times):
    axes = ("z", "y", "xh", "xl", "core")
    place = jnp.stack([lax.axis_index(name) for name in axes]).astype(jnp.int32)
    times2d = times.reshape(64, BLOCK)
    swap = shifted(2, 1)

    def to_core(value):
        return lax.ppermute(value, "core", swap)

    def to_xl(value):
        return lax.ppermute(value, "xl", swap)

    def shape(*dims, kind=BF16):
        return jax.ShapeDtypeStruct(dims, kind)

    x2, g2 = to_xl(inputs), to_xl(out_grad)
    x1, g1 = to_core(inputs), to_core(out_grad)
    held = [
        shape(PAIR, ROWS), shape(PAIR, HEAD), shape(PAIR, HEAD), shape(ROWS, PAIR)
    ]
    x_half, g_half, far_q, far_k, far_v, far_o = whole_call(
        near_kernel,
        (place, inputs, x1, out_grad, g1, w_query, key_weight, value_weight, w_output),
        [shape(BLOCK, 768, kind=F32), shape(BLOCK, ROWS, kind=F32)] + held,
        [pltpu.VMEM(h.shape, BF16) for h in held]
        + [pltpu.VMEM((BLOCK, ROWS), F32), pltpu.SemaphoreType.DMA((9,))],
        hbm=(5, 6, 7, 8),
        hbm_outs=(1,),
        flops=2 * 128 * 2048 * 1280,
        traffic=10 << 20,
    )
    x2, x_half, g_half = lax.optimization_barrier((x2, x_half, g_half))
    x3 = to_core(x2)
    kv_own, q_own = whole_call(
        far_inputs_kernel,
        (place, x2, x3, far_q, far_k, far_v, x_half),
        [shape(16, BLOCK, 2 * HEAD), shape(BLOCK, ROWS)],
        [
            pltpu.VMEM((BLOCK, 2 * HEAD), BF16),
            pltpu.VMEM((BLOCK, ROWS), BF16),
            pltpu.SemaphoreType.DMA((17,)),
        ],
        hbm_outs=(0, 1),
        flops=2 * 128 * 2048 * 768,
        traffic=4 << 20,
    )
    g2, q_own = lax.optimization_barrier((g2, q_own))
    g3 = to_core(g2)
    (qd_own,) = whole_call(
        far_grads_kernel,
        (place, g2, g3, far_o, g_half, q_own),
        [shape(BLOCK, 1024)],
        [
            pltpu.VMEM((BLOCK, ROWS), F32),
            pltpu.VMEM((BLOCK, 1024), BF16),
            pltpu.SemaphoreType.DMA((3,)),
        ],
        hbm=(4, 5),
        hbm_outs=(0,),
        flops=FAR_FLOPS,
        traffic=3 << 20,
    )
    kv = lax.all_to_all(kv_own, ("z", "xh"), 0, 0, tiled=True).reshape(16 * BLOCK, 2 * HEAD)
    blocks = [qd_own] + [lax.ppermute(qd_own, "y", shifted(4, s)) for s in (1, 2, 3)]

    own_stats = stats(place, times2d, kv, blocks)
    gathered = [own_stats] + [lax.ppermute(own_stats, "y", shifted(4, s)) for s in (1, 2, 3)]
    dkv, *dqs = grads(place, times2d, kv, blocks, gathered)

    dkv_parts = lax.all_to_all(dkv, ("z", "xh"), 0, 0, tiled=True)
    dq_parts = [dqs[0]] + [lax.ppermute(dqs[s], "y", shifted(4, -s)) for s in (1, 2, 3)]

    def add(*values):
        return sum(v.astype(F32) for v in values)

    far0, far1, near1, near0, held_k, held_v = whole_call(
        query_back_kernel,
        (place, *dq_parts, w_query, key_weight, value_weight),
        [shape(BLOCK, 1024)] * 4 + [shape(2 * PAIR, HEAD)] * 2,
        [pltpu.VMEM((4, 1024, ROWS), BF16), pltpu.SemaphoreType.DMA((6,))],
        hbm=(5, 6, 7),
        flops=2 * 128 * 4096 * 512,
        traffic=8 << 20,
    )
    far_query = add(far1, to_core(far0)).astype(BF16)
    near_query = add(near0, to_core(near1)).astype(BF16)

    far0, far1, dk, dv, dkv_own = whole_call(
        key_far_kernel,
        (place, dkv_parts, held_k, held_v, far_query),
        [shape(BLOCK, 1024), shape(BLOCK, 1024, kind=F32)]
        + [shape(BLOCK, HEAD)] * 2
        + [shape(BLOCK, 2 * HEAD)],
        flops=2 * 128 * 2048 * 256,
        traffic=2 << 20,
    )
    far_sum, dkv_own = lax.optimization_barrier(
        (add(far1, to_core(far0)).astype(BF16), dkv_own)
    )
    from_far = to_xl(far_sum)
    near1, near0 = whole_call(
        key_near_kernel,
        (place, dkv_own, held_k, held_v, near_query),
        [shape(BLOCK, 1024), shape(BLOCK, 1024, kind=F32)],
        flops=2 * 128 * 2048 * 256,
        traffic=2 << 20,
    )
    input_grad = add(near0, to_core(near1), from_far).astype(BF16)
    return input_grad, dk, dv


def solution(mesh):
    split = Mesh(mesh.devices.reshape(8, 4, 2, 2, 2), ("z", "y", "xh", "xl", "core"))
    ctx, tp = ("z", "y", "xh"), ("xl", "core")
    in_specs = (
        P(ctx, tp),
        P(ctx, tp),
        P(None, tp),
        P(None, tp),
        P(None, tp),
        P(tp, None),
        P(),
    )
    out_specs = (P(ctx, tp), P(ctx, tp), P(ctx, tp))
    return jax.shard_map(
        local, mesh=split, in_specs=in_specs, out_specs=out_specs, check_vma=False
    )
```

time: 899 us -> 130 us (0.14)
  waiting for transfers between devices: 618 us -> 45 us
  matrix products: 131 us -> 0 us
  local copies, waits for them, and re-layouts: 92.5 us -> 4.05 us
  starting transfers between devices: 0.24 us -> 54.3 us
  loops' own time: 33.5 us -> 0 us
  Pallas kernels: 0 us -> 23.6 us
  between operations: 14.3 us -> 0.79 us
    reduce_scatter x2 -> x0, waiting for transfers between devices: 395 us -> none  [the longest x1 328 us: local(): lax.psum_scatter(key_terms, 'ctx', scatter_dimension=0, tiled=True)]
    all_gather x4 -> x0, waiting for transfers between devices: 222 us -> none  [the longest x1 111 us: local(): lax.all_gather(keys_own, 'ctx', axis=0, tiled=True)]
    dot_general x119 -> x0, matrix products: 131 us -> none  [the longest x52 69.1 us: contract_last(): lax.dot_general(left, right, (((1,), (1,)), ((), ())), preferred_element_...]
    dynamic_slice x97 -> x0, local copies, waits for them, and re-layouts: 65.5 us -> none  [the longest x48 36.7 us: key_slices(): key_times = lax.dynamic_slice_in_dim(times, first_row, key_span, 0)]
    another operation x3 -> x0, loops' own time: 33.5 us -> none  [the longest x1 11.5 us: local(): lax.scan(grad_step, jnp.zeros((count, HEAD_SIZE), jnp.float32), block_ids)]
    ppermute x0 -> x20, waiting for transfers between devices: none -> 31.3 us  [the longest x3 10.6 us: local(): lax.ppermute(qd_own, 'y', shifted(4, s))]
    ppermute x0 -> x20, starting transfers between devices: none -> 27.4 us  [the longest x8 15.7 us: to_core(): return lax.ppermute(value, 'core', swap)]
    all_to_all x0 -> x2, starting transfers between devices: none -> 26.9 us  [the longest x1 17.9 us: local(): dkv_parts = lax.all_to_all(dkv, ('z', 'xh'), 0, 0, tiled=True)]
  transfers between devices with their start and end apart: 6 -> 22, of which waited for: 6 -> 17; matrix products, arithmetic and copies ran while one was open for 7% -> 1% of each run, Pallas kernels for 0% -> 12%
where the time goes in v2:
time: 130 us
  starting transfers between devices  54.3 us (42%)
  waiting for transfers between devices  45 us (35%)
  Pallas kernels  23.6 us (18%)
  local copies, waits for them, and re-layouts  4.05 us (3%)
  other arithmetic  2.03 us (2%)
    pallas_call x8, Pallas kernels, whole_call(): pl.pallas_call(kernel, in_specs=in_specs, out_specs=[pl.BlockSpec(memory_...  23.6 us
    all_to_all x1, starting transfers between devices, local(): dkv_parts = lax.all_to_all(dkv, ('z', 'xh'), 0, 0, tiled=True)  17.9 us
    ppermute x8, starting transfers between devices, to_core(): return lax.ppermute(value, 'core', swap)  15.7 us
    ppermute x3, waiting for transfers between devices, local(): lax.ppermute(qd_own, 'y', shifted(4, s))  10.6 us
    all_to_all x1, starting transfers between devices, local(): lax.all_to_all(kv_own, ('z', 'xh'), 0, 0, tiled=True)  9.02 us
    all_to_all x1, waiting for transfers between devices, local(): dkv_parts = lax.all_to_all(dkv, ('z', 'xh'), 0, 0, tiled=True)  7.25 us
    ppermute x3, waiting for transfers between devices, to_xl(): return lax.ppermute(value, 'xl', swap)  6.61 us
    all_to_all x1, waiting for transfers between devices, local(): lax.all_to_all(kv_own, ('z', 'xh'), 0, 0, tiled=True)  6.42 us
  transfers between devices with their start and end apart: 22, of which 17 were waited for; matrix products, arithmetic and copies ran while one was open for 1% of the time, Pallas kernels for 12%

profile of v2, /device:TPU:1, one launch (start us, length us, event | category | flops | bytes accessed | tf_op | source)
XLA Modules:
  0.0 129.8 jit_solution(7209566587441342291)
XLA Ops:
  0.6 3.3 %collective-permute-start.1 = (bf16[128,1024]{1,0:T(8,128)(2,1)}, bf16[128,1024]{1,0:T(8,128)(2,1)S(1)}, u32[]{:S(2)}, u32[]{:S(2)}) collective-permute-start(bf16[128,1024]{1,0:T(8,128)(2,1)} %x0.1), channel_id=1, source_target_pairs={{0,1},{1,0},{2,3},{3,2},{4,5},{5,4},{6,7},{7,6},{8,9},{9,8},{10,11... | collective-permute-start | bytes 786440 | tf_op jit(solution)/shard_map/ppermute | solution.py:398
  4.0 0.1 collective-permute-start.2
  4.1 1.2 collective-permute-done.1.x1
  5.3 0.4 collective-permute-done.2.g1
  5.7 0.9 copy-done
  6.7 5.1 %shard_map.94 = (f32[128,768]{1,0:T(8,128)S(1)}, f32[128,512]{1,0:T(8,128)S(1)}, bf16[2048,512]{1,0:T(8,128)(2,1)S(1)}, bf16[2048,128]{1,0:T(8,128)(2,1)S(1)}, b...) custom-call(s32[5]{0:T(128)S(1)} %stack.23.place, bf16[128,1024]{1,0:T(8,128)(2,1)S(1)} %copy-done, ...), custom_call_target="tpu_custom_call" | custom-call | flops 671088640 | bytes 10485760 | tf_op jit(solution)/shard_map/pallas_call | solution.py:131
  11.8 1.2 collective-permute-start.3
  13.0 1.2 collective-permute-done.3.x3
  14.2 2.1 %shard_map.95 = (bf16[16,128,256]{2,1,0:T(8,128)(2,1)}, bf16[128,512]{1,0:T(8,128)(2,1)S(1)}) custom-call(s32[5]{0:T(128)S(1)} %stack.23.place, bf16[128,1024]{1,0:T(8,128)(2,1)S(1)} %collective-permute-done.x2, bf16[128,1024]{1,0:T(8,128)(2,1)S(1)} %collective-permute-done.3.x3, bf16[2048,512]{1,0:T(8,128)(2,1)S(1)} %get-tuple-element.39.wq, ...), custom_call_target="tpu_custom_call" | custom-call | flops 402653184 | bytes 4194304 | tf_op jit(solution)/shard_map/pallas_call | solution.py:131
  16.3 0.7 copy-done.6
  17.0 9.0 %all-to-all-start = ((bf16[16,128,256]{2,1,0:T(8,128)(2,1)}), bf16[16,128,256]{2,1,0:T(8,128)(2,1)S(1)}, u32[]{:S(2)}, u32[]{:S(2)}) async-start(bf16[16,128,256]{2,1,0:T(8,128)(2,1)} %get-tuple-element.43), calls=%async_computation | async-start | bytes 2097152 | tf_op jit(solution)/shard_map/all_to_all | solution.py:453
  26.0 0.7 collective-permute-start.5
  26.7 0.7 copy-done.4
  27.4 0.5 collective-permute-done.5.g3
  27.9 0.9 copy-done.5
  28.8 2.2 %shard_map.96.qd0 = bf16[128,1024]{1,0:T(8,128)(2,1)S(1)} custom-call(s32[5]{0:T(128)S(1)} %stack.23.place, bf16[128,1024]{1,0:T(8,128)(2,1)S(1)} %copy-done.5, bf16[128,1024]{1,0:T(8,128)(2,1)S(1)} %collective-permute-done.5.g3, bf16[512,2048]{1,0:T(8,128)(2,1)S(1)} %get-tuple-element.46.wo, f32[128,512]{1,0:T(8,128)} %copy-done.3, bf16[128,512]{1,0:T(8,128)(2,1)} %copy-done.6), custom_call_target="tpu_custom_call" | custom-call | flops 15000000512 | bytes 3145728 | tf_op jit(solution)/shard_map/pallas_call | solution.py:131
  31.0 1.4 %collective-permute-start.6 = (bf16[128,1024]{1,0:T(8,128)(2,1)S(1)}, bf16[128,1024]{1,0:T(8,128)(2,1)S(1)}, u32[]{:S(2)}, u32[]{:S(2)}) collective-permute-start(bf16[128,1024]{1,0:T(8,128)(2,1)S(1)} %shard_map.96.qd0), channel_id=1, source_target_pairs={{0,8},{8,16},{16,24},{24,0},{1,9},{9,17},{17,25},{25,1},{2,10},{10... | collective-permute-start | bytes 786440 | tf_op jit(solution)/shard_map/ppermute | solution.py:454
  32.4 2.6 %collective-permute-start.7 = (bf16[128,1024]{1,0:T(8,128)(2,1)S(1)}, bf16[128,1024]{1,0:T(8,128)(2,1)S(1)}, u32[]{:S(2)}, u32[]{:S(2)}) collective-permute-start(bf16[128,1024]{1,0:T(8,128)(2,1)S(1)} %shard_map.96.qd0), channel_id=1, source_target_pairs={{0,16},{8,24},{16,0},{24,8},{1,17},{9,25},{17,1},{25,9},{2,18},{10... | collective-permute-start | bytes 786440 | tf_op jit(solution)/shard_map/ppermute | solution.py:454
  35.0 1.1 collective-permute-start.8
  36.1 3.9 %collective-permute-done.6.qd1 = bf16[128,1024]{1,0:T(8,128)(2,1)S(1)} collective-permute-done((bf16[128,1024]{1,0:T(8,128)(2,1)S(1)}, bf16[128,1024]{1,0:T(8,128)(2,1)S(1)}, u32[]{:S(2)}, u32[]{:S(2)}) %collective-permute-start.6) | collective-permute-done | bytes 262176 | tf_op jit(solution)/shard_map/ppermute | solution.py:454
  40.0 6.7 %collective-permute-done.7.qd2 = bf16[128,1024]{1,0:T(8,128)(2,1)S(1)} collective-permute-done((bf16[128,1024]{1,0:T(8,128)(2,1)S(1)}, bf16[128,1024]{1,0:T(8,128)(2,1)S(1)}, u32[]{:S(2)}, u32[]{:S(2)}) %collective-permute-start.7) | collective-permute-done | bytes 262176 | tf_op jit(solution)/shard_map/ppermute | solution.py:454
  46.7 6.4 %all-to-all-done = bf16[16,128,256]{2,1,0:T(8,128)(2,1)S(1)} async-done(((bf16[16,128,256]{2,1,0:T(8,128)(2,1)}), bf16[16,128,256]{2,1,0:T(8,128)(2,1)S(1)}, u32[]{:S(2)}, u32[]{:S(2)}) %all-to-all-start) | async-done | bytes 1048608 | tf_op jit(solution)/shard_map/all_to_all | solution.py:453
  53.1 2.7 %shard_map.97.st0 = f32[4,2048]{1,0:T(4,128)S(1)} custom-call(s32[5]{0:T(128)S(1)} %stack.23.place, s32[64,128]{1,0:T(8,128)} %bitcast.9, bf16[2048,256]{1,0:T(8,128)(2,1)S(1)} %bitcast.7, bf16[128,1024]{1,0:T(8,128)(2,1)} %copy-done.2, bf16[128,1024]{1,0:T(8,128)(2,1)S(1)} %collective-permute-done.6.qd1, bf16[128,1024]{1,0:T(8,128)(2,1)S(1)} %collective-permute-done.7.qd2, ...), custom_call_target="tpu_custom_call" | custom-call | flops 2147483648 | bytes 2097152 | tf_op jit(solution)/shard_map/pallas_call | solution.py:131
  55.9 3.2 %collective-permute-start.10 = (f32[4,2048]{1,0:T(4,128)S(1)}, f32[4,2048]{1,0:T(4,128)S(1)}, u32[]{:S(2)}, u32[]{:S(2)}) collective-permute-start(f32[4,2048]{1,0:T(4,128)S(1)} %shard_map.97.st0), channel_id=1, source_target_pairs={{0,16},{8,24},{16,0},{24,8},{1,17},{9,25},{17,1},{25,9},{2,18},{10... | collective-permute-start | bytes 98312 | tf_op jit(solution)/shard_map/ppermute | solution.py:457
  59.0 0.8 collective-permute-start.11
  59.8 0.7 collective-permute-start.9
  60.5 1.3 collective-permute-done.11.st3
  61.8 2.0 %collective-permute-done.9.st1 = f32[4,2048]{1,0:T(4,128)S(1)} collective-permute-done((f32[4,2048]{1,0:T(4,128)S(1)}, f32[4,2048]{1,0:T(4,128)S(1)}, u32[]{:S(2)}, u32[]{:S(2)}) %collective-permute-start.9) | collective-permute-done | bytes 32800 | tf_op jit(solution)/shard_map/ppermute | solution.py:457
  63.8 4.7 %shard_map.98 = (bf16[16,128,256]{2,1,0:T(8,128)(2,1)}, bf16[128,512]{1,0:T(8,128)(2,1)S(1)}, bf16[128,512]{1,0:T(8,128)(2,1)S(1)}, bf16[128,512]{1,0:T(8,128)(2,1)S(1)}, bf16[128,512]{1,0:T(8,128)(2,1)S(1)}) custom-call(s32[5]{0:T(128)S(1)} %stack.23.place, s32[64,128]{1,0:T(8,128)} %bitcast.10, bf16[2048,256]{1,0:T(8,128)(2,1)S(1)} %bitcast.8, ...), custom_call_target="tpu_custom_call" | custom-call | flops 5368709120 | bytes 4194304 | tf_op jit(solution)/shard_map/pallas_call | solution.py:131
  68.5 17.9 %all-to-all-start.1 = ((bf16[16,128,256]{2,1,0:T(8,128)(2,1)}), bf16[16,128,256]{2,1,0:T(8,128)(2,1)S(1)}, u32[]{:S(2)}, u32[]{:S(2)}) async-start(bf16[16,128,256]{2,1,0:T(8,128)(2,1)} %get-tuple-element.49), calls=%async_computation.1 | async-start | bytes 2097152 | tf_op jit(solution)/shard_map/all_to_all | solution.py:460
  86.5 1.6 %collective-permute-start.13 = (bf16[128,512]{1,0:T(8,128)(2,1)S(1)}, bf16[128,512]{1,0:T(8,128)(2,1)S(1)}, u32[]{:S(2)}, u32[]{:S(2)}) collective-permute-start(bf16[128,512]{1,0:T(8,128)(2,1)S(1)} %get-tuple-element.52), channel_id=1, source_target_pairs={{0,16},{8,24},{16,0},{24,8},{1,17},{9,25},{17,1},{25,9},{2,18},{10... | collective-permute-start | bytes 393224 | tf_op jit(solution)/shard_map/ppermute | solution.py:461
  88.1 2.2 %collective-permute-done.12.dq1 = bf16[128,512]{1,0:T(8,128)(2,1)S(1)} collective-permute-done((bf16[128,512]{1,0:T(8,128)(2,1)S(1)}, bf16[128,512]{1,0:T(8,128)(2,1)S(1)}, u32[]{:S(2)}, u32[]{:S(2)}) %collective-permute-start.12) | collective-permute-done | bytes 131104 | tf_op jit(solution)/shard_map/ppermute | solution.py:461
  90.3 1.6 %collective-permute-done.13.dq2 = bf16[128,512]{1,0:T(8,128)(2,1)S(1)} collective-permute-done((bf16[128,512]{1,0:T(8,128)(2,1)S(1)}, bf16[128,512]{1,0:T(8,128)(2,1)S(1)}, u32[]{:S(2)}, u32[]{:S(2)}) %collective-permute-start.13) | collective-permute-done | bytes 131104 | tf_op jit(solution)/shard_map/ppermute | solution.py:461
  91.9 1.4 %collective-permute-done.14.dq3 = bf16[128,512]{1,0:T(8,128)(2,1)S(1)} collective-permute-done((bf16[128,512]{1,0:T(8,128)(2,1)S(1)}, bf16[128,512]{1,0:T(8,128)(2,1)S(1)}, u32[]{:S(2)}, u32[]{:S(2)}) %collective-permute-start.14) | collective-permute-done | bytes 131104 | tf_op jit(solution)/shard_map/ppermute | solution.py:461
  93.3 4.4 %shard_map.99 = (bf16[128,1024]{1,0:T(8,128)(2,1)S(1)}, bf16[128,1024]{1,0:T(8,128)(2,1)S(1)}, bf16[128,1024]{1,0:T(8,128)(2,1)}, bf16[128,1024]{1,0:T(8,128)(2,...) custom-call(s32[5]{0:T(128)S(1)} %stack.23.place, bf16[128,512]{1,0:T(8,128)(2,1)S(1)} %get-tuple-element.50.dq0, ...), custom_call_target="tpu_custom_call" | custom-call | flops 536870912 | bytes 8388608 | tf_op jit(solution)/shard_map/pallas_call | solution.py:131
  97.7 0.7 copy-done.1
  98.4 4.7 %collective-permute-start.15 = (bf16[128,1024]{1,0:T(8,128)(2,1)S(1)}, bf16[128,1024]{1,0:T(8,128)(2,1)S(1)}, u32[]{:S(2)}, u32[]{:S(2)}) collective-permute-start(bf16[128,1024]{1,0:T(8,128)(2,1)S(1)} %get-tuple-element.57), channel_id=1, source_target_pairs={{0,1},{1,0},{2,3},{3,2},{4,5},{5,4},{6,7},{7,6},{8,9},{9,8},{10,11... | collective-permute-start | bytes 786440 | tf_op jit(solution)/shard_map/ppermute | solution.py:398
  103.2 1.5 %collective-permute-done.15 = bf16[128,1024]{1,0:T(8,128)(2,1)S(1)} collective-permute-done((bf16[128,1024]{1,0:T(8,128)(2,1)S(1)}, bf16[128,1024]{1,0:T(8,128)(2,1)S(1)}, u32[]{:S(2)}, u32[]{:S(2)}) %collective-permute-start.15) | collective-permute-done | bytes 262176 | tf_op jit(solution)/shard_map/ppermute | solution.py:398
  104.7 7.3 %all-to-all-done.1.parts = bf16[16,128,256]{2,1,0:T(8,128)(2,1)S(1)} async-done(((bf16[16,128,256]{2,1,0:T(8,128)(2,1)}), bf16[16,128,256]{2,1,0:T(8,128)(2,1)S(1)}, u32[]{:S(2)}, u32[]{:S(2)}) %all-to-all-start.1) | async-done | bytes 1048608 | tf_op jit(solution)/shard_map/all_to_all | solution.py:460
  112.0 1.4 %shard_map.100 = (bf16[128,1024]{1,0:T(8,128)(2,1)S(1)}, f32[128,1024]{1,0:T(8,128)S(1)}, bf16[128,128]{1,0:T(8,128)(2,1)}, bf16[128,128]{1,0:T(8,128)(2,1)}, bf16[128,256]{1,0:T(8,128)(2,1)S(1)}) custom-call(s32[5]{0:T(128)S(1)} %stack.23.place, bf16[16,128,256]{2,1,0:T(8,128)(2,1)S(1)} %all-to-all-done.1.parts, ...), custom_call_target="tpu_custom_call" | custom-call | flops 134217728 | bytes 2097152 | tf_op jit(solution)/shard_map/pallas_call | solution.py:131
  113.4 5.1 %collective-permute-start.16 = (bf16[128,1024]{1,0:T(8,128)(2,1)S(1)}, bf16[128,1024]{1,0:T(8,128)(2,1)S(1)}, u32[]{:S(2)}, u32[]{:S(2)}) collective-permute-start(bf16[128,1024]{1,0:T(8,128)(2,1)S(1)} %get-tuple-element.59), channel_id=1, source_target_pairs={{0,1},{1,0},{2,3},{3,2},{4,5},{5,4},{6,7},{7,6},{8,9},{9,8},{10,11... | collective-permute-start | bytes 786440 | tf_op jit(solution)/shard_map/ppermute | solution.py:398
  118.5 1.1 add_convert_fusion.1.queries
  119.7 1.0 shard_map.101
  120.7 0.5 collective-permute-start.18
  121.2 0.3 collective-permute-start.19
  121.5 0.9 collective-permute-done.18
  122.3 6.6 %collective-permute-done.19 = bf16[128,1024]{1,0:T(8,128)(2,1)S(1)} collective-permute-done((bf16[128,1024]{1,0:T(8,128)(2,1)S(1)}, bf16[128,1024]{1,0:T(8,128)(2,1)S(1)}, u32[]{:S(2)}, u32[]{:S(2)}) %collective-permute-start.19) | collective-permute-done | bytes 262176 | tf_op jit(solution)/shard_map/ppermute | solution.py:401
  129.0 0.8 add_convert_fusion
  (23 shorter events, 0.4 us)
Async XLA Ops:
  0.6 4.7 %collective-permute-start.1 = (bf16[128,1024]{1,0:T(8,128)(2,1)}, bf16[128,1024]{1,0:T(8,128)(2,1)S(1)}, u32[]{:S(2)}, u32[]{:S(2)}) collective-permute-start(bf16[128,1024]{1,0:T(8,128)(2,1)} %x0.1), channel_id=1, source_target_pairs={{0,1},{1,0},{2,3},{3,2},{4,5},{5,4},{6,7},{7,6},{8,9},{9,8},{10,11... | collective-permute-start | bytes 786440 | tf_op jit(solution)/shard_map/ppermute | solution.py:398
  4.0 1.7 %collective-permute-start.2 = (bf16[128,1024]{1,0:T(8,128)(2,1)}, bf16[128,1024]{1,0:T(8,128)(2,1)S(1)}, u32[]{:S(2)}, u32[]{:S(2)}) collective-permute-start(bf16[128,1024]{1,0:T(8,128)(2,1)} %g0.1), channel_id=1, source_target_pairs={{0,1},{1,0},{2,3},{3,2},{4,5},{5,4},{6,7},{7,6},{8,9},{9,8},{10,11... | collective-permute-start | bytes 786440 | tf_op jit(solution)/shard_map/ppermute | solution.py:398
  4.1 7.7 %collective-permute-start = (bf16[128,1024]{1,0:T(8,128)(2,1)}, bf16[128,1024]{1,0:T(8,128)(2,1)S(1)}, u32[]{:S(2)}, u32[]{:S(2)}) collective-permute-start(bf16[128,1024]{1,0:T(8,128)(2,1)} %x0.1), channel_id=1, source_target_pairs={{0,2},{2,0},{1,3},{3,1},{4,6},{6,4},{5,7},{7,5},{8,10},{10,8},{9,1... | collective-permute-start | bytes 786440 | tf_op jit(solution)/shard_map/ppermute | solution.py:401
  5.7 0.9 copy-start
  11.8 5.2 %copy-start.3 = (f32[128,512]{1,0:T(8,128)}, f32[128,512]{1,0:T(8,128)S(1)}, u32[]{:S(2)}) copy-start(f32[128,512]{1,0:T(8,128)S(1)} %get-tuple-element.47.g_half) | copy-start | bytes 786436
  11.8 2.4 %collective-permute-start.3 = (bf16[128,1024]{1,0:T(8,128)(2,1)S(1)}, bf16[128,1024]{1,0:T(8,128)(2,1)S(1)}, u32[]{:S(2)}, u32[]{:S(2)}) collective-permute-start(bf16[128,1024]{1,0:T(8,128)(2,1)S(1)} %collective-permute-done.x2), channel_id=1, source_target_pairs={{0,1},{1,0},{2,3},{3,2},{4,5},{5,4},{6,7},{7,6},{8,9},{9,8},{10,11... | collective-permute-start | bytes 786440 | tf_op jit(solution)/shard_map/ppermute | solution.py:398
  13.0 13.0 %collective-permute-start.4 = (bf16[128,1024]{1,0:T(8,128)(2,1)}, bf16[128,1024]{1,0:T(8,128)(2,1)S(1)}, u32[]{:S(2)}, u32[]{:S(2)}) collective-permute-start(bf16[128,1024]{1,0:T(8,128)(2,1)} %g0.1), channel_id=1, source_target_pairs={{0,2},{2,0},{1,3},{3,1},{4,6},{6,4},{5,7},{7,5},{8,10},{10,8},{9,1... | collective-permute-start | bytes 786440 | tf_op jit(solution)/shard_map/ppermute | solution.py:401
  16.3 0.7 copy-start.6
  17.0 36.2 %all-to-all-start = ((bf16[16,128,256]{2,1,0:T(8,128)(2,1)}), bf16[16,128,256]{2,1,0:T(8,128)(2,1)S(1)}, u32[]{:S(2)}, u32[]{:S(2)}) async-start(bf16[16,128,256]{2,1,0:T(8,128)(2,1)} %get-tuple-element.43), calls=%async_computation | async-start | bytes 2097152 | tf_op jit(solution)/shard_map/all_to_all | solution.py:453
  26.0 1.9 %collective-permute-start.5 = (bf16[128,1024]{1,0:T(8,128)(2,1)S(1)}, bf16[128,1024]{1,0:T(8,128)(2,1)S(1)}, u32[]{:S(2)}, u32[]{:S(2)}) collective-permute-start(bf16[128,1024]{1,0:T(8,128)(2,1)S(1)} %collective-permute-done.4.g2), channel_id=1, source_target_pairs={{0,1},{1,0},{2,3},{3,2},{4,5},{5,4},{6,7},{7,6},{8,9},{9,8},{10,11... | collective-permute-start | bytes 786440 | tf_op jit(solution)/shard_map/ppermute | solution.py:398
  26.7 0.7 copy-start.4
  27.9 0.9 copy-start.5
  31.0 22.1 %copy-start.2 = (bf16[128,1024]{1,0:T(8,128)(2,1)}, bf16[128,1024]{1,0:T(8,128)(2,1)S(1)}, u32[]{:S(2)}) copy-start(bf16[128,1024]{1,0:T(8,128)(2,1)S(1)} %shard_map.96.qd0) | copy-start | bytes 786436
  31.0 8.9 %collective-permute-start.6 = (bf16[128,1024]{1,0:T(8,128)(2,1)S(1)}, bf16[128,1024]{1,0:T(8,128)(2,1)S(1)}, u32[]{:S(2)}, u32[]{:S(2)}) collective-permute-start(bf16[128,1024]{1,0:T(8,128)(2,1)S(1)} %shard_map.96.qd0), channel_id=1, source_target_pairs={{0,8},{8,16},{16,24},{24,0},{1,9},{9,17},{17,25},{25,1},{2,10},{10... | collective-permute-start | bytes 786440 | tf_op jit(solution)/shard_map/ppermute | solution.py:454
  32.4 14.3 %collective-permute-start.7 = (bf16[128,1024]{1,0:T(8,128)(2,1)S(1)}, bf16[128,1024]{1,0:T(8,128)(2,1)S(1)}, u32[]{:S(2)}, u32[]{:S(2)}) collective-permute-start(bf16[128,1024]{1,0:T(8,128)(2,1)S(1)} %shard_map.96.qd0), channel_id=1, source_target_pairs={{0,16},{8,24},{16,0},{24,8},{1,17},{9,25},{17,1},{25,9},{2,18},{10... | collective-permute-start | bytes 786440 | tf_op jit(solution)/shard_map/ppermute | solution.py:454
  35.0 11.7 %collective-permute-start.8 = (bf16[128,1024]{1,0:T(8,128)(2,1)S(1)}, bf16[128,1024]{1,0:T(8,128)(2,1)S(1)}, u32[]{:S(2)}, u32[]{:S(2)}) collective-permute-start(bf16[128,1024]{1,0:T(8,128)(2,1)S(1)} %shard_map.96.qd0), channel_id=1, source_target_pairs={{0,24},{8,0},{16,8},{24,16},{1,25},{9,1},{17,9},{25,17},{2,26},{10... | collective-permute-start | bytes 786440 | tf_op jit(solution)/shard_map/ppermute | solution.py:454
  55.9 4.7 %collective-permute-start.10 = (f32[4,2048]{1,0:T(4,128)S(1)}, f32[4,2048]{1,0:T(4,128)S(1)}, u32[]{:S(2)}, u32[]{:S(2)}) collective-permute-start(f32[4,2048]{1,0:T(4,128)S(1)} %shard_map.97.st0), channel_id=1, source_target_pairs={{0,16},{8,24},{16,0},{24,8},{1,17},{9,25},{17,1},{25,9},{2,18},{10... | collective-permute-start | bytes 98312 | tf_op jit(solution)/shard_map/ppermute | solution.py:457
  59.0 2.8 %collective-permute-start.11 = (f32[4,2048]{1,0:T(4,128)S(1)}, f32[4,2048]{1,0:T(4,128)S(1)}, u32[]{:S(2)}, u32[]{:S(2)}) collective-permute-start(f32[4,2048]{1,0:T(4,128)S(1)} %shard_map.97.st0), channel_id=1, source_target_pairs={{0,24},{8,0},{16,8},{24,16},{1,25},{9,1},{17,9},{25,17},{2,26},{10... | collective-permute-start | bytes 98312 | tf_op jit(solution)/shard_map/ppermute | solution.py:457
  59.8 4.0 %collective-permute-start.9 = (f32[4,2048]{1,0:T(4,128)S(1)}, f32[4,2048]{1,0:T(4,128)S(1)}, u32[]{:S(2)}, u32[]{:S(2)}) collective-permute-start(f32[4,2048]{1,0:T(4,128)S(1)} %shard_map.97.st0), channel_id=1, source_target_pairs={{0,8},{8,16},{16,24},{24,0},{1,9},{9,17},{17,25},{25,1},{2,10},{10... | collective-permute-start | bytes 98312 | tf_op jit(solution)/shard_map/ppermute | solution.py:457
  68.5 43.5 %all-to-all-start.1 = ((bf16[16,128,256]{2,1,0:T(8,128)(2,1)}), bf16[16,128,256]{2,1,0:T(8,128)(2,1)S(1)}, u32[]{:S(2)}, u32[]{:S(2)}) async-start(bf16[16,128,256]{2,1,0:T(8,128)(2,1)} %get-tuple-element.49), calls=%async_computation.1 | async-start | bytes 2097152 | tf_op jit(solution)/shard_map/all_to_all | solution.py:460
  86.4 3.9 %collective-permute-start.12 = (bf16[128,512]{1,0:T(8,128)(2,1)S(1)}, bf16[128,512]{1,0:T(8,128)(2,1)S(1)}, u32[]{:S(2)}, u32[]{:S(2)}) collective-permute-start(bf16[128,512]{1,0:T(8,128)(2,1)S(1)} %get-tuple-element.51), channel_id=1, source_target_pairs={{0,24},{8,0},{16,8},{24,16},{1,25},{9,1},{17,9},{25,17},{2,26},{10... | collective-permute-start | bytes 393224 | tf_op jit(solution)/shard_map/ppermute | solution.py:461
  86.5 5.4 %collective-permute-start.13 = (bf16[128,512]{1,0:T(8,128)(2,1)S(1)}, bf16[128,512]{1,0:T(8,128)(2,1)S(1)}, u32[]{:S(2)}, u32[]{:S(2)}) collective-permute-start(bf16[128,512]{1,0:T(8,128)(2,1)S(1)} %get-tuple-element.52), channel_id=1, source_target_pairs={{0,16},{8,24},{16,0},{24,8},{1,17},{9,25},{17,1},{25,9},{2,18},{10... | collective-permute-start | bytes 393224 | tf_op jit(solution)/shard_map/ppermute | solution.py:461
  88.0 5.2 %collective-permute-start.14 = (bf16[128,512]{1,0:T(8,128)(2,1)S(1)}, bf16[128,512]{1,0:T(8,128)(2,1)S(1)}, u32[]{:S(2)}, u32[]{:S(2)}) collective-permute-start(bf16[128,512]{1,0:T(8,128)(2,1)S(1)} %get-tuple-element.53), channel_id=1, source_target_pairs={{0,8},{8,16},{16,24},{24,0},{1,9},{9,17},{17,25},{25,1},{2,10},{10... | collective-permute-start | bytes 393224 | tf_op jit(solution)/shard_map/ppermute | solution.py:461
  97.7 0.7 copy-start.1
  98.4 6.2 %collective-permute-start.15 = (bf16[128,1024]{1,0:T(8,128)(2,1)S(1)}, bf16[128,1024]{1,0:T(8,128)(2,1)S(1)}, u32[]{:S(2)}, u32[]{:S(2)}) collective-permute-start(bf16[128,1024]{1,0:T(8,128)(2,1)S(1)} %get-tuple-element.57), channel_id=1, source_target_pairs={{0,1},{1,0},{2,3},{3,2},{4,5},{5,4},{6,7},{7,6},{8,9},{9,8},{10,11... | collective-permute-start | bytes 786440 | tf_op jit(solution)/shard_map/ppermute | solution.py:398
  103.2 15.3 %collective-permute-start.17 = (bf16[128,1024]{1,0:T(8,128)(2,1)}, bf16[128,1024]{1,0:T(8,128)(2,1)}, u32[]{:S(2)}, u32[]{:S(2)}) collective-permute-start(bf16[128,1024]{1,0:T(8,128)(2,1)} %get-tuple-element.63), channel_id=1, source_target_pairs={{0,1},{1,0},{2,3},{3,2},{4,5},{5,4},{6,7},{7,6},{8,9},{9,8},{10,11... | collective-permute-start | bytes 786440 | tf_op jit(solution)/shard_map/ppermute | solution.py:398
  113.4 6.3 %collective-permute-start.16 = (bf16[128,1024]{1,0:T(8,128)(2,1)S(1)}, bf16[128,1024]{1,0:T(8,128)(2,1)S(1)}, u32[]{:S(2)}, u32[]{:S(2)}) collective-permute-start(bf16[128,1024]{1,0:T(8,128)(2,1)S(1)} %get-tuple-element.59), channel_id=1, source_target_pairs={{0,1},{1,0},{2,3},{3,2},{4,5},{5,4},{6,7},{7,6},{8,9},{9,8},{10,11... | collective-permute-start | bytes 786440 | tf_op jit(solution)/shard_map/ppermute | solution.py:398
  120.7 1.6 %collective-permute-start.18 = (bf16[128,1024]{1,0:T(8,128)(2,1)S(1)}, bf16[128,1024]{1,0:T(8,128)(2,1)S(1)}, u32[]{:S(2)}, u32[]{:S(2)}) collective-permute-start(bf16[128,1024]{1,0:T(8,128)(2,1)S(1)} %get-tuple-element.65), channel_id=1, source_target_pairs={{0,1},{1,0},{2,3},{3,2},{4,5},{5,4},{6,7},{7,6},{8,9},{9,8},{10,11... | collective-permute-start | bytes 786440 | tf_op jit(solution)/shard_map/ppermute | solution.py:398
  121.2 7.8 %collective-permute-start.19 = (bf16[128,1024]{1,0:T(8,128)(2,1)S(1)}, bf16[128,1024]{1,0:T(8,128)(2,1)S(1)}, u32[]{:S(2)}, u32[]{:S(2)}) collective-permute-start(bf16[128,1024]{1,0:T(8,128)(2,1)S(1)} %add_convert_fusion.2), channel_id=1, source_target_pairs={{0,2},{2,0},{1,3},{3,1},{4,6},{6,4},{5,7},{7,5},{8,10},{10,8},{9,1... | collective-permute-start | bytes 786440 | tf_op jit(solution)/shard_map/ppermute | solution.py:401

commit v3 on v2

--- a/solution.py
+++ b/solution.py
@@ -13,13 +13,12 @@
 LOG2E = 1.4426950408889634
 SCALE2 = FACTOR * LOG2E
 NEG_FILL = -1e30
+LOWEST_TOP = -1e29
 BLOCK = 128
 HEADS = 4
 ROWS = HEADS * BLOCK
 CHUNK = 2 * BLOCK
 FAR_FLOPS = 15_000_000_000
-PARTS = 4
-PART = 2048 // PARTS
 STEP = 512
 VMEM_LIMIT = 20 * 1024 * 1024
 BF16 = jnp.bfloat16
@@ -148,107 +147,99 @@
     )
 
 
-def visible_tile(times, key_block, query_block):
-    key_row = jnp.broadcast_to(times[pl.ds(key_block, 1), :], (BLOCK, BLOCK))
-    seen = key_row.T <= times[pl.ds(query_block, 1), :]
-    return jnp.concatenate([seen] * HEADS, axis=1)
-
-
-def for_tiles(place, times, tile):
-    z, y, xh = place[0], place[1], place[2]
-
-    def past(first, keys):
-        for part in range(PARTS):
-            tile(pl.multiple_of(first, CHUNK), keys, part * PART, PART, None)
-
-    def some(i, carry):
-        past(i * STEP, STEP)
-        return carry
-
-    lax.fori_loop(0, z * CHUNK // STEP, some, 0)
-    if STEP > CHUNK:
-
-        @pl.when(z % 2 == 1)
-        def _():
-            past((z - 1) * CHUNK, CHUNK)
-
-    for s in range(4):
-        query_block = 8 * z + 2 * ((y - s + 4) % 4) + xh
-        mask = jnp.concatenate(
-            [visible_tile(times, 8 * z + 2 * y + h, query_block) for h in range(2)], axis=0
-        )
-        tile(pl.multiple_of(z * CHUNK, CHUNK), CHUNK, s * ROWS, ROWS, mask)
-
-    @pl.when((z < 7) & (y == 0) & (xh == 1))
-    def _():
-        mask = visible_tile(times, 8 * (z + 1), 8 * z + 7)
-        tile(pl.multiple_of((z + 1) * CHUNK, CHUNK), BLOCK, ROWS, ROWS, mask)
-
-
-def fetch(times, own, times_buf, own_buf, sems):
+def visible(times, key_block, query_block):
+    keys = jnp.broadcast_to(times[pl.ds(key_block, 1), :], (BLOCK, BLOCK)).T
+    return jnp.where(keys <= times[pl.ds(query_block, 1), :], 0.0, NEG_FILL)
+
+
+def stack_kernel(place, times_hbm, qd0, qd1, qd2, qd3, q_rows, g_rows, bias, times, own, sems):
     copies = [
-        pltpu.make_async_copy(own, own_buf, sems.at[0]),
-        pltpu.make_async_copy(times, times_buf, sems.at[1]),
+        pltpu.make_async_copy(qd0, own, sems.at[0]),
+        pltpu.make_async_copy(times_hbm, times, sems.at[1]),
     ]
     for copy in copies:
         copy.start()
-    return copies
-
-
-FETCHED = [
-    pltpu.VMEM((64, BLOCK), jnp.int32),
-    pltpu.VMEM((BLOCK, 1024), BF16),
-    pltpu.SemaphoreType.DMA((2,)),
-]
-
-
-def stack_blocks(blocks, copies, q_rows, g_rows):
-    for s in (1, 2, 3, 0):
+    for s, qd in ((1, qd1), (2, qd2), (3, qd3), (0, own)):
         if s == 0:
-            for copy in copies:
-                copy.wait()
-        q_rows[s * ROWS : (s + 1) * ROWS, :] = stack_heads(blocks[s], 0)
-        g_rows[s * ROWS : (s + 1) * ROWS, :] = stack_heads(blocks[s], 512)
-
-
-def stats_kernel(
-    place, times_hbm, kv, qd0, qd1, qd2, qd3, out, times, own, sems, q_rows, g_rows
-):
-    copies = fetch(times_hbm, qd0, times, own, sems)
-    stack_blocks((own, qd1, qd2, qd3), copies, q_rows, g_rows)
-    out[0:1, :] = jnp.full((1, 4 * ROWS), NEG_FILL, F32)
-    out[1:4, :] = jnp.zeros((3, 4 * ROWS), F32)
-
-    def tile(first, count, row, rows, seen):
+            copies[0].wait()
+        q_rows[s * ROWS : (s + 1) * ROWS, :] = stack_heads(qd, 0)
+        g_rows[s * ROWS : (s + 1) * ROWS, :] = stack_heads(qd, 512)
+    copies[1].wait()
+    z, y, xh = place[0], place[1], place[2]
+    for s in range(4):
+        cols = slice(s * BLOCK, (s + 1) * BLOCK)
+        query_block = 8 * z + 2 * ((y - s + 4) % 4) + xh
+        for h in range(2):
+            key_block = 8 * z + 2 * y + h
+            bias[h * BLOCK : (h + 1) * BLOCK, cols] = visible(times, key_block, query_block)
+    bias[2 * BLOCK :, :BLOCK] = visible(times, 8 * jnp.minimum(z + 1, 7), 8 * z + 7)
+    bias[2 * BLOCK :, BLOCK:] = jnp.full((BLOCK, 3 * BLOCK), NEG_FILL, F32)
+
+
+def for_tiles(place, bias, tile, done):
+    z, y, xh = place[0], place[1], place[2]
+
+    def masked(part, s):
+        return jnp.concatenate([bias[part, s * BLOCK : (s + 1) * BLOCK]] * HEADS, axis=1)
+
+    for s in range(4):
+        first = pl.multiple_of(z * CHUNK, CHUNK)
+        tile(first, CHUNK, s * ROWS, ROWS, masked(slice(0, CHUNK), s))
+
+    def past(first, keys):
+        tile(pl.multiple_of(first, CHUNK), keys, 0, 4 * ROWS, None)
+
+    def some(i, carry):
+        past(i * STEP, STEP)
+        done(i)
+        return carry
+
+    lax.fori_loop(0, z // 2, some, 0)
+
+    @pl.when(z % 2 == 1)
+    def _():
+        past((z - 1) * CHUNK, CHUNK)
+
+    @pl.when((z < 7) & (y == 0) & (xh == 1))
+    def _():
+        first = pl.multiple_of((z + 1) * CHUNK, CHUNK)
+        tile(first, BLOCK, ROWS, ROWS, masked(slice(CHUNK, CHUNK + BLOCK), 0))
+
+
+def stats_kernel(place, kv, q_rows, g_rows, bias, out):
+    def tile(first, count, row, rows, hidden):
         cols = slice(row, row + rows)
         keys = kv[pl.ds(first, count), :HEAD]
         values = kv[pl.ds(first, count), HEAD:]
         scores = contract_last(keys, q_rows[cols, :]) * SCALE2
-        if seen is not None:
-            scores = jnp.where(seen, scores, NEG_FILL)
-        old = out[0:1, cols]
-        top = jnp.maximum(old, jnp.max(scores, axis=0, keepdims=True))
+        first_visit = hidden is not None and count == CHUNK
+        if hidden is not None:
+            scores = scores + hidden
+        top = jnp.maximum(jnp.max(scores, axis=0, keepdims=True), LOWEST_TOP)
+        if not first_visit:
+            old = out[0:1, cols]
+            top = jnp.maximum(old, top)
         prob = jnp.exp2(scores - top)
-        if seen is not None:
-            prob = jnp.where(seen, prob, 0.0)
         prob_grad = contract_last(values, g_rows[cols, :])
-        shrink = jnp.exp2(old - top)
+        norm = jnp.sum(prob, axis=0, keepdims=True)
+        dot = jnp.sum(prob * prob_grad, axis=0, keepdims=True)
+        if not first_visit:
+            shrink = jnp.exp2(old - top)
+            norm += out[1:2, cols] * shrink
+            dot += out[2:3, cols] * shrink
         out[0:1, cols] = top
-        out[1:2, cols] = out[1:2, cols] * shrink + jnp.sum(prob, axis=0, keepdims=True)
-        out[2:3, cols] = out[2:3, cols] * shrink + jnp.sum(
-            prob * prob_grad, axis=0, keepdims=True
-        )
-
-    for_tiles(place, times, tile)
-
-
-def stats(place, times, kv, blocks):
+        out[1:2, cols] = norm
+        out[2:3, cols] = dot
+
+    out[3:4, :] = jnp.zeros((1, 4 * ROWS), F32)
+    for_tiles(place, bias, tile, lambda i: None)
+
+
+def stats(place, kv, rows):
     (out,) = whole_call(
         stats_kernel,
-        (place, times, kv, *blocks),
+        (place, kv, *rows),
         [jax.ShapeDtypeStruct((4, 4 * ROWS), F32)],
-        FETCHED + [pltpu.VMEM((4 * ROWS, HEAD), BF16)] * 2,
-        hbm=(1, 3),
         flops=4 * 2048 * 2048 * 128,
         traffic=2 << 20,
         exps=2048 * 2048,
@@ -257,13 +248,17 @@
 
 
 def grads_kernel(
-    place, times_hbm, kv, qd0, qd1, qd2, qd3, st0, st1, st2, st3,
+    place, kv, q_rows, g_rows, bias, st0, st1, st2, st3,
     dkv, dq0, dq1, dq2, dq3,
-    times, own, sems, sums, q_rows, g_rows, q_sum, row_stats, dkv_buf, dq_buf, out_sems,
+    sums, q_sum, row_stats, dkv_buf, dq_buf, out_sems,
 ):
-    copies = fetch(times_hbm, qd0, times, own, sems)
-    sums[...] = jnp.zeros_like(sums)
-    q_sum[...] = jnp.zeros_like(q_sum)
+    z = place[0]
+
+    def clear(i, carry):
+        dkv_buf[i] = jnp.zeros((BLOCK, 2 * HEAD), BF16)
+        return carry
+
+    lax.fori_loop(2 * z + 2, 16, clear, 0)
     for s in range(4):
         cols = slice(s * ROWS, (s + 1) * ROWS)
         tops, norms, dots = [], [], []
@@ -277,62 +272,78 @@
         norm = sum(n * f for n, f in zip(norms, scales))
         row_stats[0:1, cols] = top + jnp.log2(norm)
         row_stats[1:2, cols] = sum(d * f for d, f in zip(dots, scales)) / norm
-    stack_blocks((own, qd1, qd2, qd3), copies, q_rows, g_rows)
-
-    def tile(first, count, row, rows, seen):
+
+    def tile(first, count, row, rows, hidden):
         cols = slice(row, row + rows)
         keys = kv[pl.ds(first, count), :HEAD]
         values = kv[pl.ds(first, count), HEAD:]
         q, g = q_rows[cols, :], g_rows[cols, :]
-        prob = jnp.exp2(contract_last(keys, q) * SCALE2 - row_stats[0:1, cols])
-        if seen is not None:
-            prob = jnp.where(seen, prob, 0.0)
+        scores = contract_last(keys, q) * SCALE2
+        if hidden is not None:
+            scores = scores + hidden
+        prob = jnp.exp2(scores - row_stats[0:1, cols])
         prob_grad = contract_last(values, g)
         score_grad = (prob * (prob_grad - row_stats[1:2, cols])).astype(BF16)
-        sums[pl.ds(first, count), :HEAD] += matmul(score_grad, q)
-        sums[pl.ds(first, count), HEAD:] += matmul(prob.astype(BF16), g)
-        q_sum[:, cols] += lax.dot_general(
+        dk = matmul(score_grad, q)
+        dv = matmul(prob.astype(BF16), g)
+        dq = lax.dot_general(
             keys, score_grad, (((0,), (0,)), ((), ())), preferred_element_type=F32
         )
-
-    for_tiles(place, times, tile)
+        block = first // BLOCK
+        if hidden is not None and count == CHUNK:
+            q_sum[:, cols] = dq
+            if row:
+                dk += sums[:, :HEAD]
+                dv += sums[:, HEAD:]
+            sums[:, :HEAD] = dk
+            sums[:, HEAD:] = dv
+            if row < 3 * ROWS:
+                return
+        else:
+            q_sum[:, cols] += dq
+        for i in range(count // BLOCK):
+            part = slice(i * BLOCK, (i + 1) * BLOCK)
+            dkv_buf[block + i, :, :HEAD] = dk[part, :].astype(BF16)
+            dkv_buf[block + i, :, HEAD:] = dv[part, :].astype(BF16)
+
+    def send(i):
+        part = pl.ds(4 * i, 4)
+        return pltpu.make_async_copy(dkv_buf.at[part], dkv.at[part], out_sems.at[i])
+
+    for_tiles(place, bias, tile, lambda i: send(i).start())
+    for i in range(4):
+
+        @pl.when(i >= z // 2)
+        def _():
+            send(i).start()
+
     outs = []
-    for i in range(16):
-        dkv_buf[i] = sums[i * BLOCK : (i + 1) * BLOCK, :].astype(BF16)
-        if i % 4 == 3:
-            part = pl.ds(i - 3, 4)
-            outs.append(
-                pltpu.make_async_copy(dkv_buf.at[part], dkv.at[part], out_sems.at[i // 4])
-            )
-            outs[-1].start()
     for s, dq in enumerate((dq0, dq1, dq2, dq3)):
         for h in range(HEADS):
             part = q_sum[:, s * ROWS + h * HEAD : s * ROWS + (h + 1) * HEAD]
             dq_buf[s, :, h * HEAD : (h + 1) * HEAD] = (part.T * FACTOR).astype(BF16)
         outs.append(pltpu.make_async_copy(dq_buf.at[s], dq, out_sems.at[4 + s]))
         outs[-1].start()
+    for i in range(4):
+        send(i).wait()
     for copy in outs:
         copy.wait()
 
 
-def grads(place, times, kv, blocks, gathered):
+def grads(place, kv, rows, gathered):
     return whole_call(
         grads_kernel,
-        (place, times, kv, *blocks, *gathered),
+        (place, kv, *rows, *gathered),
         [jax.ShapeDtypeStruct((16, BLOCK, 2 * HEAD), BF16)]
         + [jax.ShapeDtypeStruct((BLOCK, ROWS), BF16)] * 4,
-        FETCHED
-        + [
-            pltpu.VMEM((16 * BLOCK, 2 * HEAD), F32),
-            pltpu.VMEM((4 * ROWS, HEAD), BF16),
-            pltpu.VMEM((4 * ROWS, HEAD), BF16),
+        [
+            pltpu.VMEM((CHUNK, 2 * HEAD), F32),
             pltpu.VMEM((HEAD, 4 * ROWS), F32),
             pltpu.VMEM((8, 4 * ROWS), F32),
             pltpu.VMEM((16, BLOCK, 2 * HEAD), BF16),
             pltpu.VMEM((4, BLOCK, ROWS), BF16),
             pltpu.SemaphoreType.DMA((8,)),
         ],
-        hbm=(1, 3),
         hbm_outs=(0, 1, 2, 3, 4),
         flops=10 * 2048 * 2048 * 128,
         traffic=4 << 20,
@@ -382,10 +393,10 @@
     far1[...] = queries[...].astype(F32) + key_terms(place, 2, dk[...], dv[...], wk, wv)
 
 
-def key_near_kernel(place, dkv, wk, wv, queries, near1, near0):
+def key_near_kernel(place, dkv, wk, wv, near1, near0):
     dk, dv = dkv[:, :HEAD], dkv[:, HEAD:]
     near1[...] = key_terms(place, 1, dk, dv, wk, wv).astype(BF16)
-    near0[...] = queries[...].astype(F32) + key_terms(place, 0, dk, dv, wk, wv)
+    near0[...] = key_terms(place, 0, dk, dv, wk, wv)
 
 
 def local(inputs, out_grad, w_query, key_weight, value_weight, w_output, times):
@@ -453,9 +464,21 @@
     kv = lax.all_to_all(kv_own, ("z", "xh"), 0, 0, tiled=True).reshape(16 * BLOCK, 2 * HEAD)
     blocks = [qd_own] + [lax.ppermute(qd_own, "y", shifted(4, s)) for s in (1, 2, 3)]
 
-    own_stats = stats(place, times2d, kv, blocks)
+    rows = whole_call(
+        stack_kernel,
+        (place, times2d, *blocks),
+        [shape(4 * ROWS, HEAD)] * 2 + [shape(CHUNK + BLOCK, ROWS, kind=F32)],
+        [
+            pltpu.VMEM((64, BLOCK), jnp.int32),
+            pltpu.VMEM((BLOCK, 1024), BF16),
+            pltpu.SemaphoreType.DMA((2,)),
+        ],
+        hbm=(1, 2),
+        traffic=2 << 20,
+    )
+    own_stats = stats(place, kv, rows)
     gathered = [own_stats] + [lax.ppermute(own_stats, "y", shifted(4, s)) for s in (1, 2, 3)]
-    dkv, *dqs = grads(place, times2d, kv, blocks, gathered)
+    dkv, *dqs = grads(place, kv, rows, gathered)
 
     dkv_parts = lax.all_to_all(dkv, ("z", "xh"), 0, 0, tiled=True)
     dq_parts = [dqs[0]] + [lax.ppermute(dqs[s], "y", shifted(4, -s)) for s in (1, 2, 3)]
@@ -474,6 +497,9 @@
     )
     far_query = add(far1, to_core(far0)).astype(BF16)
     near_query = add(near0, to_core(near1)).astype(BF16)
+    dkv_parts, far_query, near_query = lax.optimization_barrier(
+        (dkv_parts, far_query, near_query)
+    )
 
     far0, far1, dk, dv, dkv_own = whole_call(
         key_far_kernel,
@@ -490,12 +516,13 @@
     from_far = to_xl(far_sum)
     near1, near0 = whole_call(
         key_near_kernel,
-        (place, dkv_own, held_k, held_v, near_query),
+        (place, dkv_own, held_k, held_v),
         [shape(BLOCK, 1024), shape(BLOCK, 1024, kind=F32)],
         flops=2 * 128 * 2048 * 256,
         traffic=2 << 20,
     )
-    input_grad = add(near0, to_core(near1), from_far).astype(BF16)
+    before = lax.optimization_barrier(add(from_far, near_query))
+    input_grad = add(before, near0, to_core(near1)).astype(BF16)
     return input_grad, dk, dv
 
 

time: 130 us -> 127 us (0.977)
  local copies, waits for them, and re-layouts: 4.05 us -> 2.35 us
    unnamed x14 -> x12, local copies, waits for them, and re-layouts: 3.97 us -> 2.26 us
    pallas_call x8 -> x9, Pallas kernels: 23.6 us -> 22.5 us  [whole_call(): pl.pallas_call(kernel, in_specs=in_specs, out_specs=[pl.BlockSpec(memory_...]
  transfers between devices with their start and end apart: 22 -> 22, of which waited for: 17 -> 16; matrix products, arithmetic and copies ran while one was open for 1% -> 1% of each run, Pallas kernels for 12% -> 13%
where the time goes in v3:
time: 127 us; the launch traced here: 126 us
  starting transfers between devices  54.5 us (43%)
  waiting for transfers between devices  44.2 us (35%)
  Pallas kernels  22.5 us (18%)
  local copies, waits for them, and re-layouts  2.35 us (2%)
  other arithmetic  1.78 us (1%)
    pallas_call x9, Pallas kernels, whole_call(): pl.pallas_call(kernel, in_specs=in_specs, out_specs=[pl.BlockSpec(memory_...  22.5 us
    all_to_all x1, starting transfers between devices, local(): dkv_parts = lax.all_to_all(dkv, ('z', 'xh'), 0, 0, tiled=True)  17.4 us
    ppermute x8, starting transfers between devices, to_core(): return lax.ppermute(value, 'core', swap)  16.4 us
    ppermute x3, waiting for transfers between devices, local(): lax.ppermute(qd_own, 'y', shifted(4, s))  10.6 us
    all_to_all x1, starting transfers between devices, local(): lax.all_to_all(kv_own, ('z', 'xh'), 0, 0, tiled=True)  9.02 us
    all_to_all x1, waiting for transfers between devices, local(): dkv_parts = lax.all_to_all(dkv, ('z', 'xh'), 0, 0, tiled=True)  8.13 us
    ppermute x8, waiting for transfers between devices, to_core(): return lax.ppermute(value, 'core', swap)  5.89 us
    all_to_all x1, waiting for transfers between devices, local(): lax.all_to_all(kv_own, ('z', 'xh'), 0, 0, tiled=True)  5.56 us
  transfers between devices with their start and end apart: 22, of which 16 were waited for; matrix products, arithmetic and copies ran while one was open for 1% of the time, Pallas kernels for 13%

profile of v3, /device:TPU:1, one launch (start us, length us, event | category | flops | bytes accessed | tf_op | source)
XLA Modules:
  0.0 126.2 jit_solution(10199927197644072401)
XLA Ops:
  0.6 3.3 %collective-permute-start.1 = (bf16[128,1024]{1,0:T(8,128)(2,1)}, bf16[128,1024]{1,0:T(8,128)(2,1)S(1)}, u32[]{:S(2)}, u32[]{:S(2)}) collective-permute-start(bf16[128,1024]{1,0:T(8,128)(2,1)} %x0.1), channel_id=1, source_target_pairs={{0,1},{1,0},{2,3},{3,2},{4,5},{5,4},{6,7},{7,6},{8,9},{9,8},{10,11... | collective-permute-start | bytes 786440 | tf_op jit(solution)/shard_map/ppermute | solution.py:409
  4.0 0.1 collective-permute-start.2
  4.1 1.2 collective-permute-done.1.x1
  5.3 0.4 collective-permute-done.2.g1
  5.7 0.9 copy-done
  6.7 5.1 %shard_map.94 = (f32[128,768]{1,0:T(8,128)S(1)}, f32[128,512]{1,0:T(8,128)S(1)}, bf16[2048,512]{1,0:T(8,128)(2,1)S(1)}, bf16[2048,128]{1,0:T(8,128)(2,1)S(1)}, b...) custom-call(s32[5]{0:T(128)S(1)} %stack.23.place, bf16[128,1024]{1,0:T(8,128)(2,1)S(1)} %copy-done, ...), custom_call_target="tpu_custom_call" | custom-call | flops 671088640 | bytes 10485760 | tf_op jit(solution)/shard_map/pallas_call | solution.py:130
  11.8 1.2 collective-permute-start.3
  13.0 1.2 collective-permute-done.3.x3
  14.2 2.1 %shard_map.95 = (bf16[16,128,256]{2,1,0:T(8,128)(2,1)}, bf16[128,512]{1,0:T(8,128)(2,1)S(1)}) custom-call(s32[5]{0:T(128)S(1)} %stack.23.place, bf16[128,1024]{1,0:T(8,128)(2,1)S(1)} %collective-permute-done.x2, bf16[128,1024]{1,0:T(8,128)(2,1)S(1)} %collective-permute-done.3.x3, bf16[2048,512]{1,0:T(8,128)(2,1)S(1)} %get-tuple-element.45.wq, ...), custom_call_target="tpu_custom_call" | custom-call | flops 402653184 | bytes 4194304 | tf_op jit(solution)/shard_map/pallas_call | solution.py:130
  16.3 0.6 copy-done.4
  17.0 9.0 %all-to-all-start = ((bf16[16,128,256]{2,1,0:T(8,128)(2,1)}), bf16[16,128,256]{2,1,0:T(8,128)(2,1)S(1)}, u32[]{:S(2)}, u32[]{:S(2)}) async-start(bf16[16,128,256]{2,1,0:T(8,128)(2,1)} %get-tuple-element.49), calls=%async_computation | async-start | bytes 2097152 | tf_op jit(solution)/shard_map/all_to_all | solution.py:464
  26.0 0.7 collective-permute-start.5
  26.7 1.2 collective-permute-done.5.g3
  27.9 2.2 %shard_map.96.qd0 = bf16[128,1024]{1,0:T(8,128)(2,1)S(1)} custom-call(s32[5]{0:T(128)S(1)} %stack.23.place, bf16[128,1024]{1,0:T(8,128)(2,1)S(1)} %collective-permute-done.4.g2, bf16[128,1024]{1,0:T(8,128)(2,1)S(1)} %collective-permute-done.5.g3, bf16[512,2048]{1,0:T(8,128)(2,1)S(1)} %get-tuple-element.52.wo, f32[128,512]{1,0:T(8,128)} %copy-done.2, ...), custom_call_target="tpu_custom_call" | custom-call | flops 15000000512 | bytes 3145728 | tf_op jit(solution)/shard_map/pallas_call | solution.py:130
  30.1 1.4 %collective-permute-start.6 = (bf16[128,1024]{1,0:T(8,128)(2,1)S(1)}, bf16[128,1024]{1,0:T(8,128)(2,1)S(1)}, u32[]{:S(2)}, u32[]{:S(2)}) collective-permute-start(bf16[128,1024]{1,0:T(8,128)(2,1)S(1)} %shard_map.96.qd0), channel_id=1, source_target_pairs={{0,8},{8,16},{16,24},{24,0},{1,9},{9,17},{17,25},{25,1},{2,10},{10... | collective-permute-start | bytes 786440 | tf_op jit(solution)/shard_map/ppermute | solution.py:465
  31.5 2.6 %collective-permute-start.7 = (bf16[128,1024]{1,0:T(8,128)(2,1)S(1)}, bf16[128,1024]{1,0:T(8,128)(2,1)S(1)}, u32[]{:S(2)}, u32[]{:S(2)}) collective-permute-start(bf16[128,1024]{1,0:T(8,128)(2,1)S(1)} %shard_map.96.qd0), channel_id=1, source_target_pairs={{0,16},{8,24},{16,0},{24,8},{1,17},{9,25},{17,1},{25,9},{2,18},{10... | collective-permute-start | bytes 786440 | tf_op jit(solution)/shard_map/ppermute | solution.py:465
  34.1 1.1 collective-permute-start.8
  35.2 3.9 %collective-permute-done.6.qd1 = bf16[128,1024]{1,0:T(8,128)(2,1)S(1)} collective-permute-done((bf16[128,1024]{1,0:T(8,128)(2,1)S(1)}, bf16[128,1024]{1,0:T(8,128)(2,1)S(1)}, u32[]{:S(2)}, u32[]{:S(2)}) %collective-permute-start.6) | collective-permute-done | bytes 262176 | tf_op jit(solution)/shard_map/ppermute | solution.py:465
  39.0 6.7 %collective-permute-done.7.qd2 = bf16[128,1024]{1,0:T(8,128)(2,1)S(1)} collective-permute-done((bf16[128,1024]{1,0:T(8,128)(2,1)S(1)}, bf16[128,1024]{1,0:T(8,128)(2,1)S(1)}, u32[]{:S(2)}, u32[]{:S(2)}) %collective-permute-start.7) | collective-permute-done | bytes 262176 | tf_op jit(solution)/shard_map/ppermute | solution.py:465
  45.8 1.8 %shard_map.97 = (bf16[2048,128]{1,0:T(8,128)(2,1)S(1)}, bf16[2048,128]{1,0:T(8,128)(2,1)S(1)}, f32[384,512]{1,0:T(8,128)S(1)}) custom-call(s32[5]{0:T(128)S(1)} %stack.23.place, s32[64,128]{1,0:T(8,128)} %bitcast.9, bf16[128,1024]{1,0:T(8,128)(2,1)} %copy-done.1, bf16[128,1024]{1,0:T(8,128)(2,1)S(1)} %collective-permute-done.6.qd1, ...), custom_call_target="tpu_custom_call" | custom-call | bytes 2097152 | tf_op jit(solution)/shard_map/pallas_call | solution.py:130
  47.6 5.6 %all-to-all-done = bf16[16,128,256]{2,1,0:T(8,128)(2,1)S(1)} async-done(((bf16[16,128,256]{2,1,0:T(8,128)(2,1)}), bf16[16,128,256]{2,1,0:T(8,128)(2,1)S(1)}, u32[]{:S(2)}, u32[]{:S(2)}) %all-to-all-start) | async-done | bytes 1048608 | tf_op jit(solution)/shard_map/all_to_all | solution.py:464
  53.1 1.4 %shard_map.98.st0 = f32[4,2048]{1,0:T(4,128)S(1)} custom-call(s32[5]{0:T(128)S(1)} %stack.23.place, bf16[2048,256]{1,0:T(8,128)(2,1)S(1)} %bitcast.7, bf16[2048,128]{1,0:T(8,128)(2,1)S(1)} %get-tuple-element.55.q_rows, bf16[2048,128]{1,0:T(8,128)(2,1)S(1)} %get-tuple-element.56.g_rows, f32[384,512]{1,0:T(8,128)S(1)} %get-tuple-element.57.bias), custom_call_target="tpu_custom_call" | custom-call | flops 2147483648 | bytes 2097152 | tf_op jit(solution)/shard_map/pallas_call | solution.py:130
  54.5 3.2 %collective-permute-start.10 = (f32[4,2048]{1,0:T(4,128)S(1)}, f32[4,2048]{1,0:T(4,128)S(1)}, u32[]{:S(2)}, u32[]{:S(2)}) collective-permute-start(f32[4,2048]{1,0:T(4,128)S(1)} %shard_map.98.st0), channel_id=1, source_target_pairs={{0,16},{8,24},{16,0},{24,8},{1,17},{9,25},{17,1},{25,9},{2,18},{10... | collective-permute-start | bytes 98312 | tf_op jit(solution)/shard_map/ppermute | solution.py:480
  57.7 0.8 collective-permute-start.11
  58.5 0.7 collective-permute-start.9
  59.2 1.3 %collective-permute-done.11.st3 = f32[4,2048]{1,0:T(4,128)S(1)} collective-permute-done((f32[4,2048]{1,0:T(4,128)S(1)}, f32[4,2048]{1,0:T(4,128)S(1)}, u32[]{:S(2)}, u32[]{:S(2)}) %collective-permute-start.11) | collective-permute-done | bytes 32800 | tf_op jit(solution)/shard_map/ppermute | solution.py:480
  60.5 2.0 %collective-permute-done.9.st1 = f32[4,2048]{1,0:T(4,128)S(1)} collective-permute-done((f32[4,2048]{1,0:T(4,128)S(1)}, f32[4,2048]{1,0:T(4,128)S(1)}, u32[]{:S(2)}, u32[]{:S(2)}) %collective-permute-start.9) | collective-permute-done | bytes 32800 | tf_op jit(solution)/shard_map/ppermute | solution.py:480
  62.5 3.8 %shard_map.99 = (bf16[16,128,256]{2,1,0:T(8,128)(2,1)}, bf16[128,512]{1,0:T(8,128)(2,1)S(1)}, bf16[128,512]{1,0:T(8,128)(2,1)S(1)}, bf16[128,512]{1,0:T(8,128)(2,1)S(1)}, bf16[128,512]{1,0:T(8,128)(2,1)S(1)}) custom-call(s32[5]{0:T(128)S(1)} %stack.23.place, bf16[2048,256]{1,0:T(8,128)(2,1)S(1)} %bitcast.8, bf16[2048,128]{1,0:T(8,128)(2,1)S(1)} %get-tuple-element.55.q_rows, ...), custom_call_target="tpu_custom_call" | custom-call | flops 5368709120 | bytes 4194304 | tf_op jit(solution)/shard_map/pallas_call | solution.py:130
  66.3 0.6 copy-done.3
  67.0 17.4 %all-to-all-start.1 = ((bf16[16,128,256]{2,1,0:T(8,128)(2,1)}), bf16[16,128,256]{2,1,0:T(8,128)(2,1)S(1)}, u32[]{:S(2)}, u32[]{:S(2)}) async-start(bf16[16,128,256]{2,1,0:T(8,128)(2,1)} %get-tuple-element.58), calls=%async_computation.1 | async-start | bytes 2097152 | tf_op jit(solution)/shard_map/all_to_all | solution.py:483
  84.5 1.5 %collective-permute-start.13 = (bf16[128,512]{1,0:T(8,128)(2,1)S(1)}, bf16[128,512]{1,0:T(8,128)(2,1)S(1)}, u32[]{:S(2)}, u32[]{:S(2)}) collective-permute-start(bf16[128,512]{1,0:T(8,128)(2,1)S(1)} %get-tuple-element.61), channel_id=1, source_target_pairs={{0,16},{8,24},{16,0},{24,8},{1,17},{9,25},{17,1},{25,9},{2,18},{10... | collective-permute-start | bytes 393224 | tf_op jit(solution)/shard_map/ppermute | solution.py:484
  86.0 2.5 %collective-permute-done.12.dq1 = bf16[128,512]{1,0:T(8,128)(2,1)S(1)} collective-permute-done((bf16[128,512]{1,0:T(8,128)(2,1)}, bf16[128,512]{1,0:T(8,128)(2,1)S(1)}, u32[]{:S(2)}, u32[]{:S(2)}) %collective-permute-start.12) | collective-permute-done | bytes 131104 | tf_op jit(solution)/shard_map/ppermute | solution.py:484
  88.5 1.4 %collective-permute-done.13.dq2 = bf16[128,512]{1,0:T(8,128)(2,1)S(1)} collective-permute-done((bf16[128,512]{1,0:T(8,128)(2,1)S(1)}, bf16[128,512]{1,0:T(8,128)(2,1)S(1)}, u32[]{:S(2)}, u32[]{:S(2)}) %collective-permute-start.13) | collective-permute-done | bytes 131104 | tf_op jit(solution)/shard_map/ppermute | solution.py:484
  89.9 1.4 %collective-permute-done.14.dq3 = bf16[128,512]{1,0:T(8,128)(2,1)S(1)} collective-permute-done((bf16[128,512]{1,0:T(8,128)(2,1)S(1)}, bf16[128,512]{1,0:T(8,128)(2,1)S(1)}, u32[]{:S(2)}, u32[]{:S(2)}) %collective-permute-start.14) | collective-permute-done | bytes 131104 | tf_op jit(solution)/shard_map/ppermute | solution.py:484
  91.3 3.7 %shard_map.100 = (bf16[128,1024]{1,0:T(8,128)(2,1)S(1)}, bf16[128,1024]{1,0:T(8,128)(2,1)S(1)}, bf16[128,1024]{1,0:T(8,128)(2,1)S(1)}, bf16[128,1024]{1,0:T(8,12...) custom-call(s32[5]{0:T(128)S(1)} %stack.23.place, bf16[128,512]{1,0:T(8,128)(2,1)S(1)} %get-tuple-element.59.dq0, ...), custom_call_target="tpu_custom_call" | custom-call | flops 536870912 | bytes 8388608 | tf_op jit(solution)/shard_map/pallas_call | solution.py:130
  95.0 4.8 %collective-permute-start.16 = (bf16[128,1024]{1,0:T(8,128)(2,1)S(1)}, bf16[128,1024]{1,0:T(8,128)(2,1)S(1)}, u32[]{:S(2)}, u32[]{:S(2)}) collective-permute-start(bf16[128,1024]{1,0:T(8,128)(2,1)S(1)} %get-tuple-element.66), channel_id=1, source_target_pairs={{0,1},{1,0},{2,3},{3,2},{4,5},{5,4},{6,7},{7,6},{8,9},{9,8},{10,11... | collective-permute-start | bytes 786440 | tf_op jit(solution)/shard_map/ppermute | solution.py:409
  99.8 0.3 collective-permute-start.15
  100.1 0.8 collective-permute-done.16
  101.0 0.8 add_convert_fusion.2
  101.8 8.1 %all-to-all-done.1.parts = bf16[16,128,256]{2,1,0:T(8,128)(2,1)S(1)} async-done(((bf16[16,128,256]{2,1,0:T(8,128)(2,1)}), bf16[16,128,256]{2,1,0:T(8,128)(2,1)S(1)}, u32[]{:S(2)}, u32[]{:S(2)}) %all-to-all-start.1) | async-done | bytes 1048608 | tf_op jit(solution)/shard_map/all_to_all | solution.py:483
  110.0 1.4 %shard_map.101 = (bf16[128,1024]{1,0:T(8,128)(2,1)S(1)}, f32[128,1024]{1,0:T(8,128)S(1)}, bf16[128,128]{1,0:T(8,128)(2,1)}, bf16[128,128]{1,0:T(8,128)(2,1)}, bf16[128,256]{1,0:T(8,128)(2,1)S(1)}) custom-call(s32[5]{0:T(128)S(1)} %stack.23.place, bf16[16,128,256]{2,1,0:T(8,128)(2,1)S(1)} %all-to-all-done.1.parts, ...), custom_call_target="tpu_custom_call" | custom-call | flops 134217728 | bytes 2097152 | tf_op jit(solution)/shard_map/pallas_call | solution.py:130
  111.3 5.1 %collective-permute-start.17 = (bf16[128,1024]{1,0:T(8,128)(2,1)S(1)}, bf16[128,1024]{1,0:T(8,128)(2,1)S(1)}, u32[]{:S(2)}, u32[]{:S(2)}) collective-permute-start(bf16[128,1024]{1,0:T(8,128)(2,1)S(1)} %get-tuple-element.72), channel_id=1, source_target_pairs={{0,1},{1,0},{2,3},{3,2},{4,5},{5,4},{6,7},{7,6},{8,9},{9,8},{10,11... | collective-permute-start | bytes 786440 | tf_op jit(solution)/shard_map/ppermute | solution.py:409
  116.5 1.2 collective-permute-done.17
  117.7 0.4 collective-permute-start.18
  118.1 1.0 shard_map.102
  119.1 0.7 collective-permute-start.19
  119.8 5.5 %collective-permute-done.18 = bf16[128,1024]{1,0:T(8,128)(2,1)S(1)} collective-permute-done((bf16[128,1024]{1,0:T(8,128)(2,1)S(1)}, bf16[128,1024]{1,0:T(8,128)(2,1)S(1)}, u32[]{:S(2)}, u32[]{:S(2)}) %collective-permute-start.18) | collective-permute-done | bytes 262176 | tf_op jit(solution)/shard_map/ppermute | solution.py:412
  125.4 0.8 add_convert_fusion
  (23 shorter events, 0.4 us)
Async XLA Ops:
  0.6 4.7 %collective-permute-start.1 = (bf16[128,1024]{1,0:T(8,128)(2,1)}, bf16[128,1024]{1,0:T(8,128)(2,1)S(1)}, u32[]{:S(2)}, u32[]{:S(2)}) collective-permute-start(bf16[128,1024]{1,0:T(8,128)(2,1)} %x0.1), channel_id=1, source_target_pairs={{0,1},{1,0},{2,3},{3,2},{4,5},{5,4},{6,7},{7,6},{8,9},{9,8},{10,11... | collective-permute-start | bytes 786440 | tf_op jit(solution)/shard_map/ppermute | solution.py:409
  4.0 1.7 %collective-permute-start.2 = (bf16[128,1024]{1,0:T(8,128)(2,1)}, bf16[128,1024]{1,0:T(8,128)(2,1)S(1)}, u32[]{:S(2)}, u32[]{:S(2)}) collective-permute-start(bf16[128,1024]{1,0:T(8,128)(2,1)} %g0.1), channel_id=1, source_target_pairs={{0,1},{1,0},{2,3},{3,2},{4,5},{5,4},{6,7},{7,6},{8,9},{9,8},{10,11... | collective-permute-start | bytes 786440 | tf_op jit(solution)/shard_map/ppermute | solution.py:409
  4.1 7.7 %collective-permute-start = (bf16[128,1024]{1,0:T(8,128)(2,1)}, bf16[128,1024]{1,0:T(8,128)(2,1)S(1)}, u32[]{:S(2)}, u32[]{:S(2)}) collective-permute-start(bf16[128,1024]{1,0:T(8,128)(2,1)} %x0.1), channel_id=1, source_target_pairs={{0,2},{2,0},{1,3},{3,1},{4,6},{6,4},{5,7},{7,5},{8,10},{10,8},{9,1... | collective-permute-start | bytes 786440 | tf_op jit(solution)/shard_map/ppermute | solution.py:412
  5.7 0.9 copy-start
  11.8 4.5 %copy-start.2 = (f32[128,512]{1,0:T(8,128)}, f32[128,512]{1,0:T(8,128)S(1)}, u32[]{:S(2)}) copy-start(f32[128,512]{1,0:T(8,128)S(1)} %get-tuple-element.53.g_half) | copy-start | bytes 786436
  11.8 2.4 %collective-permute-start.3 = (bf16[128,1024]{1,0:T(8,128)(2,1)S(1)}, bf16[128,1024]{1,0:T(8,128)(2,1)S(1)}, u32[]{:S(2)}, u32[]{:S(2)}) collective-permute-start(bf16[128,1024]{1,0:T(8,128)(2,1)S(1)} %collective-permute-done.x2), channel_id=1, source_target_pairs={{0,1},{1,0},{2,3},{3,2},{4,5},{5,4},{6,7},{7,6},{8,9},{9,8},{10,11... | collective-permute-start | bytes 786440 | tf_op jit(solution)/shard_map/ppermute | solution.py:409
  13.0 13.0 %collective-permute-start.4 = (bf16[128,1024]{1,0:T(8,128)(2,1)}, bf16[128,1024]{1,0:T(8,128)(2,1)S(1)}, u32[]{:S(2)}, u32[]{:S(2)}) collective-permute-start(bf16[128,1024]{1,0:T(8,128)(2,1)} %g0.1), channel_id=1, source_target_pairs={{0,2},{2,0},{1,3},{3,1},{4,6},{6,4},{5,7},{7,5},{8,10},{10,8},{9,1... | collective-permute-start | bytes 786440 | tf_op jit(solution)/shard_map/ppermute | solution.py:412
  16.3 0.7 copy-start.4
  17.0 36.2 %all-to-all-start = ((bf16[16,128,256]{2,1,0:T(8,128)(2,1)}), bf16[16,128,256]{2,1,0:T(8,128)(2,1)S(1)}, u32[]{:S(2)}, u32[]{:S(2)}) async-start(bf16[16,128,256]{2,1,0:T(8,128)(2,1)} %get-tuple-element.49), calls=%async_computation | async-start | bytes 2097152 | tf_op jit(solution)/shard_map/all_to_all | solution.py:464
  26.0 1.9 %collective-permute-start.5 = (bf16[128,1024]{1,0:T(8,128)(2,1)S(1)}, bf16[128,1024]{1,0:T(8,128)(2,1)S(1)}, u32[]{:S(2)}, u32[]{:S(2)}) collective-permute-start(bf16[128,1024]{1,0:T(8,128)(2,1)S(1)} %collective-permute-done.4.g2), channel_id=1, source_target_pairs={{0,1},{1,0},{2,3},{3,2},{4,5},{5,4},{6,7},{7,6},{8,9},{9,8},{10,11... | collective-permute-start | bytes 786440 | tf_op jit(solution)/shard_map/ppermute | solution.py:409
  30.1 15.7 %copy-start.1 = (bf16[128,1024]{1,0:T(8,128)(2,1)}, bf16[128,1024]{1,0:T(8,128)(2,1)S(1)}, u32[]{:S(2)}) copy-start(bf16[128,1024]{1,0:T(8,128)(2,1)S(1)} %shard_map.96.qd0) | copy-start | bytes 786436
  30.1 8.9 %collective-permute-start.6 = (bf16[128,1024]{1,0:T(8,128)(2,1)S(1)}, bf16[128,1024]{1,0:T(8,128)(2,1)S(1)}, u32[]{:S(2)}, u32[]{:S(2)}) collective-permute-start(bf16[128,1024]{1,0:T(8,128)(2,1)S(1)} %shard_map.96.qd0), channel_id=1, source_target_pairs={{0,8},{8,16},{16,24},{24,0},{1,9},{9,17},{17,25},{25,1},{2,10},{10... | collective-permute-start | bytes 786440 | tf_op jit(solution)/shard_map/ppermute | solution.py:465
  31.5 14.3 %collective-permute-start.7 = (bf16[128,1024]{1,0:T(8,128)(2,1)S(1)}, bf16[128,1024]{1,0:T(8,128)(2,1)S(1)}, u32[]{:S(2)}, u32[]{:S(2)}) collective-permute-start(bf16[128,1024]{1,0:T(8,128)(2,1)S(1)} %shard_map.96.qd0), channel_id=1, source_target_pairs={{0,16},{8,24},{16,0},{24,8},{1,17},{9,25},{17,1},{25,9},{2,18},{10... | collective-permute-start | bytes 786440 | tf_op jit(solution)/shard_map/ppermute | solution.py:465
  34.1 11.7 %collective-permute-start.8 = (bf16[128,1024]{1,0:T(8,128)(2,1)S(1)}, bf16[128,1024]{1,0:T(8,128)(2,1)S(1)}, u32[]{:S(2)}, u32[]{:S(2)}) collective-permute-start(bf16[128,1024]{1,0:T(8,128)(2,1)S(1)} %shard_map.96.qd0), channel_id=1, source_target_pairs={{0,24},{8,0},{16,8},{24,16},{1,25},{9,1},{17,9},{25,17},{2,26},{10... | collective-permute-start | bytes 786440 | tf_op jit(solution)/shard_map/ppermute | solution.py:465
  54.5 4.7 %collective-permute-start.10 = (f32[4,2048]{1,0:T(4,128)S(1)}, f32[4,2048]{1,0:T(4,128)S(1)}, u32[]{:S(2)}, u32[]{:S(2)}) collective-permute-start(f32[4,2048]{1,0:T(4,128)S(1)} %shard_map.98.st0), channel_id=1, source_target_pairs={{0,16},{8,24},{16,0},{24,8},{1,17},{9,25},{17,1},{25,9},{2,18},{10... | collective-permute-start | bytes 98312 | tf_op jit(solution)/shard_map/ppermute | solution.py:480
  57.7 2.8 %collective-permute-start.11 = (f32[4,2048]{1,0:T(4,128)S(1)}, f32[4,2048]{1,0:T(4,128)S(1)}, u32[]{:S(2)}, u32[]{:S(2)}) collective-permute-start(f32[4,2048]{1,0:T(4,128)S(1)} %shard_map.98.st0), channel_id=1, source_target_pairs={{0,24},{8,0},{16,8},{24,16},{1,25},{9,1},{17,9},{25,17},{2,26},{10... | collective-permute-start | bytes 98312 | tf_op jit(solution)/shard_map/ppermute | solution.py:480
  58.5 4.0 %collective-permute-start.9 = (f32[4,2048]{1,0:T(4,128)S(1)}, f32[4,2048]{1,0:T(4,128)S(1)}, u32[]{:S(2)}, u32[]{:S(2)}) collective-permute-start(f32[4,2048]{1,0:T(4,128)S(1)} %shard_map.98.st0), channel_id=1, source_target_pairs={{0,8},{8,16},{16,24},{24,0},{1,9},{9,17},{17,25},{25,1},{2,10},{10... | collective-permute-start | bytes 98312 | tf_op jit(solution)/shard_map/ppermute | solution.py:480
  66.3 0.7 copy-start.3
  67.0 43.0 %all-to-all-start.1 = ((bf16[16,128,256]{2,1,0:T(8,128)(2,1)}), bf16[16,128,256]{2,1,0:T(8,128)(2,1)S(1)}, u32[]{:S(2)}, u32[]{:S(2)}) async-start(bf16[16,128,256]{2,1,0:T(8,128)(2,1)} %get-tuple-element.58), calls=%async_computation.1 | async-start | bytes 2097152 | tf_op jit(solution)/shard_map/all_to_all | solution.py:483
  84.4 4.1 %collective-permute-start.12 = (bf16[128,512]{1,0:T(8,128)(2,1)}, bf16[128,512]{1,0:T(8,128)(2,1)S(1)}, u32[]{:S(2)}, u32[]{:S(2)}) collective-permute-start(bf16[128,512]{1,0:T(8,128)(2,1)} %copy-done.3), channel_id=1, source_target_pairs={{0,24},{8,0},{16,8},{24,16},{1,25},{9,1},{17,9},{25,17},{2,26},{10... | collective-permute-start | bytes 393224 | tf_op jit(solution)/shard_map/ppermute | solution.py:484
  84.5 5.4 %collective-permute-start.13 = (bf16[128,512]{1,0:T(8,128)(2,1)S(1)}, bf16[128,512]{1,0:T(8,128)(2,1)S(1)}, u32[]{:S(2)}, u32[]{:S(2)}) collective-permute-start(bf16[128,512]{1,0:T(8,128)(2,1)S(1)} %get-tuple-element.61), channel_id=1, source_target_pairs={{0,16},{8,24},{16,0},{24,8},{1,17},{9,25},{17,1},{25,9},{2,18},{10... | collective-permute-start | bytes 393224 | tf_op jit(solution)/shard_map/ppermute | solution.py:484
  86.0 5.3 %collective-permute-start.14 = (bf16[128,512]{1,0:T(8,128)(2,1)S(1)}, bf16[128,512]{1,0:T(8,128)(2,1)S(1)}, u32[]{:S(2)}, u32[]{:S(2)}) collective-permute-start(bf16[128,512]{1,0:T(8,128)(2,1)S(1)} %get-tuple-element.62), channel_id=1, source_target_pairs={{0,8},{8,16},{16,24},{24,0},{1,9},{9,17},{17,25},{25,1},{2,10},{10... | collective-permute-start | bytes 393224 | tf_op jit(solution)/shard_map/ppermute | solution.py:484
  95.0 6.0 %collective-permute-start.16 = (bf16[128,1024]{1,0:T(8,128)(2,1)S(1)}, bf16[128,1024]{1,0:T(8,128)(2,1)S(1)}, u32[]{:S(2)}, u32[]{:S(2)}) collective-permute-start(bf16[128,1024]{1,0:T(8,128)(2,1)S(1)} %get-tuple-element.66), channel_id=1, source_target_pairs={{0,1},{1,0},{2,3},{3,2},{4,5},{5,4},{6,7},{7,6},{8,9},{9,8},{10,11... | collective-permute-start | bytes 786440 | tf_op jit(solution)/shard_map/ppermute | solution.py:409
  99.8 1.9 %collective-permute-start.15 = (bf16[128,1024]{1,0:T(8,128)(2,1)S(1)}, bf16[128,1024]{1,0:T(8,128)(2,1)S(1)}, u32[]{:S(2)}, u32[]{:S(2)}) collective-permute-start(bf16[128,1024]{1,0:T(8,128)(2,1)S(1)} %get-tuple-element.64), channel_id=1, source_target_pairs={{0,1},{1,0},{2,3},{3,2},{4,5},{5,4},{6,7},{7,6},{8,9},{9,8},{10,11... | collective-permute-start | bytes 786440 | tf_op jit(solution)/shard_map/ppermute | solution.py:409
  110.0 15.3 %copy-start.5 = (bf16[128,1024]{1,0:T(8,128)(2,1)S(1)}, bf16[128,1024]{1,0:T(8,128)(2,1)}, u32[]{:S(2)}) copy-start(bf16[128,1024]{1,0:T(8,128)(2,1)} %add_convert_fusion.2) | copy-start | bytes 786436
  111.3 6.3 %collective-permute-start.17 = (bf16[128,1024]{1,0:T(8,128)(2,1)S(1)}, bf16[128,1024]{1,0:T(8,128)(2,1)S(1)}, u32[]{:S(2)}, u32[]{:S(2)}) collective-permute-start(bf16[128,1024]{1,0:T(8,128)(2,1)S(1)} %get-tuple-element.72), channel_id=1, source_target_pairs={{0,1},{1,0},{2,3},{3,2},{4,5},{5,4},{6,7},{7,6},{8,9},{9,8},{10,11... | collective-permute-start | bytes 786440 | tf_op jit(solution)/shard_map/ppermute | solution.py:409
  117.7 7.6 %collective-permute-start.18 = (bf16[128,1024]{1,0:T(8,128)(2,1)S(1)}, bf16[128,1024]{1,0:T(8,128)(2,1)S(1)}, u32[]{:S(2)}, u32[]{:S(2)}) collective-permute-start(bf16[128,1024]{1,0:T(8,128)(2,1)S(1)} %add_convert_fusion.1), channel_id=1, source_target_pairs={{0,2},{2,0},{1,3},{3,1},{4,6},{6,4},{5,7},{7,5},{8,10},{10,8},{9,1... | collective-permute-start | bytes 786440 | tf_op jit(solution)/shard_map/ppermute | solution.py:412
  119.1 6.3 %collective-permute-start.19 = (bf16[128,1024]{1,0:T(8,128)(2,1)S(1)}, bf16[128,1024]{1,0:T(8,128)(2,1)S(1)}, u32[]{:S(2)}, u32[]{:S(2)}) collective-permute-start(bf16[128,1024]{1,0:T(8,128)(2,1)S(1)} %get-tuple-element.78), channel_id=1, source_target_pairs={{0,1},{1,0},{2,3},{3,2},{4,5},{5,4},{6,7},{7,6},{8,9},{9,8},{10,11... | collective-permute-start | bytes 786440 | tf_op jit(solution)/shard_map/ppermute | solution.py:409

commit v4 on v3

--- a/solution.py
+++ b/solution.py
@@ -18,8 +18,10 @@
 HEADS = 4
 ROWS = HEADS * BLOCK
 CHUNK = 2 * BLOCK
-FAR_FLOPS = 15_000_000_000
+FAR_FLOPS = 10_000_000_000
 STEP = 512
+STAT_FLOPS = 4 * 2048 * 2048 * 128
+GRAD_FLOPS = 10 * 2048 * 2048 * 128
 VMEM_LIMIT = 20 * 1024 * 1024
 BF16 = jnp.bfloat16
 F32 = jnp.float32
@@ -134,7 +136,10 @@
             pl.BlockSpec(memory_space=pltpu.HBM) if i in hbm_outs else vmem
             for i in range(len(outs))
         ],
-        out_shape=outs,
+        out_shape=[
+            pltpu.HBM(out.shape, out.dtype) if i in hbm_outs else out
+            for i, out in enumerate(outs)
+        ],
         scratch_shapes=list(scratch),
         compiler_params=pltpu.CompilerParams(vmem_limit_bytes=VMEM_LIMIT),
         cost_estimate=pl.CostEstimate(flops=flops, bytes_accessed=traffic, transcendentals=exps),
@@ -152,7 +157,18 @@
     return jnp.where(keys <= times[pl.ds(query_block, 1), :], 0.0, NEG_FILL)
 
 
-def stack_kernel(place, times_hbm, qd0, qd1, qd2, qd3, q_rows, g_rows, bias, times, own, sems):
+def stack_kernel(
+    place, times_hbm, qd0, qd1, qd2, qd3, wk, wv,
+    q_rows, g_rows, bias, far_kv, times, own, weights, sems,
+):
+    packs = []
+    rows = pl.ds(pl.multiple_of((1 - place[3]) * PAIR, PAIR), PAIR)
+    for k, weight in enumerate((wk, wv)):
+        held = weights.at[k]
+        fetched = pltpu.make_async_copy(weight.at[rows, :], held, sems.at[2 + 2 * k])
+        packs.append((fetched, pltpu.make_async_copy(held, far_kv.at[k], sems.at[3 + 2 * k])))
+    for fetched, _ in packs:
+        fetched.start()
     copies = [
         pltpu.make_async_copy(qd0, own, sems.at[0]),
         pltpu.make_async_copy(times_hbm, times, sems.at[1]),
@@ -164,6 +180,9 @@
             copies[0].wait()
         q_rows[s * ROWS : (s + 1) * ROWS, :] = stack_heads(qd, 0)
         g_rows[s * ROWS : (s + 1) * ROWS, :] = stack_heads(qd, 512)
+    for fetched, stored in packs:
+        fetched.wait()
+        stored.start()
     copies[1].wait()
     z, y, xh = place[0], place[1], place[2]
     for s in range(4):
@@ -174,6 +193,8 @@
             bias[h * BLOCK : (h + 1) * BLOCK, cols] = visible(times, key_block, query_block)
     bias[2 * BLOCK :, :BLOCK] = visible(times, 8 * jnp.minimum(z + 1, 7), 8 * z + 7)
     bias[2 * BLOCK :, BLOCK:] = jnp.full((BLOCK, 3 * BLOCK), NEG_FILL, F32)
+    for _, stored in packs:
+        stored.wait()
 
 
 def for_tiles(place, bias, tile, done):
@@ -240,9 +261,8 @@
         stats_kernel,
         (place, kv, *rows),
         [jax.ShapeDtypeStruct((4, 4 * ROWS), F32)],
-        flops=4 * 2048 * 2048 * 128,
+        flops=STAT_FLOPS,
         traffic=2 << 20,
-        exps=2048 * 2048,
     )
     return out
 
@@ -345,9 +365,8 @@
             pltpu.SemaphoreType.DMA((8,)),
         ],
         hbm_outs=(0, 1, 2, 3, 4),
-        flops=10 * 2048 * 2048 * 128,
+        flops=GRAD_FLOPS,
         traffic=4 << 20,
-        exps=2048 * 2048,
     )
 
 
@@ -357,14 +376,18 @@
 
 
 def query_back_kernel(
-    place, dq0, dq1, dq2, dq3, wq, wk, wv, far0, far1, near1, near0, out_k, out_v, held, sems
+    place, dq0, dq1, dq2, dq3, wq, wk, wv, got_kv, far0, far1, near1, near0, out_kv, held, sems
 ):
     copies = [
         pltpu.make_async_copy(wq.at[feature_rows(place, flip), :], held.at[i], sems.at[i])
         for i, flip in enumerate((3, 2, 1, 0))
     ]
-    copies.append(pltpu.make_async_copy(wk, out_k, sems.at[4]))
-    copies.append(pltpu.make_async_copy(wv, out_v, sems.at[5]))
+    rows = pl.ds(pl.multiple_of(place[3] * PAIR, PAIR), PAIR)
+    sources = (wk.at[rows, :], wv.at[rows, :], got_kv.at[0], got_kv.at[1])
+    for i, source in enumerate(sources):
+        low = (i % 2) * HEAD
+        target = out_kv.at[i // 2, :, low : low + HEAD]
+        copies.append(pltpu.make_async_copy(source, target, sems.at[4 + i]))
     for copy in copies:
         copy.start()
     parts = [d[...].astype(F32) for d in (dq0, dq1, dq2, dq3)]
@@ -372,16 +395,11 @@
     for i, out in enumerate((far0, far1, near1, near0)):
         copies[i].wait()
         out[...] = contract_last(total, held[i]).astype(out.dtype)
-    copies[4].wait()
-    copies[5].wait()
-
-
-def key_terms(place, flip, dk, dv, wk, wv):
-    rows = feature_rows(place, flip)
-    return contract_last(dk, wk[rows, :]) + contract_last(dv, wv[rows, :])
-
-
-def key_far_kernel(place, parts, wk, wv, queries, far0, far1, dk, dv, dkv):
+    for copy in copies[4:]:
+        copy.wait()
+
+
+def key_sum_kernel(place, parts, dk, dv, dkv):
     total = parts[0].astype(F32)
     for i in range(1, 16):
         total = total + parts[i].astype(F32)
@@ -389,14 +407,20 @@
     dv[...] = total[:, HEAD:].astype(BF16)
     dkv[:, :HEAD] = dk[...]
     dkv[:, HEAD:] = dv[...]
-    far0[...] = key_terms(place, 3, dk[...], dv[...], wk, wv).astype(BF16)
-    far1[...] = queries[...].astype(F32) + key_terms(place, 2, dk[...], dv[...], wk, wv)
-
-
-def key_near_kernel(place, dkv, wk, wv, near1, near0):
-    dk, dv = dkv[:, :HEAD], dkv[:, HEAD:]
-    near1[...] = key_terms(place, 1, dk, dv, wk, wv).astype(BF16)
-    near0[...] = key_terms(place, 0, dk, dv, wk, wv)
+
+
+def key_near_kernel(place, dkv, weights, queries, own, other):
+    mine, siblings = core_halves(place[4])
+    own[...] = queries[...].astype(F32) + contract_last(dkv[...], weights[0, mine, :])
+    other[...] = contract_last(dkv[...], weights[0, siblings, :])
+
+
+def key_far_kernel(place, dkv, weights, own, other, queries, own_out, other_out):
+    mine, siblings = core_halves(place[4])
+    other_out[...] = (other[...] + contract_last(dkv[...], weights[1, siblings, :])).astype(BF16)
+    own_out[...] = (
+        own[...] + queries[...].astype(F32) + contract_last(dkv[...], weights[1, mine, :])
+    )
 
 
 def local(inputs, out_grad, w_query, key_weight, value_weight, w_output, times):
@@ -464,65 +488,70 @@
     kv = lax.all_to_all(kv_own, ("z", "xh"), 0, 0, tiled=True).reshape(16 * BLOCK, 2 * HEAD)
     blocks = [qd_own] + [lax.ppermute(qd_own, "y", shifted(4, s)) for s in (1, 2, 3)]
 
-    rows = whole_call(
+    *rows, far_kv = whole_call(
         stack_kernel,
-        (place, times2d, *blocks),
-        [shape(4 * ROWS, HEAD)] * 2 + [shape(CHUNK + BLOCK, ROWS, kind=F32)],
+        (place, times2d, *blocks, key_weight, value_weight),
+        [shape(4 * ROWS, HEAD)] * 2
+        + [shape(CHUNK + BLOCK, ROWS, kind=F32)]
+        + [shape(2, PAIR, HEAD)],
         [
             pltpu.VMEM((64, BLOCK), jnp.int32),
             pltpu.VMEM((BLOCK, 1024), BF16),
-            pltpu.SemaphoreType.DMA((2,)),
+            pltpu.VMEM((2, PAIR, HEAD), BF16),
+            pltpu.SemaphoreType.DMA((6,)),
         ],
-        hbm=(1, 2),
+        hbm=(1, 2, 6, 7),
+        hbm_outs=(3,),
         traffic=2 << 20,
     )
+    got_kv = to_xl(far_kv)
     own_stats = stats(place, kv, rows)
     gathered = [own_stats] + [lax.ppermute(own_stats, "y", shifted(4, s)) for s in (1, 2, 3)]
     dkv, *dqs = grads(place, kv, rows, gathered)
 
+    dkv, got_kv = lax.optimization_barrier((dkv, got_kv))
     dkv_parts = lax.all_to_all(dkv, ("z", "xh"), 0, 0, tiled=True)
     dq_parts = [dqs[0]] + [lax.ppermute(dqs[s], "y", shifted(4, -s)) for s in (1, 2, 3)]
 
     def add(*values):
         return sum(v.astype(F32) for v in values)
 
-    far0, far1, near1, near0, held_k, held_v = whole_call(
+    far0, far1, near1, near0, held_kv = whole_call(
         query_back_kernel,
-        (place, *dq_parts, w_query, key_weight, value_weight),
-        [shape(BLOCK, 1024)] * 4 + [shape(2 * PAIR, HEAD)] * 2,
-        [pltpu.VMEM((4, 1024, ROWS), BF16), pltpu.SemaphoreType.DMA((6,))],
-        hbm=(5, 6, 7),
+        (place, *dq_parts, w_query, key_weight, value_weight, got_kv),
+        [shape(BLOCK, 1024)] * 4 + [shape(2, PAIR, 2 * HEAD)],
+        [pltpu.VMEM((4, 1024, ROWS), BF16), pltpu.SemaphoreType.DMA((8,))],
+        hbm=(5, 6, 7, 8),
         flops=2 * 128 * 4096 * 512,
         traffic=8 << 20,
     )
-    far_query = add(far1, to_core(far0)).astype(BF16)
-    near_query = add(near0, to_core(near1)).astype(BF16)
-    dkv_parts, far_query, near_query = lax.optimization_barrier(
-        (dkv_parts, far_query, near_query)
-    )
-
-    far0, far1, dk, dv, dkv_own = whole_call(
+    far_queries = to_xl(add(far1, to_core(far0)).astype(BF16))
+    near_queries = add(near0, to_core(near1)).astype(BF16)
+    dkv_parts, near_queries = lax.optimization_barrier((dkv_parts, near_queries))
+
+    dk, dv, dkv_own = whole_call(
+        key_sum_kernel,
+        (place, dkv_parts),
+        [shape(BLOCK, HEAD)] * 2 + [shape(BLOCK, 2 * HEAD)],
+        traffic=2 << 20,
+    )
+    dkv_far = to_xl(dkv_own)
+    halves = [shape(BLOCK, 1024, kind=F32)] * 2
+    own_half, other_half = whole_call(
+        key_near_kernel,
+        (place, dkv_own, held_kv, near_queries),
+        halves,
+        flops=2 * 128 * 256 * 2048,
+        traffic=2 << 20,
+    )
+    own_half, other_half = whole_call(
         key_far_kernel,
-        (place, dkv_parts, held_k, held_v, far_query),
-        [shape(BLOCK, 1024), shape(BLOCK, 1024, kind=F32)]
-        + [shape(BLOCK, HEAD)] * 2
-        + [shape(BLOCK, 2 * HEAD)],
-        flops=2 * 128 * 2048 * 256,
+        (place, dkv_far, held_kv, own_half, other_half, far_queries),
+        [halves[0], shape(BLOCK, 1024)],
+        flops=2 * 128 * 256 * 2048,
         traffic=2 << 20,
     )
-    far_sum, dkv_own = lax.optimization_barrier(
-        (add(far1, to_core(far0)).astype(BF16), dkv_own)
-    )
-    from_far = to_xl(far_sum)
-    near1, near0 = whole_call(
-        key_near_kernel,
-        (place, dkv_own, held_k, held_v),
-        [shape(BLOCK, 1024), shape(BLOCK, 1024, kind=F32)],
-        flops=2 * 128 * 2048 * 256,
-        traffic=2 << 20,
-    )
-    before = lax.optimization_barrier(add(from_far, near_query))
-    input_grad = add(before, near0, to_core(near1)).astype(BF16)
+    input_grad = add(own_half, to_core(other_half)).astype(BF16)
     return input_grad, dk, dv
 
 

time: 127 us -> 125 us (0.984)
  starting transfers between devices: 54.5 us -> 46.1 us
  waiting for transfers between devices: 44.2 us -> 48.5 us
  Pallas kernels: 22.5 us -> 26 us
  local copies, waits for them, and re-layouts: 2.35 us -> 1.05 us
    all_to_all x1, starting transfers between devices: 17.4 us -> 11 us  [local(): dkv_parts = lax.all_to_all(dkv, ('z', 'xh'), 0, 0, tiled=True)]
    ppermute x3 -> x5, waiting for transfers between devices: 5.5 us -> 10.8 us  [to_xl(): return lax.ppermute(value, 'xl', swap)]
    pallas_call x9 -> x10, Pallas kernels: 22.5 us -> 26 us  [whole_call(): pl.pallas_call(kernel, in_specs=in_specs, out_specs=[pl.BlockSpec(memory_...]
    ppermute x8 -> x7, starting transfers between devices: 16.4 us -> 14 us  [to_core(): return lax.ppermute(value, 'core', swap)]
    all_to_all x1, waiting for transfers between devices: 5.56 us -> 3.22 us  [local(): lax.all_to_all(kv_own, ('z', 'xh'), 0, 0, tiled=True)]
    unnamed x12 -> x10, local copies, waits for them, and re-layouts: 2.26 us -> 0.97 us
    ppermute x8 -> x7, waiting for transfers between devices: 5.89 us -> 6.1 us  [to_core(): return lax.ppermute(value, 'core', swap)]
  transfers between devices with their start and end apart: 22 -> 23, of which waited for: 16 -> 18; matrix products, arithmetic and copies ran while one was open for 1% -> 1% of each run, Pallas kernels for 13% -> 20%
where the time goes in v4:
time: 125 us; the launch traced here: 124 us
  waiting for transfers between devices  48.5 us (39%)
  starting transfers between devices  46.1 us (37%)
  Pallas kernels  26 us (21%)
  other arithmetic  1.6 us (1%)
    pallas_call x10, Pallas kernels, whole_call(): pl.pallas_call(kernel, in_specs=in_specs, out_specs=[pl.BlockSpec(memory_...  26 us
    ppermute x7, starting transfers between devices, to_core(): return lax.ppermute(value, 'core', swap)  14 us
    all_to_all x1, starting transfers between devices, local(): dkv_parts = lax.all_to_all(dkv, ('z', 'xh'), 0, 0, tiled=True)  11 us
    ppermute x5, waiting for transfers between devices, to_xl(): return lax.ppermute(value, 'xl', swap)  10.8 us
    ppermute x3, waiting for transfers between devices, local(): lax.ppermute(qd_own, 'y', shifted(4, s))  10.8 us
    all_to_all x1, starting transfers between devices, local(): lax.all_to_all(kv_own, ('z', 'xh'), 0, 0, tiled=True)  9.03 us
    all_to_all x1, waiting for transfers between devices, local(): dkv_parts = lax.all_to_all(dkv, ('z', 'xh'), 0, 0, tiled=True)  7.95 us
    ppermute x3, waiting for transfers between devices, local(): lax.ppermute(dqs[s], 'y', shifted(4, -s))  6.33 us
  transfers between devices with their start and end apart: 23, of which 18 were waited for; matrix products, arithmetic and copies ran while one was open for 1% of the time, Pallas kernels for 20%

profile of v4, /device:TPU:1, one launch (start us, length us, event | category | flops | bytes accessed | tf_op | source)
XLA Modules:
  0.0 124.1 jit_solution(12910615456493620484)
XLA Ops:
  0.6 3.3 %collective-permute-start.1 = (bf16[128,1024]{1,0:T(8,128)(2,1)}, bf16[128,1024]{1,0:T(8,128)(2,1)S(1)}, u32[]{:S(2)}, u32[]{:S(2)}) collective-permute-start(bf16[128,1024]{1,0:T(8,128)(2,1)} %x0.1), channel_id=1, source_target_pairs={{0,1},{1,0},{2,3},{3,2},{4,5},{5,4},{6,7},{7,6},{8,9},{9,8},{10,11... | collective-permute-start | bytes 786440 | tf_op jit(solution)/shard_map/ppermute | solution.py:433
  4.1 1.2 collective-permute-done.1.x1
  5.3 0.4 collective-permute-done.2.g1
  5.7 0.9 copy-done
  6.7 5.2 %shard_map.94 = (f32[128,768]{1,0:T(8,128)S(1)}, f32[128,512]{1,0:T(8,128)}, bf16[2048,512]{1,0:T(8,128)(2,1)S(1)}, bf16[2048,128]{1,0:T(8,128)(2,1)S(1)}, bf16[...) custom-call(s32[5]{0:T(128)S(1)} %stack.23.place, bf16[128,1024]{1,0:T(8,128)(2,1)S(1)} %copy-done, ...), custom_call_target="tpu_custom_call" | custom-call | flops 671088640 | bytes 10485760 | tf_op jit(solution)/shard_map/pallas_call | solution.py:132
  11.9 1.1 collective-permute-start.3
  13.0 1.2 collective-permute-done.3.x3
  14.2 2.2 %shard_map.95 = (bf16[16,128,256]{2,1,0:T(8,128)(2,1)}, bf16[128,512]{1,0:T(8,128)(2,1)}) custom-call(s32[5]{0:T(128)S(1)} %stack.23.place, bf16[128,1024]{1,0:T(8,128)(2,1)S(1)} %collective-permute-done.x2, bf16[128,1024]{1,0:T(8,128)(2,1)S(1)} %collective-permute-done.3.x3, bf16[2048,512]{1,0:T(8,128)(2,1)S(1)} %get-tuple-element.44.wq, ...), custom_call_target="tpu_custom_call" | custom-call | flops 402653184 | bytes 4194304 | tf_op jit(solution)/shard_map/pallas_call | solution.py:132
  16.3 9.0 %all-to-all-start = ((bf16[16,128,256]{2,1,0:T(8,128)(2,1)}), bf16[16,128,256]{2,1,0:T(8,128)(2,1)S(1)}, u32[]{:S(2)}, u32[]{:S(2)}) async-start(bf16[16,128,256]{2,1,0:T(8,128)(2,1)} %get-tuple-element.48), calls=%async_computation | async-start | bytes 2097152 | tf_op jit(solution)/shard_map/all_to_all | solution.py:488
  25.4 0.7 collective-permute-start.5
  26.1 1.2 collective-permute-done.5.g3
  27.3 2.9 %shard_map.96.qd0 = bf16[128,1024]{1,0:T(8,128)(2,1)} custom-call(s32[5]{0:T(128)S(1)} %stack.23.place, bf16[128,1024]{1,0:T(8,128)(2,1)S(1)} %collective-permute-done.4.g2, bf16[128,1024]{1,0:T(8,128)(2,1)S(1)} %collective-permute-done.5.g3, bf16[512,2048]{1,0:T(8,128)(2,1)S(1)} %get-tuple-element.51.wo, f32[128,512]{1,0:T(8,128)} %get-tuple-element.52.g_half, ...), custom_call_target="tpu_custom_call" | custom-call | flops 10000000000 | bytes 3145728 | tf_op jit(solution)/shard_map/pallas_call | solution.py:132
  30.1 1.4 %collective-permute-start.6 = (bf16[128,1024]{1,0:T(8,128)(2,1)}, bf16[128,1024]{1,0:T(8,128)(2,1)S(1)}, u32[]{:S(2)}, u32[]{:S(2)}) collective-permute-start(bf16[128,1024]{1,0:T(8,128)(2,1)} %shard_map.96.qd0), channel_id=1, source_target_pairs={{0,8},{8,16},{16,24},{24,0},{1,9},{9,17},{17,25},{25,1},{2,10},{10... | collective-permute-start | bytes 786440 | tf_op jit(solution)/shard_map/ppermute | solution.py:489
  31.5 2.6 %collective-permute-start.7 = (bf16[128,1024]{1,0:T(8,128)(2,1)}, bf16[128,1024]{1,0:T(8,128)(2,1)S(1)}, u32[]{:S(2)}, u32[]{:S(2)}) collective-permute-start(bf16[128,1024]{1,0:T(8,128)(2,1)} %shard_map.96.qd0), channel_id=1, source_target_pairs={{0,16},{8,24},{16,0},{24,8},{1,17},{9,25},{17,1},{25,9},{2,18},{10... | collective-permute-start | bytes 786440 | tf_op jit(solution)/shard_map/ppermute | solution.py:489
  34.1 1.1 collective-permute-start.8
  35.2 4.1 %collective-permute-done.6.qd1 = bf16[128,1024]{1,0:T(8,128)(2,1)S(1)} collective-permute-done((bf16[128,1024]{1,0:T(8,128)(2,1)}, bf16[128,1024]{1,0:T(8,128)(2,1)S(1)}, u32[]{:S(2)}, u32[]{:S(2)}) %collective-permute-start.6) | collective-permute-done | bytes 262176 | tf_op jit(solution)/shard_map/ppermute | solution.py:489
  39.3 6.7 %collective-permute-done.7.qd2 = bf16[128,1024]{1,0:T(8,128)(2,1)S(1)} collective-permute-done((bf16[128,1024]{1,0:T(8,128)(2,1)}, bf16[128,1024]{1,0:T(8,128)(2,1)S(1)}, u32[]{:S(2)}, u32[]{:S(2)}) %collective-permute-start.7) | collective-permute-done | bytes 262176 | tf_op jit(solution)/shard_map/ppermute | solution.py:489
  46.0 2.9 %shard_map.97 = (bf16[2048,128]{1,0:T(8,128)(2,1)S(1)}, bf16[2048,128]{1,0:T(8,128)(2,1)S(1)}, f32[384,512]{1,0:T(8,128)S(1)}, bf16[2,2048,128]{2,1,0:T(8,128)(2,1)}) custom-call(s32[5]{0:T(128)S(1)} %stack.23.place, s32[64,128]{1,0:T(8,128)} %bitcast.9, bf16[128,1024]{1,0:T(8,128)(2,1)} %shard_map.96.qd0, bf16[128,1024]{1,0:T(8,128)(2,1)S(1)} %collective-permute-done.6.qd1, ...), custom_call_target="tpu_custom_call" | custom-call | bytes 2097152 | tf_op jit(solution)/shard_map/pallas_call | solution.py:132
  48.9 0.4 collective-permute-start.12
  49.3 3.2 %all-to-all-done = bf16[16,128,256]{2,1,0:T(8,128)(2,1)S(1)} async-done(((bf16[16,128,256]{2,1,0:T(8,128)(2,1)}), bf16[16,128,256]{2,1,0:T(8,128)(2,1)S(1)}, u32[]{:S(2)}, u32[]{:S(2)}) %all-to-all-start) | async-done | bytes 1048608 | tf_op jit(solution)/shard_map/all_to_all | solution.py:488
  52.5 1.6 %shard_map.98.st0 = f32[4,2048]{1,0:T(4,128)S(1)} custom-call(s32[5]{0:T(128)S(1)} %stack.23.place, bf16[2048,256]{1,0:T(8,128)(2,1)S(1)} %bitcast.7, bf16[2048,128]{1,0:T(8,128)(2,1)S(1)} %get-tuple-element.54.q_rows, bf16[2048,128]{1,0:T(8,128)(2,1)S(1)} %get-tuple-element.55.g_rows, f32[384,512]{1,0:T(8,128)S(1)} %get-tuple-element.56.bias), custom_call_target="tpu_custom_call" | custom-call | flops 2147483648 | bytes 2097152 | tf_op jit(solution)/shard_map/pallas_call | solution.py:132
  54.1 3.0 %collective-permute-start.10 = (f32[4,2048]{1,0:T(4,128)S(1)}, f32[4,2048]{1,0:T(4,128)S(1)}, u32[]{:S(2)}, u32[]{:S(2)}) collective-permute-start(f32[4,2048]{1,0:T(4,128)S(1)} %shard_map.98.st0), channel_id=1, source_target_pairs={{0,16},{8,24},{16,0},{24,8},{1,17},{9,25},{17,1},{25,9},{2,18},{10... | collective-permute-start | bytes 98312 | tf_op jit(solution)/shard_map/ppermute | solution.py:509
  57.1 0.8 collective-permute-start.11
  57.9 0.7 collective-permute-start.9
  58.6 1.7 %collective-permute-done.11.st3 = f32[4,2048]{1,0:T(4,128)S(1)} collective-permute-done((f32[4,2048]{1,0:T(4,128)S(1)}, f32[4,2048]{1,0:T(4,128)S(1)}, u32[]{:S(2)}, u32[]{:S(2)}) %collective-permute-start.11) | collective-permute-done | bytes 32800 | tf_op jit(solution)/shard_map/ppermute | solution.py:509
  60.3 1.6 %collective-permute-done.9.st1 = f32[4,2048]{1,0:T(4,128)S(1)} collective-permute-done((f32[4,2048]{1,0:T(4,128)S(1)}, f32[4,2048]{1,0:T(4,128)S(1)}, u32[]{:S(2)}, u32[]{:S(2)}) %collective-permute-start.9) | collective-permute-done | bytes 32800 | tf_op jit(solution)/shard_map/ppermute | solution.py:509
  61.9 3.8 %shard_map.99 = (bf16[16,128,256]{2,1,0:T(8,128)(2,1)}, bf16[128,512]{1,0:T(8,128)(2,1)}, bf16[128,512]{1,0:T(8,128)(2,1)}, bf16[128,512]{1,0:T(8,128)(2,1)}, bf16[128,512]{1,0:T(8,128)(2,1)}) custom-call(s32[5]{0:T(128)S(1)} %stack.23.place, bf16[2048,256]{1,0:T(8,128)(2,1)S(1)} %bitcast.8, bf16[2048,128]{1,0:T(8,128)(2,1)S(1)} %get-tuple-element.54.q_rows, ...), custom_call_target="tpu_custom_call" | custom-call | flops 5368709120 | bytes 4194304 | tf_op jit(solution)/shard_map/pallas_call | solution.py:132
  65.7 7.6 %collective-permute-done.12.got_kv = bf16[2,2048,128]{2,1,0:T(8,128)(2,1)} collective-permute-done((bf16[2,2048,128]{2,1,0:T(8,128)(2,1)}, bf16[2,2048,128]{2,1,0:T(8,128)(2,1)}, u32[]{:S(2)}, u32[]{:S(2)}) %collective-permute-start.12) | collective-permute-done | bytes 1048608 | tf_op jit(solution)/shard_map/ppermute | solution.py:436
  73.3 11.0 %all-to-all-start.1 = ((bf16[16,128,256]{2,1,0:T(8,128)(2,1)}), bf16[16,128,256]{2,1,0:T(8,128)(2,1)S(1)}, u32[]{:S(2)}, u32[]{:S(2)}) async-start(bf16[16,128,256]{2,1,0:T(8,128)(2,1)} %get-tuple-element.59), calls=%async_computation.1 | async-start | bytes 2097152 | tf_op jit(solution)/shard_map/all_to_all | solution.py:513
  84.3 1.3 %collective-permute-start.13 = (bf16[128,512]{1,0:T(8,128)(2,1)S(1)}, bf16[128,512]{1,0:T(8,128)(2,1)S(1)}, u32[]{:S(2)}, u32[]{:S(2)}) collective-permute-start(bf16[128,512]{1,0:T(8,128)(2,1)S(1)} %copy-done.4), channel_id=1, source_target_pairs={{0,24},{8,0},{16,8},{24,16},{1,25},{9,1},{17,9},{25,17},{2,26},{10... | collective-permute-start | bytes 393224 | tf_op jit(solution)/shard_map/ppermute | solution.py:514
  85.6 0.7 collective-permute-start.15
  86.3 1.9 %collective-permute-done.13.dq1 = bf16[128,512]{1,0:T(8,128)(2,1)S(1)} collective-permute-done((bf16[128,512]{1,0:T(8,128)(2,1)S(1)}, bf16[128,512]{1,0:T(8,128)(2,1)S(1)}, u32[]{:S(2)}, u32[]{:S(2)}) %collective-permute-start.13) | collective-permute-done | bytes 131104 | tf_op jit(solution)/shard_map/ppermute | solution.py:514
  88.2 2.8 %collective-permute-done.14.dq2 = bf16[128,512]{1,0:T(8,128)(2,1)S(1)} collective-permute-done((bf16[128,512]{1,0:T(8,128)(2,1)S(1)}, bf16[128,512]{1,0:T(8,128)(2,1)S(1)}, u32[]{:S(2)}, u32[]{:S(2)}) %collective-permute-start.14) | collective-permute-done | bytes 131104 | tf_op jit(solution)/shard_map/ppermute | solution.py:514
  91.0 1.6 %collective-permute-done.15.dq3 = bf16[128,512]{1,0:T(8,128)(2,1)S(1)} collective-permute-done((bf16[128,512]{1,0:T(8,128)(2,1)S(1)}, bf16[128,512]{1,0:T(8,128)(2,1)S(1)}, u32[]{:S(2)}, u32[]{:S(2)}) %collective-permute-start.15) | collective-permute-done | bytes 131104 | tf_op jit(solution)/shard_map/ppermute | solution.py:514
  92.6 3.8 %shard_map.100 = (bf16[128,1024]{1,0:T(8,128)(2,1)S(1)}, bf16[128,1024]{1,0:T(8,128)(2,1)S(1)}, bf16[128,1024]{1,0:T(8,128)(2,1)S(1)}, bf16[128,1024]{1,0:T(8,128)(2,1)S(1)}, bf16[2,2048,256]{2,1,0:T(8,128)(2,1)S(1)}) custom-call(s32[5]{0:T(128)S(1)} %stack.23.place, bf16[128,512]{1,0:T(8,128)(2,1)S(1)} %copy-done.1, ...), custom_call_target="tpu_custom_call" | custom-call | flops 536870912 | bytes 8388608 | tf_op jit(solution)/shard_map/pallas_call | solution.py:132
  96.4 3.4 %collective-permute-start.18 = (bf16[128,1024]{1,0:T(8,128)(2,1)S(1)}, bf16[128,1024]{1,0:T(8,128)(2,1)S(1)}, u32[]{:S(2)}, u32[]{:S(2)}) collective-permute-start(bf16[128,1024]{1,0:T(8,128)(2,1)S(1)} %get-tuple-element.74), channel_id=1, source_target_pairs={{0,1},{1,0},{2,3},{3,2},{4,5},{5,4},{6,7},{7,6},{8,9},{9,8},{10,11... | collective-permute-start | bytes 786440 | tf_op jit(solution)/shard_map/ppermute | solution.py:433
  99.8 1.1 collective-permute-done.18
  100.9 0.8 add_convert_fusion.1
  101.6 0.2 collective-permute-start.19
  102.0 7.9 %all-to-all-done.1.parts = bf16[16,128,256]{2,1,0:T(8,128)(2,1)S(1)} async-done(((bf16[16,128,256]{2,1,0:T(8,128)(2,1)}), bf16[16,128,256]{2,1,0:T(8,128)(2,1)S(1)}, u32[]{:S(2)}, u32[]{:S(2)}) %all-to-all-start.1) | async-done | bytes 1048608 | tf_op jit(solution)/shard_map/all_to_all | solution.py:513
  109.9 1.3 %shard_map.101 = (bf16[128,128]{1,0:T(8,128)(2,1)}, bf16[128,128]{1,0:T(8,128)(2,1)}, bf16[128,256]{1,0:T(8,128)(2,1)S(1)}) custom-call(s32[5]{0:T(128)S(1)} %stack.23.place, bf16[16,128,256]{2,1,0:T(8,128)(2,1)S(1)} %all-to-all-done.1.parts), custom_call_target="tpu_custom_call" | custom-call | bytes 2097152 | tf_op jit(solution)/shard_map/pallas_call | solution.py:132
  111.3 1.0 shard_map.102
  112.3 2.6 %collective-permute-done.19.queries = bf16[128,1024]{1,0:T(8,128)(2,1)} collective-permute-done((bf16[128,1024]{1,0:T(8,128)(2,1)}, bf16[128,1024]{1,0:T(8,128)(2,1)}, u32[]{:S(2)}, u32[]{:S(2)}) %collective-permute-start.19) | collective-permute-done | bytes 262176 | tf_op jit(solution)/shard_map/ppermute | solution.py:436
  114.9 0.6 collective-permute-done.17.dkv
  115.5 1.4 %shard_map.103 = (f32[128,1024]{1,0:T(8,128)S(1)}, bf16[128,1024]{1,0:T(8,128)(2,1)S(1)}) custom-call(s32[5]{0:T(128)S(1)} %stack.23.place, bf16[128,256]{1,0:T(8,128)(2,1)S(1)} %collective-permute-done.17.dkv, bf16[2,2048,256]{2,1,0:T(8,128)(2,1)S(1)} %get-tuple-element.69.weights, f32[128,1024]{1,0:T(8,128)S(1)} %get-tuple-element.71.own, ...), custom_call_target="tpu_custom_call" | custom-call | flops 134217728 | bytes 2097152 | tf_op jit(solution)/shard_map/pallas_call | solution.py:132
  116.9 5.3 %collective-permute-start.20 = (bf16[128,1024]{1,0:T(8,128)(2,1)S(1)}, bf16[128,1024]{1,0:T(8,128)(2,1)S(1)}, u32[]{:S(2)}, u32[]{:S(2)}) collective-permute-start(bf16[128,1024]{1,0:T(8,128)(2,1)S(1)} %get-tuple-element.76), channel_id=1, source_target_pairs={{0,1},{1,0},{2,3},{3,2},{4,5},{5,4},{6,7},{7,6},{8,9},{9,8},{10,11... | collective-permute-start | bytes 786440 | tf_op jit(solution)/shard_map/ppermute | solution.py:433
  122.2 1.2 collective-permute-done.20
  123.3 0.8 add_convert_fusion
  (22 shorter events, 0.4 us)
Async XLA Ops:
  0.6 4.7 %collective-permute-start.1 = (bf16[128,1024]{1,0:T(8,128)(2,1)}, bf16[128,1024]{1,0:T(8,128)(2,1)S(1)}, u32[]{:S(2)}, u32[]{:S(2)}) collective-permute-start(bf16[128,1024]{1,0:T(8,128)(2,1)} %x0.1), channel_id=1, source_target_pairs={{0,1},{1,0},{2,3},{3,2},{4,5},{5,4},{6,7},{7,6},{8,9},{9,8},{10,11... | collective-permute-start | bytes 786440 | tf_op jit(solution)/shard_map/ppermute | solution.py:433
  4.0 1.7 %collective-permute-start.2 = (bf16[128,1024]{1,0:T(8,128)(2,1)}, bf16[128,1024]{1,0:T(8,128)(2,1)S(1)}, u32[]{:S(2)}, u32[]{:S(2)}) collective-permute-start(bf16[128,1024]{1,0:T(8,128)(2,1)} %g0.1), channel_id=1, source_target_pairs={{0,1},{1,0},{2,3},{3,2},{4,5},{5,4},{6,7},{7,6},{8,9},{9,8},{10,11... | collective-permute-start | bytes 786440 | tf_op jit(solution)/shard_map/ppermute | solution.py:433
  4.1 7.8 %collective-permute-start = (bf16[128,1024]{1,0:T(8,128)(2,1)}, bf16[128,1024]{1,0:T(8,128)(2,1)S(1)}, u32[]{:S(2)}, u32[]{:S(2)}) collective-permute-start(bf16[128,1024]{1,0:T(8,128)(2,1)} %x0.1), channel_id=1, source_target_pairs={{0,2},{2,0},{1,3},{3,1},{4,6},{6,4},{5,7},{7,5},{8,10},{10,8},{9,1... | collective-permute-start | bytes 786440 | tf_op jit(solution)/shard_map/ppermute | solution.py:436
  5.7 0.9 copy-start
  11.9 2.3 %collective-permute-start.3 = (bf16[128,1024]{1,0:T(8,128)(2,1)S(1)}, bf16[128,1024]{1,0:T(8,128)(2,1)S(1)}, u32[]{:S(2)}, u32[]{:S(2)}) collective-permute-start(bf16[128,1024]{1,0:T(8,128)(2,1)S(1)} %collective-permute-done.x2), channel_id=1, source_target_pairs={{0,1},{1,0},{2,3},{3,2},{4,5},{5,4},{6,7},{7,6},{8,9},{9,8},{10,11... | collective-permute-start | bytes 786440 | tf_op jit(solution)/shard_map/ppermute | solution.py:433
  13.0 12.4 %collective-permute-start.4 = (bf16[128,1024]{1,0:T(8,128)(2,1)}, bf16[128,1024]{1,0:T(8,128)(2,1)S(1)}, u32[]{:S(2)}, u32[]{:S(2)}) collective-permute-start(bf16[128,1024]{1,0:T(8,128)(2,1)} %g0.1), channel_id=1, source_target_pairs={{0,2},{2,0},{1,3},{3,1},{4,6},{6,4},{5,7},{7,5},{8,10},{10,8},{9,1... | collective-permute-start | bytes 786440 | tf_op jit(solution)/shard_map/ppermute | solution.py:436
  16.3 36.2 %all-to-all-start = ((bf16[16,128,256]{2,1,0:T(8,128)(2,1)}), bf16[16,128,256]{2,1,0:T(8,128)(2,1)S(1)}, u32[]{:S(2)}, u32[]{:S(2)}) async-start(bf16[16,128,256]{2,1,0:T(8,128)(2,1)} %get-tuple-element.48), calls=%async_computation | async-start | bytes 2097152 | tf_op jit(solution)/shard_map/all_to_all | solution.py:488
  25.4 1.9 %collective-permute-start.5 = (bf16[128,1024]{1,0:T(8,128)(2,1)S(1)}, bf16[128,1024]{1,0:T(8,128)(2,1)S(1)}, u32[]{:S(2)}, u32[]{:S(2)}) collective-permute-start(bf16[128,1024]{1,0:T(8,128)(2,1)S(1)} %collective-permute-done.4.g2), channel_id=1, source_target_pairs={{0,1},{1,0},{2,3},{3,2},{4,5},{5,4},{6,7},{7,6},{8,9},{9,8},{10,11... | collective-permute-start | bytes 786440 | tf_op jit(solution)/shard_map/ppermute | solution.py:433
  30.1 9.1 %collective-permute-start.6 = (bf16[128,1024]{1,0:T(8,128)(2,1)}, bf16[128,1024]{1,0:T(8,128)(2,1)S(1)}, u32[]{:S(2)}, u32[]{:S(2)}) collective-permute-start(bf16[128,1024]{1,0:T(8,128)(2,1)} %shard_map.96.qd0), channel_id=1, source_target_pairs={{0,8},{8,16},{16,24},{24,0},{1,9},{9,17},{17,25},{25,1},{2,10},{10... | collective-permute-start | bytes 786440 | tf_op jit(solution)/shard_map/ppermute | solution.py:489
  31.5 14.5 %collective-permute-start.7 = (bf16[128,1024]{1,0:T(8,128)(2,1)}, bf16[128,1024]{1,0:T(8,128)(2,1)S(1)}, u32[]{:S(2)}, u32[]{:S(2)}) collective-permute-start(bf16[128,1024]{1,0:T(8,128)(2,1)} %shard_map.96.qd0), channel_id=1, source_target_pairs={{0,16},{8,24},{16,0},{24,8},{1,17},{9,25},{17,1},{25,9},{2,18},{10... | collective-permute-start | bytes 786440 | tf_op jit(solution)/shard_map/ppermute | solution.py:489
  34.1 11.9 %collective-permute-start.8 = (bf16[128,1024]{1,0:T(8,128)(2,1)}, bf16[128,1024]{1,0:T(8,128)(2,1)S(1)}, u32[]{:S(2)}, u32[]{:S(2)}) collective-permute-start(bf16[128,1024]{1,0:T(8,128)(2,1)} %shard_map.96.qd0), channel_id=1, source_target_pairs={{0,24},{8,0},{16,8},{24,16},{1,25},{9,1},{17,9},{25,17},{2,26},{10... | collective-permute-start | bytes 786440 | tf_op jit(solution)/shard_map/ppermute | solution.py:489
  48.9 24.4 %collective-permute-start.12 = (bf16[2,2048,128]{2,1,0:T(8,128)(2,1)}, bf16[2,2048,128]{2,1,0:T(8,128)(2,1)}, u32[]{:S(2)}, u32[]{:S(2)}) collective-permute-start(bf16[2,2048,128]{2,1,0:T(8,128)(2,1)} %get-tuple-element.58), channel_id=1, source_target_pairs={{0,2},{2,0},{1,3},{3,1},{4,6},{6,4},{5,7},{7,5},{8,10},{10,8},{9,1... | collective-permute-start | bytes 3145736 | tf_op jit(solution)/shard_map/ppermute | solution.py:436
  54.1 4.5 %collective-permute-start.10 = (f32[4,2048]{1,0:T(4,128)S(1)}, f32[4,2048]{1,0:T(4,128)S(1)}, u32[]{:S(2)}, u32[]{:S(2)}) collective-permute-start(f32[4,2048]{1,0:T(4,128)S(1)} %shard_map.98.st0), channel_id=1, source_target_pairs={{0,16},{8,24},{16,0},{24,8},{1,17},{9,25},{17,1},{25,9},{2,18},{10... | collective-permute-start | bytes 98312 | tf_op jit(solution)/shard_map/ppermute | solution.py:509
  57.1 3.2 %collective-permute-start.11 = (f32[4,2048]{1,0:T(4,128)S(1)}, f32[4,2048]{1,0:T(4,128)S(1)}, u32[]{:S(2)}, u32[]{:S(2)}) collective-permute-start(f32[4,2048]{1,0:T(4,128)S(1)} %shard_map.98.st0), channel_id=1, source_target_pairs={{0,24},{8,0},{16,8},{24,16},{1,25},{9,1},{17,9},{25,17},{2,26},{10... | collective-permute-start | bytes 98312 | tf_op jit(solution)/shard_map/ppermute | solution.py:509
  57.9 4.0 %collective-permute-start.9 = (f32[4,2048]{1,0:T(4,128)S(1)}, f32[4,2048]{1,0:T(4,128)S(1)}, u32[]{:S(2)}, u32[]{:S(2)}) collective-permute-start(f32[4,2048]{1,0:T(4,128)S(1)} %shard_map.98.st0), channel_id=1, source_target_pairs={{0,8},{8,16},{16,24},{24,0},{1,9},{9,17},{17,25},{25,1},{2,10},{10... | collective-permute-start | bytes 98312 | tf_op jit(solution)/shard_map/ppermute | solution.py:509
  65.7 18.6 %copy-start.4 = (bf16[128,512]{1,0:T(8,128)(2,1)S(1)}, bf16[128,512]{1,0:T(8,128)(2,1)}, u32[]{:S(2)}) copy-start(bf16[128,512]{1,0:T(8,128)(2,1)} %get-tuple-element.61) | copy-start | bytes 393220
  65.7 19.9 %copy-start.3 = (bf16[128,512]{1,0:T(8,128)(2,1)S(1)}, bf16[128,512]{1,0:T(8,128)(2,1)}, u32[]{:S(2)}) copy-start(bf16[128,512]{1,0:T(8,128)(2,1)} %get-tuple-element.62) | copy-start | bytes 393220
  65.7 19.9 %copy-start.2 = (bf16[128,512]{1,0:T(8,128)(2,1)S(1)}, bf16[128,512]{1,0:T(8,128)(2,1)}, u32[]{:S(2)}) copy-start(bf16[128,512]{1,0:T(8,128)(2,1)} %get-tuple-element.63) | copy-start | bytes 393220
  65.7 26.9 %copy-start.1 = (bf16[128,512]{1,0:T(8,128)(2,1)S(1)}, bf16[128,512]{1,0:T(8,128)(2,1)}, u32[]{:S(2)}) copy-start(bf16[128,512]{1,0:T(8,128)(2,1)} %get-tuple-element.60.dq0) | copy-start | bytes 393220
  73.3 36.6 %all-to-all-start.1 = ((bf16[16,128,256]{2,1,0:T(8,128)(2,1)}), bf16[16,128,256]{2,1,0:T(8,128)(2,1)S(1)}, u32[]{:S(2)}, u32[]{:S(2)}) async-start(bf16[16,128,256]{2,1,0:T(8,128)(2,1)} %get-tuple-element.59), calls=%async_computation.1 | async-start | bytes 2097152 | tf_op jit(solution)/shard_map/all_to_all | solution.py:513
  84.3 3.9 %collective-permute-start.13 = (bf16[128,512]{1,0:T(8,128)(2,1)S(1)}, bf16[128,512]{1,0:T(8,128)(2,1)S(1)}, u32[]{:S(2)}, u32[]{:S(2)}) collective-permute-start(bf16[128,512]{1,0:T(8,128)(2,1)S(1)} %copy-done.4), channel_id=1, source_target_pairs={{0,24},{8,0},{16,8},{24,16},{1,25},{9,1},{17,9},{25,17},{2,26},{10... | collective-permute-start | bytes 393224 | tf_op jit(solution)/shard_map/ppermute | solution.py:514
  85.6 5.4 %collective-permute-start.14 = (bf16[128,512]{1,0:T(8,128)(2,1)S(1)}, bf16[128,512]{1,0:T(8,128)(2,1)S(1)}, u32[]{:S(2)}, u32[]{:S(2)}) collective-permute-start(bf16[128,512]{1,0:T(8,128)(2,1)S(1)} %copy-done.3), channel_id=1, source_target_pairs={{0,16},{8,24},{16,0},{24,8},{1,17},{9,25},{17,1},{25,9},{2,18},{10... | collective-permute-start | bytes 393224 | tf_op jit(solution)/shard_map/ppermute | solution.py:514
  85.6 7.0 %collective-permute-start.15 = (bf16[128,512]{1,0:T(8,128)(2,1)S(1)}, bf16[128,512]{1,0:T(8,128)(2,1)S(1)}, u32[]{:S(2)}, u32[]{:S(2)}) collective-permute-start(bf16[128,512]{1,0:T(8,128)(2,1)S(1)} %copy-done.2), channel_id=1, source_target_pairs={{0,8},{8,16},{16,24},{24,0},{1,9},{9,17},{17,25},{25,1},{2,10},{10... | collective-permute-start | bytes 393224 | tf_op jit(solution)/shard_map/ppermute | solution.py:514
  96.4 4.5 %collective-permute-start.18 = (bf16[128,1024]{1,0:T(8,128)(2,1)S(1)}, bf16[128,1024]{1,0:T(8,128)(2,1)S(1)}, u32[]{:S(2)}, u32[]{:S(2)}) collective-permute-start(bf16[128,1024]{1,0:T(8,128)(2,1)S(1)} %get-tuple-element.74), channel_id=1, source_target_pairs={{0,1},{1,0},{2,3},{3,2},{4,5},{5,4},{6,7},{7,6},{8,9},{9,8},{10,11... | collective-permute-start | bytes 786440 | tf_op jit(solution)/shard_map/ppermute | solution.py:433
  99.7 2.2 %collective-permute-start.16 = (bf16[128,1024]{1,0:T(8,128)(2,1)S(1)}, bf16[128,1024]{1,0:T(8,128)(2,1)S(1)}, u32[]{:S(2)}, u32[]{:S(2)}) collective-permute-start(bf16[128,1024]{1,0:T(8,128)(2,1)S(1)} %get-tuple-element.66), channel_id=1, source_target_pairs={{0,1},{1,0},{2,3},{3,2},{4,5},{5,4},{6,7},{7,6},{8,9},{9,8},{10,11... | collective-permute-start | bytes 786440 | tf_op jit(solution)/shard_map/ppermute | solution.py:433
  101.6 13.2 %collective-permute-start.19 = (bf16[128,1024]{1,0:T(8,128)(2,1)}, bf16[128,1024]{1,0:T(8,128)(2,1)}, u32[]{:S(2)}, u32[]{:S(2)}) collective-permute-start(bf16[128,1024]{1,0:T(8,128)(2,1)} %add_convert_fusion.1), channel_id=1, source_target_pairs={{0,2},{2,0},{1,3},{3,1},{4,6},{6,4},{5,7},{7,5},{8,10},{10,8},{9,1... | collective-permute-start | bytes 786440 | tf_op jit(solution)/shard_map/ppermute | solution.py:436
  111.3 4.2 %collective-permute-start.17 = (bf16[128,256]{1,0:T(8,128)(2,1)S(1)}, bf16[128,256]{1,0:T(8,128)(2,1)S(1)}, u32[]{:S(2)}, u32[]{:S(2)}) collective-permute-start(bf16[128,256]{1,0:T(8,128)(2,1)S(1)} %get-tuple-element.68.dkv), channel_id=1, source_target_pairs={{0,2},{2,0},{1,3},{3,1},{4,6},{6,4},{5,7},{7,5},{8,10},{10,8},{9,1... | collective-permute-start | bytes 196616 | tf_op jit(solution)/shard_map/ppermute | solution.py:436
  116.9 6.4 %collective-permute-start.20 = (bf16[128,1024]{1,0:T(8,128)(2,1)S(1)}, bf16[128,1024]{1,0:T(8,128)(2,1)S(1)}, u32[]{:S(2)}, u32[]{:S(2)}) collective-permute-start(bf16[128,1024]{1,0:T(8,128)(2,1)S(1)} %get-tuple-element.76), channel_id=1, source_target_pairs={{0,1},{1,0},{2,3},{3,2},{4,5},{5,4},{6,7},{7,6},{8,9},{9,8},{10,11... | collective-permute-start | bytes 786440 | tf_op jit(solution)/shard_map/ppermute | solution.py:433

commit v5 on v4

--- a/solution.py
+++ b/solution.py
@@ -20,6 +20,7 @@
 CHUNK = 2 * BLOCK
 FAR_FLOPS = 10_000_000_000
 STEP = 512
+NEAR_FLOPS = 2 * 128 * 2048 * 512
 STAT_FLOPS = 4 * 2048 * 2048 * 128
 GRAD_FLOPS = 10 * 2048 * 2048 * 128
 VMEM_LIMIT = 20 * 1024 * 1024
@@ -92,14 +93,17 @@
             + matmul(x3[...], weight[other, :])
         ).astype(BF16)
 
-    kv_buf[:, :HEAD] = product(wk, 0, 128)
-    kv_buf[:, HEAD:] = product(wv, 128, 256)
-    copies = [pltpu.make_async_copy(kv_buf, kv.at[i], sems.at[i]) for i in range(16)]
+    pair = jnp.concatenate([product(wk, 0, 128), product(wv, 128, 256)], axis=1)
+    for i in range(4):
+        kv_buf[i] = pair
+    copies = [
+        pltpu.make_async_copy(kv_buf, kv.at[pl.ds(4 * i, 4)], sems.at[i]) for i in range(4)
+    ]
     for copy in copies:
         copy.start()
     q_buf[...] = product(wq, 256, 768)
-    copies.append(pltpu.make_async_copy(q_buf, q, sems.at[16]))
-    copies[16].start()
+    copies.append(pltpu.make_async_copy(q_buf, q, sems.at[4]))
+    copies[4].start()
     for copy in copies:
         copy.wait()
 
@@ -375,27 +379,37 @@
     return pl.ds(pl.multiple_of(first * 1024, 1024), 1024)
 
 
-def query_back_kernel(
-    place, dq0, dq1, dq2, dq3, wq, wk, wv, got_kv, far0, far1, near1, near0, out_kv, held, sems
-):
+def query_far_kernel(place, dq0, dq1, dq2, dq3, wq, far0, far1, total, held, sems):
     copies = [
         pltpu.make_async_copy(wq.at[feature_rows(place, flip), :], held.at[i], sems.at[i])
-        for i, flip in enumerate((3, 2, 1, 0))
+        for i, flip in enumerate((3, 2))
+    ]
+    for copy in copies:
+        copy.start()
+    parts = [d[...].astype(F32) for d in (dq0, dq1, dq2, dq3)]
+    total[...] = (parts[0] + parts[1] + parts[2] + parts[3]).astype(BF16)
+    for copy, block, out in zip(copies, (0, 1), (far0, far1)):
+        copy.wait()
+        out[...] = contract_last(total[...], held[block]).astype(out.dtype)
+
+
+def query_near_kernel(place, total, wq, wk, wv, got_kv, near1, near0, out_kv, held, sems):
+    copies = [
+        pltpu.make_async_copy(wq.at[feature_rows(place, flip), :], held.at[i], sems.at[i])
+        for i, flip in enumerate((1, 0))
     ]
     rows = pl.ds(pl.multiple_of(place[3] * PAIR, PAIR), PAIR)
     sources = (wk.at[rows, :], wv.at[rows, :], got_kv.at[0], got_kv.at[1])
     for i, source in enumerate(sources):
         low = (i % 2) * HEAD
         target = out_kv.at[i // 2, :, low : low + HEAD]
-        copies.append(pltpu.make_async_copy(source, target, sems.at[4 + i]))
+        copies.append(pltpu.make_async_copy(source, target, sems.at[2 + i]))
     for copy in copies:
         copy.start()
-    parts = [d[...].astype(F32) for d in (dq0, dq1, dq2, dq3)]
-    total = (parts[0] + parts[1] + parts[2] + parts[3]).astype(BF16)
-    for i, out in enumerate((far0, far1, near1, near0)):
-        copies[i].wait()
-        out[...] = contract_last(total, held[i]).astype(out.dtype)
-    for copy in copies[4:]:
+    for copy, block, out in zip(copies, (0, 1), (near1, near0)):
+        copy.wait()
+        out[...] = contract_last(total[...], held[block]).astype(out.dtype)
+    for copy in copies[2:]:
         copy.wait()
 
 
@@ -409,18 +423,16 @@
     dkv[:, HEAD:] = dv[...]
 
 
-def key_near_kernel(place, dkv, weights, queries, own, other):
+def key_near_kernel(place, dkv, weights, queries, far_queries, own, other):
     mine, siblings = core_halves(place[4])
-    own[...] = queries[...].astype(F32) + contract_last(dkv[...], weights[0, mine, :])
+    total = queries[...].astype(F32) + far_queries[...].astype(F32)
+    own[...] = total + contract_last(dkv[...], weights[0, mine, :])
     other[...] = contract_last(dkv[...], weights[0, siblings, :])
 
 
-def key_far_kernel(place, dkv, weights, own, other, queries, own_out, other_out):
-    mine, siblings = core_halves(place[4])
-    other_out[...] = (other[...] + contract_last(dkv[...], weights[1, siblings, :])).astype(BF16)
-    own_out[...] = (
-        own[...] + queries[...].astype(F32) + contract_last(dkv[...], weights[1, mine, :])
-    )
+def key_far_kernel(flip, place, dkv, weights, before, out):
+    rows = core_halves(place[4])[flip]
+    out[...] = (before[...] + contract_last(dkv[...], weights[1, rows, :])).astype(out.dtype)
 
 
 def local(inputs, out_grad, w_query, key_weight, value_weight, w_output, times):
@@ -461,9 +473,9 @@
         (place, x2, x3, far_q, far_k, far_v, x_half),
         [shape(16, BLOCK, 2 * HEAD), shape(BLOCK, ROWS)],
         [
-            pltpu.VMEM((BLOCK, 2 * HEAD), BF16),
+            pltpu.VMEM((4, BLOCK, 2 * HEAD), BF16),
             pltpu.VMEM((BLOCK, ROWS), BF16),
-            pltpu.SemaphoreType.DMA((17,)),
+            pltpu.SemaphoreType.DMA((5,)),
         ],
         hbm_outs=(0, 1),
         flops=2 * 128 * 2048 * 768,
@@ -516,16 +528,27 @@
     def add(*values):
         return sum(v.astype(F32) for v in values)
 
-    far0, far1, near1, near0, held_kv = whole_call(
-        query_back_kernel,
-        (place, *dq_parts, w_query, key_weight, value_weight, got_kv),
-        [shape(BLOCK, 1024)] * 4 + [shape(2, PAIR, 2 * HEAD)],
-        [pltpu.VMEM((4, 1024, ROWS), BF16), pltpu.SemaphoreType.DMA((8,))],
-        hbm=(5, 6, 7, 8),
-        flops=2 * 128 * 4096 * 512,
-        traffic=8 << 20,
-    )
-    far_queries = to_xl(add(far1, to_core(far0)).astype(BF16))
+    far0, far1, dq = whole_call(
+        query_far_kernel,
+        (place, *dq_parts, w_query),
+        [shape(BLOCK, 1024)] * 2 + [shape(BLOCK, ROWS)],
+        [pltpu.VMEM((2, 1024, ROWS), BF16), pltpu.SemaphoreType.DMA((2,))],
+        hbm=(5,),
+        flops=2 * 128 * 2048 * 512,
+        traffic=2 << 20,
+    )
+    far_sum = add(far1, to_core(far0)).astype(BF16)
+    far_sum, dq = lax.optimization_barrier((far_sum, dq))
+    far_queries = to_xl(far_sum)
+    near1, near0, held_kv = whole_call(
+        query_near_kernel,
+        (place, dq, w_query, key_weight, value_weight, got_kv),
+        [shape(BLOCK, 1024)] * 2 + [shape(2, PAIR, 2 * HEAD)],
+        [pltpu.VMEM((2, 1024, ROWS), BF16), pltpu.SemaphoreType.DMA((6,))],
+        hbm=(2, 3, 4, 5),
+        flops=NEAR_FLOPS,
+        traffic=4 << 20,
+    )
     near_queries = add(near0, to_core(near1)).astype(BF16)
     dkv_parts, near_queries = lax.optimization_barrier((dkv_parts, near_queries))
 
@@ -539,19 +562,27 @@
     halves = [shape(BLOCK, 1024, kind=F32)] * 2
     own_half, other_half = whole_call(
         key_near_kernel,
-        (place, dkv_own, held_kv, near_queries),
+        (place, dkv_own, held_kv, near_queries, far_queries),
         halves,
         flops=2 * 128 * 256 * 2048,
         traffic=2 << 20,
     )
-    own_half, other_half = whole_call(
-        key_far_kernel,
-        (place, dkv_far, held_kv, own_half, other_half, far_queries),
-        [halves[0], shape(BLOCK, 1024)],
-        flops=2 * 128 * 256 * 2048,
-        traffic=2 << 20,
-    )
-    input_grad = add(own_half, to_core(other_half)).astype(BF16)
+    (other_half,) = whole_call(
+        functools.partial(key_far_kernel, 1),
+        (place, dkv_far, held_kv, other_half),
+        [shape(BLOCK, 1024)],
+        flops=2 * 128 * 256 * 1024,
+        traffic=1 << 20,
+    )
+    got_half = to_core(other_half)
+    (own_half,) = whole_call(
+        functools.partial(key_far_kernel, 0),
+        (place, dkv_far, held_kv, own_half),
+        halves[:1],
+        flops=2 * 128 * 256 * 1024,
+        traffic=1 << 20,
+    )
+    input_grad = add(own_half, got_half).astype(BF16)
     return input_grad, dk, dv
 
 

time: 125 us -> 124 us (level)
  waiting for transfers between devices: 48.5 us -> 45.7 us
  Pallas kernels: 26 us -> 28.4 us
    all_to_all x1, waiting for transfers between devices: 7.95 us -> 4.57 us  [local(): dkv_parts = lax.all_to_all(dkv, ('z', 'xh'), 0, 0, tiled=True)]
    pallas_call x10 -> x12, Pallas kernels: 26 us -> 28.4 us  [whole_call(): pl.pallas_call(kernel, in_specs=in_specs, out_specs=[pl.BlockSpec(memory_...]
  transfers between devices with their start and end apart: 23 -> 23, of which waited for: 18 -> 18; matrix products, arithmetic and copies ran while one was open for 1% -> 1% of each run, Pallas kernels for 20% -> 22%
where the time goes in v5:
time: 124 us; the launch traced here: 123 us
  starting transfers between devices  45.7 us (37%)
  waiting for transfers between devices  45.7 us (37%)
  Pallas kernels  28.4 us (23%)
  other arithmetic  1.6 us (1%)
    pallas_call x12, Pallas kernels, whole_call(): pl.pallas_call(kernel, in_specs=in_specs, out_specs=[pl.BlockSpec(memory_...  28.4 us
    ppermute x7, starting transfers between devices, to_core(): return lax.ppermute(value, 'core', swap)  13.6 us
    ppermute x5, waiting for transfers between devices, to_xl(): return lax.ppermute(value, 'xl', swap)  11.8 us
    all_to_all x1, starting transfers between devices, local(): dkv_parts = lax.all_to_all(dkv, ('z', 'xh'), 0, 0, tiled=True)  11 us
    ppermute x3, waiting for transfers between devices, local(): lax.ppermute(qd_own, 'y', shifted(4, s))  10.8 us
    all_to_all x1, starting transfers between devices, local(): lax.all_to_all(kv_own, ('z', 'xh'), 0, 0, tiled=True)  9.03 us
    ppermute x7, waiting for transfers between devices, to_core(): return lax.ppermute(value, 'core', swap)  6.23 us
    ppermute x3, waiting for transfers between devices, local(): lax.ppermute(dqs[s], 'y', shifted(4, -s))  5.83 us
  transfers between devices with their start and end apart: 23, of which 18 were waited for; matrix products, arithmetic and copies ran while one was open for 1% of the time, Pallas kernels for 22%

profile of v5, /device:TPU:1, one launch (start us, length us, event | category | flops | bytes accessed | tf_op | source)
XLA Modules:
  0.0 123.3 jit_solution(5538480364166346983)
XLA Ops:
  0.6 3.3 %collective-permute-start.1 = (bf16[128,1024]{1,0:T(8,128)(2,1)}, bf16[128,1024]{1,0:T(8,128)(2,1)S(1)}, u32[]{:S(2)}, u32[]{:S(2)}) collective-permute-start(bf16[128,1024]{1,0:T(8,128)(2,1)} %x0.1), channel_id=1, source_target_pairs={{0,1},{1,0},{2,3},{3,2},{4,5},{5,4},{6,7},{7,6},{8,9},{9,8},{10,11... | collective-permute-start | bytes 786440 | tf_op jit(solution)/shard_map/ppermute | solution.py:445
  4.1 1.2 collective-permute-done.1.x1
  5.7 0.9 copy-done
  6.7 5.2 %shard_map.94 = (f32[128,768]{1,0:T(8,128)S(1)}, f32[128,512]{1,0:T(8,128)}, bf16[2048,512]{1,0:T(8,128)(2,1)S(1)}, bf16[2048,128]{1,0:T(8,128)(2,1)S(1)}, bf16[...) custom-call(s32[5]{0:T(128)S(1)} %stack.23.place, bf16[128,1024]{1,0:T(8,128)(2,1)S(1)} %copy-done, ...), custom_call_target="tpu_custom_call" | custom-call | flops 671088640 | bytes 10485760 | tf_op jit(solution)/shard_map/pallas_call | solution.py:136
  11.9 1.1 collective-permute-start.3
  13.0 1.2 collective-permute-done.3.x3
  14.2 2.1 %shard_map.95 = (bf16[16,128,256]{2,1,0:T(8,128)(2,1)}, bf16[128,512]{1,0:T(8,128)(2,1)}) custom-call(s32[5]{0:T(128)S(1)} %stack.23.place, bf16[128,1024]{1,0:T(8,128)(2,1)S(1)} %collective-permute-done.x2, bf16[128,1024]{1,0:T(8,128)(2,1)S(1)} %collective-permute-done.3.x3, bf16[2048,512]{1,0:T(8,128)(2,1)S(1)} %get-tuple-element.45.wq, ...), custom_call_target="tpu_custom_call" | custom-call | flops 402653184 | bytes 4194304 | tf_op jit(solution)/shard_map/pallas_call | solution.py:136
  16.2 9.0 %all-to-all-start = ((bf16[16,128,256]{2,1,0:T(8,128)(2,1)}), bf16[16,128,256]{2,1,0:T(8,128)(2,1)S(1)}, u32[]{:S(2)}, u32[]{:S(2)}) async-start(bf16[16,128,256]{2,1,0:T(8,128)(2,1)} %get-tuple-element.49), calls=%async_computation | async-start | bytes 2097152 | tf_op jit(solution)/shard_map/all_to_all | solution.py:500
  25.3 0.7 collective-permute-start.5
  26.0 1.2 collective-permute-done.5.g3
  27.2 2.9 %shard_map.96.qd0 = bf16[128,1024]{1,0:T(8,128)(2,1)} custom-call(s32[5]{0:T(128)S(1)} %stack.23.place, bf16[128,1024]{1,0:T(8,128)(2,1)S(1)} %collective-permute-done.4.g2, bf16[128,1024]{1,0:T(8,128)(2,1)S(1)} %collective-permute-done.5.g3, bf16[512,2048]{1,0:T(8,128)(2,1)S(1)} %get-tuple-element.52.wo, f32[128,512]{1,0:T(8,128)} %get-tuple-element.53.g_half, ...), custom_call_target="tpu_custom_call" | custom-call | flops 10000000000 | bytes 3145728 | tf_op jit(solution)/shard_map/pallas_call | solution.py:136
  30.0 1.4 %collective-permute-start.6 = (bf16[128,1024]{1,0:T(8,128)(2,1)}, bf16[128,1024]{1,0:T(8,128)(2,1)S(1)}, u32[]{:S(2)}, u32[]{:S(2)}) collective-permute-start(bf16[128,1024]{1,0:T(8,128)(2,1)} %shard_map.96.qd0), channel_id=1, source_target_pairs={{0,8},{8,16},{16,24},{24,0},{1,9},{9,17},{17,25},{25,1},{2,10},{10... | collective-permute-start | bytes 786440 | tf_op jit(solution)/shard_map/ppermute | solution.py:501
  31.4 2.6 %collective-permute-start.7 = (bf16[128,1024]{1,0:T(8,128)(2,1)}, bf16[128,1024]{1,0:T(8,128)(2,1)S(1)}, u32[]{:S(2)}, u32[]{:S(2)}) collective-permute-start(bf16[128,1024]{1,0:T(8,128)(2,1)} %shard_map.96.qd0), channel_id=1, source_target_pairs={{0,16},{8,24},{16,0},{24,8},{1,17},{9,25},{17,1},{25,9},{2,18},{10... | collective-permute-start | bytes 786440 | tf_op jit(solution)/shard_map/ppermute | solution.py:501
  34.0 1.1 collective-permute-start.8
  35.1 4.1 %collective-permute-done.6.qd1 = bf16[128,1024]{1,0:T(8,128)(2,1)S(1)} collective-permute-done((bf16[128,1024]{1,0:T(8,128)(2,1)}, bf16[128,1024]{1,0:T(8,128)(2,1)S(1)}, u32[]{:S(2)}, u32[]{:S(2)}) %collective-permute-start.6) | collective-permute-done | bytes 262176 | tf_op jit(solution)/shard_map/ppermute | solution.py:501
  39.2 6.7 %collective-permute-done.7.qd2 = bf16[128,1024]{1,0:T(8,128)(2,1)S(1)} collective-permute-done((bf16[128,1024]{1,0:T(8,128)(2,1)}, bf16[128,1024]{1,0:T(8,128)(2,1)S(1)}, u32[]{:S(2)}, u32[]{:S(2)}) %collective-permute-start.7) | collective-permute-done | bytes 262176 | tf_op jit(solution)/shard_map/ppermute | solution.py:501
  45.9 2.9 %shard_map.97 = (bf16[2048,128]{1,0:T(8,128)(2,1)S(1)}, bf16[2048,128]{1,0:T(8,128)(2,1)S(1)}, f32[384,512]{1,0:T(8,128)S(1)}, bf16[2,2048,128]{2,1,0:T(8,128)(2,1)}) custom-call(s32[5]{0:T(128)S(1)} %stack.23.place, s32[64,128]{1,0:T(8,128)} %bitcast.9, bf16[128,1024]{1,0:T(8,128)(2,1)} %shard_map.96.qd0, bf16[128,1024]{1,0:T(8,128)(2,1)S(1)} %collective-permute-done.6.qd1, ...), custom_call_target="tpu_custom_call" | custom-call | bytes 2097152 | tf_op jit(solution)/shard_map/pallas_call | solution.py:136
  48.8 0.4 collective-permute-start.12
  49.2 3.2 %all-to-all-done = bf16[16,128,256]{2,1,0:T(8,128)(2,1)S(1)} async-done(((bf16[16,128,256]{2,1,0:T(8,128)(2,1)}), bf16[16,128,256]{2,1,0:T(8,128)(2,1)S(1)}, u32[]{:S(2)}, u32[]{:S(2)}) %all-to-all-start) | async-done | bytes 1048608 | tf_op jit(solution)/shard_map/all_to_all | solution.py:500
  52.4 1.6 %shard_map.98.st0 = f32[4,2048]{1,0:T(4,128)S(1)} custom-call(s32[5]{0:T(128)S(1)} %stack.23.place, bf16[2048,256]{1,0:T(8,128)(2,1)S(1)} %bitcast.7, bf16[2048,128]{1,0:T(8,128)(2,1)S(1)} %get-tuple-element.55.q_rows, bf16[2048,128]{1,0:T(8,128)(2,1)S(1)} %get-tuple-element.56.g_rows, f32[384,512]{1,0:T(8,128)S(1)} %get-tuple-element.57.bias), custom_call_target="tpu_custom_call" | custom-call | flops 2147483648 | bytes 2097152 | tf_op jit(solution)/shard_map/pallas_call | solution.py:136
  54.0 3.0 %collective-permute-start.10 = (f32[4,2048]{1,0:T(4,128)S(1)}, f32[4,2048]{1,0:T(4,128)S(1)}, u32[]{:S(2)}, u32[]{:S(2)}) collective-permute-start(f32[4,2048]{1,0:T(4,128)S(1)} %shard_map.98.st0), channel_id=1, source_target_pairs={{0,16},{8,24},{16,0},{24,8},{1,17},{9,25},{17,1},{25,9},{2,18},{10... | collective-permute-start | bytes 98312 | tf_op jit(solution)/shard_map/ppermute | solution.py:521
  57.0 0.8 collective-permute-start.11
  57.8 0.7 collective-permute-start.9
  58.5 1.7 %collective-permute-done.11.st3 = f32[4,2048]{1,0:T(4,128)S(1)} collective-permute-done((f32[4,2048]{1,0:T(4,128)S(1)}, f32[4,2048]{1,0:T(4,128)S(1)}, u32[]{:S(2)}, u32[]{:S(2)}) %collective-permute-start.11) | collective-permute-done | bytes 32800 | tf_op jit(solution)/shard_map/ppermute | solution.py:521
  60.2 1.6 %collective-permute-done.9.st1 = f32[4,2048]{1,0:T(4,128)S(1)} collective-permute-done((f32[4,2048]{1,0:T(4,128)S(1)}, f32[4,2048]{1,0:T(4,128)S(1)}, u32[]{:S(2)}, u32[]{:S(2)}) %collective-permute-start.9) | collective-permute-done | bytes 32800 | tf_op jit(solution)/shard_map/ppermute | solution.py:521
  61.8 3.8 %shard_map.99 = (bf16[16,128,256]{2,1,0:T(8,128)(2,1)}, bf16[128,512]{1,0:T(8,128)(2,1)}, bf16[128,512]{1,0:T(8,128)(2,1)}, bf16[128,512]{1,0:T(8,128)(2,1)}, bf16[128,512]{1,0:T(8,128)(2,1)}) custom-call(s32[5]{0:T(128)S(1)} %stack.23.place, bf16[2048,256]{1,0:T(8,128)(2,1)S(1)} %bitcast.8, bf16[2048,128]{1,0:T(8,128)(2,1)S(1)} %get-tuple-element.55.q_rows, ...), custom_call_target="tpu_custom_call" | custom-call | flops 5368709120 | bytes 4194304 | tf_op jit(solution)/shard_map/pallas_call | solution.py:136
  65.6 7.6 %collective-permute-done.12.got_kv = bf16[2,2048,128]{2,1,0:T(8,128)(2,1)} collective-permute-done((bf16[2,2048,128]{2,1,0:T(8,128)(2,1)}, bf16[2,2048,128]{2,1,0:T(8,128)(2,1)}, u32[]{:S(2)}, u32[]{:S(2)}) %collective-permute-start.12) | collective-permute-done | bytes 1048608 | tf_op jit(solution)/shard_map/ppermute | solution.py:448
  73.2 11.0 %all-to-all-start.1 = ((bf16[16,128,256]{2,1,0:T(8,128)(2,1)}), bf16[16,128,256]{2,1,0:T(8,128)(2,1)S(1)}, u32[]{:S(2)}, u32[]{:S(2)}) async-start(bf16[16,128,256]{2,1,0:T(8,128)(2,1)} %get-tuple-element.60), calls=%async_computation.1 | async-start | bytes 2097152 | tf_op jit(solution)/shard_map/all_to_all | solution.py:525
  84.2 1.3 %collective-permute-start.13 = (bf16[128,512]{1,0:T(8,128)(2,1)S(1)}, bf16[128,512]{1,0:T(8,128)(2,1)S(1)}, u32[]{:S(2)}, u32[]{:S(2)}) collective-permute-start(bf16[128,512]{1,0:T(8,128)(2,1)S(1)} %copy-done.4), channel_id=1, source_target_pairs={{0,24},{8,0},{16,8},{24,16},{1,25},{9,1},{17,9},{25,17},{2,26},{10... | collective-permute-start | bytes 393224 | tf_op jit(solution)/shard_map/ppermute | solution.py:526
  85.5 0.7 collective-permute-start.15
  86.2 1.9 %collective-permute-done.13.dq1 = bf16[128,512]{1,0:T(8,128)(2,1)S(1)} collective-permute-done((bf16[128,512]{1,0:T(8,128)(2,1)S(1)}, bf16[128,512]{1,0:T(8,128)(2,1)S(1)}, u32[]{:S(2)}, u32[]{:S(2)}) %collective-permute-start.13) | collective-permute-done | bytes 131104 | tf_op jit(solution)/shard_map/ppermute | solution.py:526
  88.1 2.8 %collective-permute-done.14.dq2 = bf16[128,512]{1,0:T(8,128)(2,1)S(1)} collective-permute-done((bf16[128,512]{1,0:T(8,128)(2,1)S(1)}, bf16[128,512]{1,0:T(8,128)(2,1)S(1)}, u32[]{:S(2)}, u32[]{:S(2)}) %collective-permute-start.14) | collective-permute-done | bytes 131104 | tf_op jit(solution)/shard_map/ppermute | solution.py:526
  90.9 1.1 collective-permute-done.15.dq3
  92.0 2.7 %shard_map.100 = (bf16[128,1024]{1,0:T(8,128)(2,1)S(1)}, bf16[128,1024]{1,0:T(8,128)(2,1)S(1)}, bf16[128,512]{1,0:T(8,128)(2,1)S(1)}) custom-call(s32[5]{0:T(128)S(1)} %stack.23.place, bf16[128,512]{1,0:T(8,128)(2,1)S(1)} %copy-done.1, bf16[128,512]{1,0:T(8,128)(2,1)S(1)} %collective-permute-done.13.dq1, bf16[128,512]{1,0:T(8,128)(2,1)S(1)} %collective-permute-done.14.dq2, ...), custom_call_target="tpu_custom_call" | custom-call | flops 268435456 | bytes 2097152 | tf_op jit(solution)/shard_map/pallas_call | solution.py:136
  94.7 4.1 %collective-permute-start.16 = (bf16[128,1024]{1,0:T(8,128)(2,1)S(1)}, bf16[128,1024]{1,0:T(8,128)(2,1)S(1)}, u32[]{:S(2)}, u32[]{:S(2)}) collective-permute-start(bf16[128,1024]{1,0:T(8,128)(2,1)S(1)} %get-tuple-element.66), channel_id=1, source_target_pairs={{0,1},{1,0},{2,3},{3,2},{4,5},{5,4},{6,7},{7,6},{8,9},{9,8},{10,11... | collective-permute-start | bytes 786440 | tf_op jit(solution)/shard_map/ppermute | solution.py:445
  98.8 1.2 collective-permute-done.16
  100.0 0.8 add_convert_fusion.2
  100.8 2.8 %shard_map.101 = (bf16[128,1024]{1,0:T(8,128)(2,1)S(1)}, bf16[128,1024]{1,0:T(8,128)(2,1)S(1)}, bf16[2,2048,256]{2,1,0:T(8,128)(2,1)S(1)}) custom-call(s32[5]{0:T(128)S(1)} %stack.23.place, bf16[128,512]{1,0:T(8,128)(2,1)S(1)} %get-tuple-element.68.total, bf16[4096,512]{1,0:T(8,128)(2,1)} %wq.5, bf16[4096,128]{1,0:T(8,128)(2,1)} %wk.5, ...), custom_call_target="tpu_custom_call" | custom-call | flops 268435456 | bytes 4194304 | tf_op jit(solution)/shard_map/pallas_call | solution.py:136
  103.6 0.5 collective-permute-start.17
  104.3 0.9 collective-permute-done.17
  105.3 4.6 %all-to-all-done.1.parts = bf16[16,128,256]{2,1,0:T(8,128)(2,1)S(1)} async-done(((bf16[16,128,256]{2,1,0:T(8,128)(2,1)}), bf16[16,128,256]{2,1,0:T(8,128)(2,1)S(1)}, u32[]{:S(2)}, u32[]{:S(2)}) %all-to-all-start.1) | async-done | bytes 1048608 | tf_op jit(solution)/shard_map/all_to_all | solution.py:525
  109.8 1.3 %shard_map.102 = (bf16[128,128]{1,0:T(8,128)(2,1)}, bf16[128,128]{1,0:T(8,128)(2,1)}, bf16[128,256]{1,0:T(8,128)(2,1)S(1)}) custom-call(s32[5]{0:T(128)S(1)} %stack.23.place, bf16[16,128,256]{2,1,0:T(8,128)(2,1)S(1)} %all-to-all-done.1.parts), custom_call_target="tpu_custom_call" | custom-call | bytes 2097152 | tf_op jit(solution)/shard_map/pallas_call | solution.py:136
  111.2 4.1 %collective-permute-done.19.far_queries = bf16[128,1024]{1,0:T(8,128)(2,1)} collective-permute-done((bf16[128,1024]{1,0:T(8,128)(2,1)}, bf16[128,1024]{1,0:T(8,128)(2,1)}, u32[]{:S(2)}, u32[]{:S(2)}) %collective-permute-start.19) | collective-permute-done | bytes 262176 | tf_op jit(solution)/shard_map/ppermute | solution.py:448
  115.3 1.5 %shard_map.103 = (f32[128,1024]{1,0:T(8,128)S(1)}, f32[128,1024]{1,0:T(8,128)S(1)}) custom-call(s32[5]{0:T(128)S(1)} %stack.23.place, bf16[128,256]{1,0:T(8,128)(2,1)S(1)} %get-tuple-element.73.dkv, bf16[2,2048,256]{2,1,0:T(8,128)(2,1)S(1)} %get-tuple-element.74.weights, bf16[128,1024]{1,0:T(8,128)(2,1)S(1)} %add_convert_fusion.1.queries, ...), custom_call_target="tpu_custom_call" | custom-call | flops 134217728 | bytes 2097152 | tf_op jit(solution)/shard_map/pallas_call | solution.py:136
  116.8 0.8 shard_map.105
  117.6 3.8 %collective-permute-start.20 = (bf16[128,1024]{1,0:T(8,128)(2,1)S(1)}, bf16[128,1024]{1,0:T(8,128)(2,1)S(1)}, u32[]{:S(2)}, u32[]{:S(2)}) collective-permute-start(bf16[128,1024]{1,0:T(8,128)(2,1)S(1)} %shard_map.105), channel_id=1, source_target_pairs={{0,1},{1,0},{2,3},{3,2},{4,5},{5,4},{6,7},{7,6},{8,9},{9,8},{10,11... | collective-permute-start | bytes 786440 | tf_op jit(solution)/shard_map/ppermute | solution.py:445
  121.4 0.8 shard_map.104
  122.6 0.8 add_convert_fusion
  (24 shorter events, 1.3 us)
Async XLA Ops:
  0.6 4.7 %collective-permute-start.1 = (bf16[128,1024]{1,0:T(8,128)(2,1)}, bf16[128,1024]{1,0:T(8,128)(2,1)S(1)}, u32[]{:S(2)}, u32[]{:S(2)}) collective-permute-start(bf16[128,1024]{1,0:T(8,128)(2,1)} %x0.1), channel_id=1, source_target_pairs={{0,1},{1,0},{2,3},{3,2},{4,5},{5,4},{6,7},{7,6},{8,9},{9,8},{10,11... | collective-permute-start | bytes 786440 | tf_op jit(solution)/shard_map/ppermute | solution.py:445
  4.0 1.7 %collective-permute-start.2 = (bf16[128,1024]{1,0:T(8,128)(2,1)}, bf16[128,1024]{1,0:T(8,128)(2,1)S(1)}, u32[]{:S(2)}, u32[]{:S(2)}) collective-permute-start(bf16[128,1024]{1,0:T(8,128)(2,1)} %g0.1), channel_id=1, source_target_pairs={{0,1},{1,0},{2,3},{3,2},{4,5},{5,4},{6,7},{7,6},{8,9},{9,8},{10,11... | collective-permute-start | bytes 786440 | tf_op jit(solution)/shard_map/ppermute | solution.py:445
  4.1 7.8 %collective-permute-start = (bf16[128,1024]{1,0:T(8,128)(2,1)}, bf16[128,1024]{1,0:T(8,128)(2,1)S(1)}, u32[]{:S(2)}, u32[]{:S(2)}) collective-permute-start(bf16[128,1024]{1,0:T(8,128)(2,1)} %x0.1), channel_id=1, source_target_pairs={{0,2},{2,0},{1,3},{3,1},{4,6},{6,4},{5,7},{7,5},{8,10},{10,8},{9,1... | collective-permute-start | bytes 786440 | tf_op jit(solution)/shard_map/ppermute | solution.py:448
  5.7 0.9 copy-start
  11.9 2.3 %collective-permute-start.3 = (bf16[128,1024]{1,0:T(8,128)(2,1)S(1)}, bf16[128,1024]{1,0:T(8,128)(2,1)S(1)}, u32[]{:S(2)}, u32[]{:S(2)}) collective-permute-start(bf16[128,1024]{1,0:T(8,128)(2,1)S(1)} %collective-permute-done.x2), channel_id=1, source_target_pairs={{0,1},{1,0},{2,3},{3,2},{4,5},{5,4},{6,7},{7,6},{8,9},{9,8},{10,11... | collective-permute-start | bytes 786440 | tf_op jit(solution)/shard_map/ppermute | solution.py:445
  13.0 12.3 %collective-permute-start.4 = (bf16[128,1024]{1,0:T(8,128)(2,1)}, bf16[128,1024]{1,0:T(8,128)(2,1)S(1)}, u32[]{:S(2)}, u32[]{:S(2)}) collective-permute-start(bf16[128,1024]{1,0:T(8,128)(2,1)} %g0.1), channel_id=1, source_target_pairs={{0,2},{2,0},{1,3},{3,1},{4,6},{6,4},{5,7},{7,5},{8,10},{10,8},{9,1... | collective-permute-start | bytes 786440 | tf_op jit(solution)/shard_map/ppermute | solution.py:448
  16.2 36.2 %all-to-all-start = ((bf16[16,128,256]{2,1,0:T(8,128)(2,1)}), bf16[16,128,256]{2,1,0:T(8,128)(2,1)S(1)}, u32[]{:S(2)}, u32[]{:S(2)}) async-start(bf16[16,128,256]{2,1,0:T(8,128)(2,1)} %get-tuple-element.49), calls=%async_computation | async-start | bytes 2097152 | tf_op jit(solution)/shard_map/all_to_all | solution.py:500
  25.3 1.9 %collective-permute-start.5 = (bf16[128,1024]{1,0:T(8,128)(2,1)S(1)}, bf16[128,1024]{1,0:T(8,128)(2,1)S(1)}, u32[]{:S(2)}, u32[]{:S(2)}) collective-permute-start(bf16[128,1024]{1,0:T(8,128)(2,1)S(1)} %collective-permute-done.4.g2), channel_id=1, source_target_pairs={{0,1},{1,0},{2,3},{3,2},{4,5},{5,4},{6,7},{7,6},{8,9},{9,8},{10,11... | collective-permute-start | bytes 786440 | tf_op jit(solution)/shard_map/ppermute | solution.py:445
  30.0 9.1 %collective-permute-start.6 = (bf16[128,1024]{1,0:T(8,128)(2,1)}, bf16[128,1024]{1,0:T(8,128)(2,1)S(1)}, u32[]{:S(2)}, u32[]{:S(2)}) collective-permute-start(bf16[128,1024]{1,0:T(8,128)(2,1)} %shard_map.96.qd0), channel_id=1, source_target_pairs={{0,8},{8,16},{16,24},{24,0},{1,9},{9,17},{17,25},{25,1},{2,10},{10... | collective-permute-start | bytes 786440 | tf_op jit(solution)/shard_map/ppermute | solution.py:501
  31.4 14.5 %collective-permute-start.7 = (bf16[128,1024]{1,0:T(8,128)(2,1)}, bf16[128,1024]{1,0:T(8,128)(2,1)S(1)}, u32[]{:S(2)}, u32[]{:S(2)}) collective-permute-start(bf16[128,1024]{1,0:T(8,128)(2,1)} %shard_map.96.qd0), channel_id=1, source_target_pairs={{0,16},{8,24},{16,0},{24,8},{1,17},{9,25},{17,1},{25,9},{2,18},{10... | collective-permute-start | bytes 786440 | tf_op jit(solution)/shard_map/ppermute | solution.py:501
  34.0 11.9 %collective-permute-start.8 = (bf16[128,1024]{1,0:T(8,128)(2,1)}, bf16[128,1024]{1,0:T(8,128)(2,1)S(1)}, u32[]{:S(2)}, u32[]{:S(2)}) collective-permute-start(bf16[128,1024]{1,0:T(8,128)(2,1)} %shard_map.96.qd0), channel_id=1, source_target_pairs={{0,24},{8,0},{16,8},{24,16},{1,25},{9,1},{17,9},{25,17},{2,26},{10... | collective-permute-start | bytes 786440 | tf_op jit(solution)/shard_map/ppermute | solution.py:501
  48.8 24.4 %collective-permute-start.12 = (bf16[2,2048,128]{2,1,0:T(8,128)(2,1)}, bf16[2,2048,128]{2,1,0:T(8,128)(2,1)}, u32[]{:S(2)}, u32[]{:S(2)}) collective-permute-start(bf16[2,2048,128]{2,1,0:T(8,128)(2,1)} %get-tuple-element.59), channel_id=1, source_target_pairs={{0,2},{2,0},{1,3},{3,1},{4,6},{6,4},{5,7},{7,5},{8,10},{10,8},{9,1... | collective-permute-start | bytes 3145736 | tf_op jit(solution)/shard_map/ppermute | solution.py:448
  54.0 4.5 %collective-permute-start.10 = (f32[4,2048]{1,0:T(4,128)S(1)}, f32[4,2048]{1,0:T(4,128)S(1)}, u32[]{:S(2)}, u32[]{:S(2)}) collective-permute-start(f32[4,2048]{1,0:T(4,128)S(1)} %shard_map.98.st0), channel_id=1, source_target_pairs={{0,16},{8,24},{16,0},{24,8},{1,17},{9,25},{17,1},{25,9},{2,18},{10... | collective-permute-start | bytes 98312 | tf_op jit(solution)/shard_map/ppermute | solution.py:521
  57.0 3.2 %collective-permute-start.11 = (f32[4,2048]{1,0:T(4,128)S(1)}, f32[4,2048]{1,0:T(4,128)S(1)}, u32[]{:S(2)}, u32[]{:S(2)}) collective-permute-start(f32[4,2048]{1,0:T(4,128)S(1)} %shard_map.98.st0), channel_id=1, source_target_pairs={{0,24},{8,0},{16,8},{24,16},{1,25},{9,1},{17,9},{25,17},{2,26},{10... | collective-permute-start | bytes 98312 | tf_op jit(solution)/shard_map/ppermute | solution.py:521
  57.8 4.0 %collective-permute-start.9 = (f32[4,2048]{1,0:T(4,128)S(1)}, f32[4,2048]{1,0:T(4,128)S(1)}, u32[]{:S(2)}, u32[]{:S(2)}) collective-permute-start(f32[4,2048]{1,0:T(4,128)S(1)} %shard_map.98.st0), channel_id=1, source_target_pairs={{0,8},{8,16},{16,24},{24,0},{1,9},{9,17},{17,25},{25,1},{2,10},{10... | collective-permute-start | bytes 98312 | tf_op jit(solution)/shard_map/ppermute | solution.py:521
  65.6 18.6 %copy-start.4 = (bf16[128,512]{1,0:T(8,128)(2,1)S(1)}, bf16[128,512]{1,0:T(8,128)(2,1)}, u32[]{:S(2)}) copy-start(bf16[128,512]{1,0:T(8,128)(2,1)} %get-tuple-element.62) | copy-start | bytes 393220
  65.6 19.9 %copy-start.3 = (bf16[128,512]{1,0:T(8,128)(2,1)S(1)}, bf16[128,512]{1,0:T(8,128)(2,1)}, u32[]{:S(2)}) copy-start(bf16[128,512]{1,0:T(8,128)(2,1)} %get-tuple-element.63) | copy-start | bytes 393220
  65.6 19.9 %copy-start.2 = (bf16[128,512]{1,0:T(8,128)(2,1)S(1)}, bf16[128,512]{1,0:T(8,128)(2,1)}, u32[]{:S(2)}) copy-start(bf16[128,512]{1,0:T(8,128)(2,1)} %get-tuple-element.64) | copy-start | bytes 393220
  65.6 26.4 %copy-start.1 = (bf16[128,512]{1,0:T(8,128)(2,1)S(1)}, bf16[128,512]{1,0:T(8,128)(2,1)}, u32[]{:S(2)}) copy-start(bf16[128,512]{1,0:T(8,128)(2,1)} %get-tuple-element.61.dq0) | copy-start | bytes 393220
  73.2 36.6 %all-to-all-start.1 = ((bf16[16,128,256]{2,1,0:T(8,128)(2,1)}), bf16[16,128,256]{2,1,0:T(8,128)(2,1)S(1)}, u32[]{:S(2)}, u32[]{:S(2)}) async-start(bf16[16,128,256]{2,1,0:T(8,128)(2,1)} %get-tuple-element.60), calls=%async_computation.1 | async-start | bytes 2097152 | tf_op jit(solution)/shard_map/all_to_all | solution.py:525
  84.2 3.9 %collective-permute-start.13 = (bf16[128,512]{1,0:T(8,128)(2,1)S(1)}, bf16[128,512]{1,0:T(8,128)(2,1)S(1)}, u32[]{:S(2)}, u32[]{:S(2)}) collective-permute-start(bf16[128,512]{1,0:T(8,128)(2,1)S(1)} %copy-done.4), channel_id=1, source_target_pairs={{0,24},{8,0},{16,8},{24,16},{1,25},{9,1},{17,9},{25,17},{2,26},{10... | collective-permute-start | bytes 393224 | tf_op jit(solution)/shard_map/ppermute | solution.py:526
  85.5 5.4 %collective-permute-start.14 = (bf16[128,512]{1,0:T(8,128)(2,1)S(1)}, bf16[128,512]{1,0:T(8,128)(2,1)S(1)}, u32[]{:S(2)}, u32[]{:S(2)}) collective-permute-start(bf16[128,512]{1,0:T(8,128)(2,1)S(1)} %copy-done.3), channel_id=1, source_target_pairs={{0,16},{8,24},{16,0},{24,8},{1,17},{9,25},{17,1},{25,9},{2,18},{10... | collective-permute-start | bytes 393224 | tf_op jit(solution)/shard_map/ppermute | solution.py:526
  85.5 6.5 %collective-permute-start.15 = (bf16[128,512]{1,0:T(8,128)(2,1)S(1)}, bf16[128,512]{1,0:T(8,128)(2,1)S(1)}, u32[]{:S(2)}, u32[]{:S(2)}) collective-permute-start(bf16[128,512]{1,0:T(8,128)(2,1)S(1)} %copy-done.2), channel_id=1, source_target_pairs={{0,8},{8,16},{16,24},{24,0},{1,9},{9,17},{17,25},{25,1},{2,10},{10... | collective-permute-start | bytes 393224 | tf_op jit(solution)/shard_map/ppermute | solution.py:526
  94.7 5.2 %collective-permute-start.16 = (bf16[128,1024]{1,0:T(8,128)(2,1)S(1)}, bf16[128,1024]{1,0:T(8,128)(2,1)S(1)}, u32[]{:S(2)}, u32[]{:S(2)}) collective-permute-start(bf16[128,1024]{1,0:T(8,128)(2,1)S(1)} %get-tuple-element.66), channel_id=1, source_target_pairs={{0,1},{1,0},{2,3},{3,2},{4,5},{5,4},{6,7},{7,6},{8,9},{9,8},{10,11... | collective-permute-start | bytes 786440 | tf_op jit(solution)/shard_map/ppermute | solution.py:445
  103.6 1.6 %collective-permute-start.17 = (bf16[128,1024]{1,0:T(8,128)(2,1)S(1)}, bf16[128,1024]{1,0:T(8,128)(2,1)S(1)}, u32[]{:S(2)}, u32[]{:S(2)}) collective-permute-start(bf16[128,1024]{1,0:T(8,128)(2,1)S(1)} %get-tuple-element.71), channel_id=1, source_target_pairs={{0,1},{1,0},{2,3},{3,2},{4,5},{5,4},{6,7},{7,6},{8,9},{9,8},{10,11... | collective-permute-start | bytes 786440 | tf_op jit(solution)/shard_map/ppermute | solution.py:445
  104.0 11.3 %collective-permute-start.19 = (bf16[128,1024]{1,0:T(8,128)(2,1)}, bf16[128,1024]{1,0:T(8,128)(2,1)}, u32[]{:S(2)}, u32[]{:S(2)}) collective-permute-start(bf16[128,1024]{1,0:T(8,128)(2,1)} %add_convert_fusion.2), channel_id=1, source_target_pairs={{0,2},{2,0},{1,3},{3,1},{4,6},{6,4},{5,7},{7,5},{8,10},{10,8},{9,1... | collective-permute-start | bytes 786440 | tf_op jit(solution)/shard_map/ppermute | solution.py:448
  111.2 5.6 %collective-permute-start.18 = (bf16[128,256]{1,0:T(8,128)(2,1)S(1)}, bf16[128,256]{1,0:T(8,128)(2,1)S(1)}, u32[]{:S(2)}, u32[]{:S(2)}) collective-permute-start(bf16[128,256]{1,0:T(8,128)(2,1)S(1)} %get-tuple-element.73.dkv), channel_id=1, source_target_pairs={{0,2},{2,0},{1,3},{3,1},{4,6},{6,4},{5,7},{7,5},{8,10},{10,8},{9,1... | collective-permute-start | bytes 196616 | tf_op jit(solution)/shard_map/ppermute | solution.py:448
  117.6 4.9 %collective-permute-start.20 = (bf16[128,1024]{1,0:T(8,128)(2,1)S(1)}, bf16[128,1024]{1,0:T(8,128)(2,1)S(1)}, u32[]{:S(2)}, u32[]{:S(2)}) collective-permute-start(bf16[128,1024]{1,0:T(8,128)(2,1)S(1)} %shard_map.105), channel_id=1, source_target_pairs={{0,1},{1,0},{2,3},{3,2},{4,5},{5,4},{6,7},{7,6},{8,9},{9,8},{10,11... | collective-permute-start | bytes 786440 | tf_op jit(solution)/shard_map/ppermute | solution.py:445

commit v6 on v5

--- a/solution.py
+++ b/solution.py
@@ -236,15 +236,15 @@
         cols = slice(row, row + rows)
         keys = kv[pl.ds(first, count), :HEAD]
         values = kv[pl.ds(first, count), HEAD:]
-        scores = contract_last(keys, q_rows[cols, :]) * SCALE2
+        scores = contract_last(keys, q_rows[cols, :])
         first_visit = hidden is not None and count == CHUNK
         if hidden is not None:
             scores = scores + hidden
-        top = jnp.maximum(jnp.max(scores, axis=0, keepdims=True), LOWEST_TOP)
+        top = jnp.maximum(jnp.max(scores, axis=0, keepdims=True) * SCALE2, LOWEST_TOP)
         if not first_visit:
             old = out[0:1, cols]
             top = jnp.maximum(old, top)
-        prob = jnp.exp2(scores - top)
+        prob = jnp.exp2(scores * SCALE2 - top)
         prob_grad = contract_last(values, g_rows[cols, :])
         norm = jnp.sum(prob, axis=0, keepdims=True)
         dot = jnp.sum(prob * prob_grad, axis=0, keepdims=True)

time: 124 us -> 124 us (level)
  no operation moved by 1% of the time
where the time goes in v6:
time: 124 us; the launch traced here: 123 us
  waiting for transfers between devices  45.7 us (37%)
  starting transfers between devices  45.5 us (37%)
  Pallas kernels  28.4 us (23%)
  other arithmetic  1.6 us (1%)
    pallas_call x12, Pallas kernels, whole_call(): pl.pallas_call(kernel, in_specs=in_specs, out_specs=[pl.BlockSpec(memory_...  28.4 us
    ppermute x7, starting transfers between devices, to_core(): return lax.ppermute(value, 'core', swap)  13.4 us
    ppermute x5, waiting for transfers between devices, to_xl(): return lax.ppermute(value, 'xl', swap)  11.7 us
    ppermute x3, waiting for transfers between devices, local(): lax.ppermute(qd_own, 'y', shifted(4, s))  10.8 us
    all_to_all x1, starting transfers between devices, local(): dkv_parts = lax.all_to_all(dkv, ('z', 'xh'), 0, 0, tiled=True)  10.7 us
    all_to_all x1, starting transfers between devices, local(): lax.all_to_all(kv_own, ('z', 'xh'), 0, 0, tiled=True)  9.03 us
    ppermute x7, waiting for transfers between devices, to_core(): return lax.ppermute(value, 'core', swap)  6.2 us
    ppermute x3, waiting for transfers between devices, local(): lax.ppermute(dqs[s], 'y', shifted(4, -s))  6.12 us
  transfers between devices with their start and end apart: 23, of which 18 were waited for; matrix products, arithmetic and copies ran while one was open for 1% of the time, Pallas kernels for 22%

profile of v6, /device:TPU:1, one launch (start us, length us, event | category | flops | bytes accessed | tf_op | source)
XLA Modules:
  0.0 123.1 jit_solution(4754154671493182053)
XLA Ops:
  0.6 3.3 %collective-permute-start.1 = (bf16[128,1024]{1,0:T(8,128)(2,1)}, bf16[128,1024]{1,0:T(8,128)(2,1)S(1)}, u32[]{:S(2)}, u32[]{:S(2)}) collective-permute-start(bf16[128,1024]{1,0:T(8,128)(2,1)} %x0.1), channel_id=1, source_target_pairs={{0,1},{1,0},{2,3},{3,2},{4,5},{5,4},{6,7},{7,6},{8,9},{9,8},{10,11... | collective-permute-start | bytes 786440 | tf_op jit(solution)/shard_map/ppermute | solution.py:445
  4.1 1.2 collective-permute-done.1.x1
  5.7 0.9 copy-done
  6.7 5.2 %shard_map.94 = (f32[128,768]{1,0:T(8,128)S(1)}, f32[128,512]{1,0:T(8,128)}, bf16[2048,512]{1,0:T(8,128)(2,1)S(1)}, bf16[2048,128]{1,0:T(8,128)(2,1)S(1)}, bf16[...) custom-call(s32[5]{0:T(128)S(1)} %stack.23.place, bf16[128,1024]{1,0:T(8,128)(2,1)S(1)} %copy-done, ...), custom_call_target="tpu_custom_call" | custom-call | flops 671088640 | bytes 10485760 | tf_op jit(solution)/shard_map/pallas_call | solution.py:136
  11.9 1.1 collective-permute-start.3
  13.0 1.2 collective-permute-done.3.x3
  14.2 2.1 %shard_map.95 = (bf16[16,128,256]{2,1,0:T(8,128)(2,1)}, bf16[128,512]{1,0:T(8,128)(2,1)}) custom-call(s32[5]{0:T(128)S(1)} %stack.23.place, bf16[128,1024]{1,0:T(8,128)(2,1)S(1)} %collective-permute-done.x2, bf16[128,1024]{1,0:T(8,128)(2,1)S(1)} %collective-permute-done.3.x3, bf16[2048,512]{1,0:T(8,128)(2,1)S(1)} %get-tuple-element.45.wq, ...), custom_call_target="tpu_custom_call" | custom-call | flops 402653184 | bytes 4194304 | tf_op jit(solution)/shard_map/pallas_call | solution.py:136
  16.2 9.0 %all-to-all-start = ((bf16[16,128,256]{2,1,0:T(8,128)(2,1)}), bf16[16,128,256]{2,1,0:T(8,128)(2,1)S(1)}, u32[]{:S(2)}, u32[]{:S(2)}) async-start(bf16[16,128,256]{2,1,0:T(8,128)(2,1)} %get-tuple-element.49), calls=%async_computation | async-start | bytes 2097152 | tf_op jit(solution)/shard_map/all_to_all | solution.py:500
  25.3 0.7 collective-permute-start.5
  26.0 1.2 collective-permute-done.5.g3
  27.2 2.9 %shard_map.96.qd0 = bf16[128,1024]{1,0:T(8,128)(2,1)} custom-call(s32[5]{0:T(128)S(1)} %stack.23.place, bf16[128,1024]{1,0:T(8,128)(2,1)S(1)} %collective-permute-done.4.g2, bf16[128,1024]{1,0:T(8,128)(2,1)S(1)} %collective-permute-done.5.g3, bf16[512,2048]{1,0:T(8,128)(2,1)S(1)} %get-tuple-element.52.wo, f32[128,512]{1,0:T(8,128)} %get-tuple-element.53.g_half, ...), custom_call_target="tpu_custom_call" | custom-call | flops 10000000000 | bytes 3145728 | tf_op jit(solution)/shard_map/pallas_call | solution.py:136
  30.0 1.4 %collective-permute-start.6 = (bf16[128,1024]{1,0:T(8,128)(2,1)}, bf16[128,1024]{1,0:T(8,128)(2,1)S(1)}, u32[]{:S(2)}, u32[]{:S(2)}) collective-permute-start(bf16[128,1024]{1,0:T(8,128)(2,1)} %shard_map.96.qd0), channel_id=1, source_target_pairs={{0,8},{8,16},{16,24},{24,0},{1,9},{9,17},{17,25},{25,1},{2,10},{10... | collective-permute-start | bytes 786440 | tf_op jit(solution)/shard_map/ppermute | solution.py:501
  31.4 2.6 %collective-permute-start.7 = (bf16[128,1024]{1,0:T(8,128)(2,1)}, bf16[128,1024]{1,0:T(8,128)(2,1)S(1)}, u32[]{:S(2)}, u32[]{:S(2)}) collective-permute-start(bf16[128,1024]{1,0:T(8,128)(2,1)} %shard_map.96.qd0), channel_id=1, source_target_pairs={{0,16},{8,24},{16,0},{24,8},{1,17},{9,25},{17,1},{25,9},{2,18},{10... | collective-permute-start | bytes 786440 | tf_op jit(solution)/shard_map/ppermute | solution.py:501
  34.0 1.1 collective-permute-start.8
  35.1 4.1 %collective-permute-done.6.qd1 = bf16[128,1024]{1,0:T(8,128)(2,1)S(1)} collective-permute-done((bf16[128,1024]{1,0:T(8,128)(2,1)}, bf16[128,1024]{1,0:T(8,128)(2,1)S(1)}, u32[]{:S(2)}, u32[]{:S(2)}) %collective-permute-start.6) | collective-permute-done | bytes 262176 | tf_op jit(solution)/shard_map/ppermute | solution.py:501
  39.2 6.7 %collective-permute-done.7.qd2 = bf16[128,1024]{1,0:T(8,128)(2,1)S(1)} collective-permute-done((bf16[128,1024]{1,0:T(8,128)(2,1)}, bf16[128,1024]{1,0:T(8,128)(2,1)S(1)}, u32[]{:S(2)}, u32[]{:S(2)}) %collective-permute-start.7) | collective-permute-done | bytes 262176 | tf_op jit(solution)/shard_map/ppermute | solution.py:501
  45.9 2.9 %shard_map.97 = (bf16[2048,128]{1,0:T(8,128)(2,1)S(1)}, bf16[2048,128]{1,0:T(8,128)(2,1)S(1)}, f32[384,512]{1,0:T(8,128)S(1)}, bf16[2,2048,128]{2,1,0:T(8,128)(2,1)}) custom-call(s32[5]{0:T(128)S(1)} %stack.23.place, s32[64,128]{1,0:T(8,128)} %bitcast.9, bf16[128,1024]{1,0:T(8,128)(2,1)} %shard_map.96.qd0, bf16[128,1024]{1,0:T(8,128)(2,1)S(1)} %collective-permute-done.6.qd1, ...), custom_call_target="tpu_custom_call" | custom-call | bytes 2097152 | tf_op jit(solution)/shard_map/pallas_call | solution.py:136
  48.8 0.4 collective-permute-start.12
  49.2 3.2 %all-to-all-done = bf16[16,128,256]{2,1,0:T(8,128)(2,1)S(1)} async-done(((bf16[16,128,256]{2,1,0:T(8,128)(2,1)}), bf16[16,128,256]{2,1,0:T(8,128)(2,1)S(1)}, u32[]{:S(2)}, u32[]{:S(2)}) %all-to-all-start) | async-done | bytes 1048608 | tf_op jit(solution)/shard_map/all_to_all | solution.py:500
  52.4 1.7 %shard_map.98.st0 = f32[4,2048]{1,0:T(4,128)S(1)} custom-call(s32[5]{0:T(128)S(1)} %stack.23.place, bf16[2048,256]{1,0:T(8,128)(2,1)S(1)} %bitcast.7, bf16[2048,128]{1,0:T(8,128)(2,1)S(1)} %get-tuple-element.55.q_rows, bf16[2048,128]{1,0:T(8,128)(2,1)S(1)} %get-tuple-element.56.g_rows, f32[384,512]{1,0:T(8,128)S(1)} %get-tuple-element.57.bias), custom_call_target="tpu_custom_call" | custom-call | flops 2147483648 | bytes 2097152 | tf_op jit(solution)/shard_map/pallas_call | solution.py:136
  54.1 3.0 %collective-permute-start.10 = (f32[4,2048]{1,0:T(4,128)S(1)}, f32[4,2048]{1,0:T(4,128)S(1)}, u32[]{:S(2)}, u32[]{:S(2)}) collective-permute-start(f32[4,2048]{1,0:T(4,128)S(1)} %shard_map.98.st0), channel_id=1, source_target_pairs={{0,16},{8,24},{16,0},{24,8},{1,17},{9,25},{17,1},{25,9},{2,18},{10... | collective-permute-start | bytes 98312 | tf_op jit(solution)/shard_map/ppermute | solution.py:521
  57.1 0.8 collective-permute-start.11
  57.9 0.7 collective-permute-start.9
  58.6 1.7 %collective-permute-done.11.st3 = f32[4,2048]{1,0:T(4,128)S(1)} collective-permute-done((f32[4,2048]{1,0:T(4,128)S(1)}, f32[4,2048]{1,0:T(4,128)S(1)}, u32[]{:S(2)}, u32[]{:S(2)}) %collective-permute-start.11) | collective-permute-done | bytes 32800 | tf_op jit(solution)/shard_map/ppermute | solution.py:521
  60.3 1.6 %collective-permute-done.9.st1 = f32[4,2048]{1,0:T(4,128)S(1)} collective-permute-done((f32[4,2048]{1,0:T(4,128)S(1)}, f32[4,2048]{1,0:T(4,128)S(1)}, u32[]{:S(2)}, u32[]{:S(2)}) %collective-permute-start.9) | collective-permute-done | bytes 32800 | tf_op jit(solution)/shard_map/ppermute | solution.py:521
  61.8 3.8 %shard_map.99 = (bf16[16,128,256]{2,1,0:T(8,128)(2,1)}, bf16[128,512]{1,0:T(8,128)(2,1)}, bf16[128,512]{1,0:T(8,128)(2,1)}, bf16[128,512]{1,0:T(8,128)(2,1)}, bf16[128,512]{1,0:T(8,128)(2,1)}) custom-call(s32[5]{0:T(128)S(1)} %stack.23.place, bf16[2048,256]{1,0:T(8,128)(2,1)S(1)} %bitcast.8, bf16[2048,128]{1,0:T(8,128)(2,1)S(1)} %get-tuple-element.55.q_rows, ...), custom_call_target="tpu_custom_call" | custom-call | flops 5368709120 | bytes 4194304 | tf_op jit(solution)/shard_map/pallas_call | solution.py:136
  65.7 7.6 %collective-permute-done.12.got_kv = bf16[2,2048,128]{2,1,0:T(8,128)(2,1)} collective-permute-done((bf16[2,2048,128]{2,1,0:T(8,128)(2,1)}, bf16[2,2048,128]{2,1,0:T(8,128)(2,1)}, u32[]{:S(2)}, u32[]{:S(2)}) %collective-permute-start.12) | collective-permute-done | bytes 1048608 | tf_op jit(solution)/shard_map/ppermute | solution.py:448
  73.2 10.7 %all-to-all-start.1 = ((bf16[16,128,256]{2,1,0:T(8,128)(2,1)}), bf16[16,128,256]{2,1,0:T(8,128)(2,1)S(1)}, u32[]{:S(2)}, u32[]{:S(2)}) async-start(bf16[16,128,256]{2,1,0:T(8,128)(2,1)} %get-tuple-element.60), calls=%async_computation.1 | async-start | bytes 2097152 | tf_op jit(solution)/shard_map/all_to_all | solution.py:525
  84.0 1.5 %collective-permute-start.13 = (bf16[128,512]{1,0:T(8,128)(2,1)S(1)}, bf16[128,512]{1,0:T(8,128)(2,1)S(1)}, u32[]{:S(2)}, u32[]{:S(2)}) collective-permute-start(bf16[128,512]{1,0:T(8,128)(2,1)S(1)} %copy-done.4), channel_id=1, source_target_pairs={{0,24},{8,0},{16,8},{24,16},{1,25},{9,1},{17,9},{25,17},{2,26},{10... | collective-permute-start | bytes 393224 | tf_op jit(solution)/shard_map/ppermute | solution.py:526
  85.5 0.7 collective-permute-start.15
  86.2 1.7 %collective-permute-done.13.dq1 = bf16[128,512]{1,0:T(8,128)(2,1)S(1)} collective-permute-done((bf16[128,512]{1,0:T(8,128)(2,1)S(1)}, bf16[128,512]{1,0:T(8,128)(2,1)S(1)}, u32[]{:S(2)}, u32[]{:S(2)}) %collective-permute-start.13) | collective-permute-done | bytes 131104 | tf_op jit(solution)/shard_map/ppermute | solution.py:526
  87.9 3.0 %collective-permute-done.14.dq2 = bf16[128,512]{1,0:T(8,128)(2,1)S(1)} collective-permute-done((bf16[128,512]{1,0:T(8,128)(2,1)S(1)}, bf16[128,512]{1,0:T(8,128)(2,1)S(1)}, u32[]{:S(2)}, u32[]{:S(2)}) %collective-permute-start.14) | collective-permute-done | bytes 131104 | tf_op jit(solution)/shard_map/ppermute | solution.py:526
  90.9 1.4 %collective-permute-done.15.dq3 = bf16[128,512]{1,0:T(8,128)(2,1)S(1)} collective-permute-done((bf16[128,512]{1,0:T(8,128)(2,1)S(1)}, bf16[128,512]{1,0:T(8,128)(2,1)S(1)}, u32[]{:S(2)}, u32[]{:S(2)}) %collective-permute-start.15) | collective-permute-done | bytes 131104 | tf_op jit(solution)/shard_map/ppermute | solution.py:526
  92.3 2.7 %shard_map.100 = (bf16[128,1024]{1,0:T(8,128)(2,1)S(1)}, bf16[128,1024]{1,0:T(8,128)(2,1)S(1)}, bf16[128,512]{1,0:T(8,128)(2,1)S(1)}) custom-call(s32[5]{0:T(128)S(1)} %stack.23.place, bf16[128,512]{1,0:T(8,128)(2,1)S(1)} %copy-done.1, bf16[128,512]{1,0:T(8,128)(2,1)S(1)} %collective-permute-done.13.dq1, bf16[128,512]{1,0:T(8,128)(2,1)S(1)} %collective-permute-done.14.dq2, ...), custom_call_target="tpu_custom_call" | custom-call | flops 268435456 | bytes 2097152 | tf_op jit(solution)/shard_map/pallas_call | solution.py:136
  95.0 3.8 %collective-permute-start.16 = (bf16[128,1024]{1,0:T(8,128)(2,1)S(1)}, bf16[128,1024]{1,0:T(8,128)(2,1)S(1)}, u32[]{:S(2)}, u32[]{:S(2)}) collective-permute-start(bf16[128,1024]{1,0:T(8,128)(2,1)S(1)} %get-tuple-element.66), channel_id=1, source_target_pairs={{0,1},{1,0},{2,3},{3,2},{4,5},{5,4},{6,7},{7,6},{8,9},{9,8},{10,11... | collective-permute-start | bytes 786440 | tf_op jit(solution)/shard_map/ppermute | solution.py:445
  98.8 1.2 collective-permute-done.16
  100.0 0.8 add_convert_fusion.2
  100.7 2.8 %shard_map.101 = (bf16[128,1024]{1,0:T(8,128)(2,1)S(1)}, bf16[128,1024]{1,0:T(8,128)(2,1)S(1)}, bf16[2,2048,256]{2,1,0:T(8,128)(2,1)S(1)}) custom-call(s32[5]{0:T(128)S(1)} %stack.23.place, bf16[128,512]{1,0:T(8,128)(2,1)S(1)} %get-tuple-element.68.total, bf16[4096,512]{1,0:T(8,128)(2,1)} %wq.5, bf16[4096,128]{1,0:T(8,128)(2,1)} %wk.5, ...), custom_call_target="tpu_custom_call" | custom-call | flops 268435456 | bytes 4194304 | tf_op jit(solution)/shard_map/pallas_call | solution.py:136
  103.5 0.5 collective-permute-start.17
  104.3 0.9 collective-permute-done.17
  105.2 4.4 %all-to-all-done.1.parts = bf16[16,128,256]{2,1,0:T(8,128)(2,1)S(1)} async-done(((bf16[16,128,256]{2,1,0:T(8,128)(2,1)}), bf16[16,128,256]{2,1,0:T(8,128)(2,1)S(1)}, u32[]{:S(2)}, u32[]{:S(2)}) %all-to-all-start.1) | async-done | bytes 1048608 | tf_op jit(solution)/shard_map/all_to_all | solution.py:525
  109.6 1.3 %shard_map.102 = (bf16[128,128]{1,0:T(8,128)(2,1)}, bf16[128,128]{1,0:T(8,128)(2,1)}, bf16[128,256]{1,0:T(8,128)(2,1)S(1)}) custom-call(s32[5]{0:T(128)S(1)} %stack.23.place, bf16[16,128,256]{2,1,0:T(8,128)(2,1)S(1)} %all-to-all-done.1.parts), custom_call_target="tpu_custom_call" | custom-call | bytes 2097152 | tf_op jit(solution)/shard_map/pallas_call | solution.py:136
  111.0 4.1 %collective-permute-done.19.far_queries = bf16[128,1024]{1,0:T(8,128)(2,1)} collective-permute-done((bf16[128,1024]{1,0:T(8,128)(2,1)}, bf16[128,1024]{1,0:T(8,128)(2,1)}, u32[]{:S(2)}, u32[]{:S(2)}) %collective-permute-start.19) | collective-permute-done | bytes 262176 | tf_op jit(solution)/shard_map/ppermute | solution.py:448
  115.0 1.4 %shard_map.103 = (f32[128,1024]{1,0:T(8,128)S(1)}, f32[128,1024]{1,0:T(8,128)S(1)}) custom-call(s32[5]{0:T(128)S(1)} %stack.23.place, bf16[128,256]{1,0:T(8,128)(2,1)S(1)} %get-tuple-element.73.dkv, bf16[2,2048,256]{2,1,0:T(8,128)(2,1)S(1)} %get-tuple-element.74.weights, bf16[128,1024]{1,0:T(8,128)(2,1)S(1)} %add_convert_fusion.1.queries, ...), custom_call_target="tpu_custom_call" | custom-call | flops 134217728 | bytes 2097152 | tf_op jit(solution)/shard_map/pallas_call | solution.py:136
  116.5 0.8 shard_map.105
  117.3 3.9 %collective-permute-start.20 = (bf16[128,1024]{1,0:T(8,128)(2,1)S(1)}, bf16[128,1024]{1,0:T(8,128)(2,1)S(1)}, u32[]{:S(2)}, u32[]{:S(2)}) collective-permute-start(bf16[128,1024]{1,0:T(8,128)(2,1)S(1)} %shard_map.105), channel_id=1, source_target_pairs={{0,1},{1,0},{2,3},{3,2},{4,5},{5,4},{6,7},{7,6},{8,9},{9,8},{10,11... | collective-permute-start | bytes 786440 | tf_op jit(solution)/shard_map/ppermute | solution.py:445
  121.2 0.8 shard_map.104
  122.4 0.8 add_convert_fusion
  (24 shorter events, 1.3 us)
Async XLA Ops:
  0.6 4.7 %collective-permute-start.1 = (bf16[128,1024]{1,0:T(8,128)(2,1)}, bf16[128,1024]{1,0:T(8,128)(2,1)S(1)}, u32[]{:S(2)}, u32[]{:S(2)}) collective-permute-start(bf16[128,1024]{1,0:T(8,128)(2,1)} %x0.1), channel_id=1, source_target_pairs={{0,1},{1,0},{2,3},{3,2},{4,5},{5,4},{6,7},{7,6},{8,9},{9,8},{10,11... | collective-permute-start | bytes 786440 | tf_op jit(solution)/shard_map/ppermute | solution.py:445
  4.0 1.7 %collective-permute-start.2 = (bf16[128,1024]{1,0:T(8,128)(2,1)}, bf16[128,1024]{1,0:T(8,128)(2,1)S(1)}, u32[]{:S(2)}, u32[]{:S(2)}) collective-permute-start(bf16[128,1024]{1,0:T(8,128)(2,1)} %g0.1), channel_id=1, source_target_pairs={{0,1},{1,0},{2,3},{3,2},{4,5},{5,4},{6,7},{7,6},{8,9},{9,8},{10,11... | collective-permute-start | bytes 786440 | tf_op jit(solution)/shard_map/ppermute | solution.py:445
  4.1 7.8 %collective-permute-start = (bf16[128,1024]{1,0:T(8,128)(2,1)}, bf16[128,1024]{1,0:T(8,128)(2,1)S(1)}, u32[]{:S(2)}, u32[]{:S(2)}) collective-permute-start(bf16[128,1024]{1,0:T(8,128)(2,1)} %x0.1), channel_id=1, source_target_pairs={{0,2},{2,0},{1,3},{3,1},{4,6},{6,4},{5,7},{7,5},{8,10},{10,8},{9,1... | collective-permute-start | bytes 786440 | tf_op jit(solution)/shard_map/ppermute | solution.py:448
  5.7 0.9 copy-start
  11.9 2.3 %collective-permute-start.3 = (bf16[128,1024]{1,0:T(8,128)(2,1)S(1)}, bf16[128,1024]{1,0:T(8,128)(2,1)S(1)}, u32[]{:S(2)}, u32[]{:S(2)}) collective-permute-start(bf16[128,1024]{1,0:T(8,128)(2,1)S(1)} %collective-permute-done.x2), channel_id=1, source_target_pairs={{0,1},{1,0},{2,3},{3,2},{4,5},{5,4},{6,7},{7,6},{8,9},{9,8},{10,11... | collective-permute-start | bytes 786440 | tf_op jit(solution)/shard_map/ppermute | solution.py:445
  13.0 12.3 %collective-permute-start.4 = (bf16[128,1024]{1,0:T(8,128)(2,1)}, bf16[128,1024]{1,0:T(8,128)(2,1)S(1)}, u32[]{:S(2)}, u32[]{:S(2)}) collective-permute-start(bf16[128,1024]{1,0:T(8,128)(2,1)} %g0.1), channel_id=1, source_target_pairs={{0,2},{2,0},{1,3},{3,1},{4,6},{6,4},{5,7},{7,5},{8,10},{10,8},{9,1... | collective-permute-start | bytes 786440 | tf_op jit(solution)/shard_map/ppermute | solution.py:448
  16.2 36.2 %all-to-all-start = ((bf16[16,128,256]{2,1,0:T(8,128)(2,1)}), bf16[16,128,256]{2,1,0:T(8,128)(2,1)S(1)}, u32[]{:S(2)}, u32[]{:S(2)}) async-start(bf16[16,128,256]{2,1,0:T(8,128)(2,1)} %get-tuple-element.49), calls=%async_computation | async-start | bytes 2097152 | tf_op jit(solution)/shard_map/all_to_all | solution.py:500
  25.3 1.9 %collective-permute-start.5 = (bf16[128,1024]{1,0:T(8,128)(2,1)S(1)}, bf16[128,1024]{1,0:T(8,128)(2,1)S(1)}, u32[]{:S(2)}, u32[]{:S(2)}) collective-permute-start(bf16[128,1024]{1,0:T(8,128)(2,1)S(1)} %collective-permute-done.4.g2), channel_id=1, source_target_pairs={{0,1},{1,0},{2,3},{3,2},{4,5},{5,4},{6,7},{7,6},{8,9},{9,8},{10,11... | collective-permute-start | bytes 786440 | tf_op jit(solution)/shard_map/ppermute | solution.py:445
  30.0 9.1 %collective-permute-start.6 = (bf16[128,1024]{1,0:T(8,128)(2,1)}, bf16[128,1024]{1,0:T(8,128)(2,1)S(1)}, u32[]{:S(2)}, u32[]{:S(2)}) collective-permute-start(bf16[128,1024]{1,0:T(8,128)(2,1)} %shard_map.96.qd0), channel_id=1, source_target_pairs={{0,8},{8,16},{16,24},{24,0},{1,9},{9,17},{17,25},{25,1},{2,10},{10... | collective-permute-start | bytes 786440 | tf_op jit(solution)/shard_map/ppermute | solution.py:501
  31.4 14.5 %collective-permute-start.7 = (bf16[128,1024]{1,0:T(8,128)(2,1)}, bf16[128,1024]{1,0:T(8,128)(2,1)S(1)}, u32[]{:S(2)}, u32[]{:S(2)}) collective-permute-start(bf16[128,1024]{1,0:T(8,128)(2,1)} %shard_map.96.qd0), channel_id=1, source_target_pairs={{0,16},{8,24},{16,0},{24,8},{1,17},{9,25},{17,1},{25,9},{2,18},{10... | collective-permute-start | bytes 786440 | tf_op jit(solution)/shard_map/ppermute | solution.py:501
  34.0 11.9 %collective-permute-start.8 = (bf16[128,1024]{1,0:T(8,128)(2,1)}, bf16[128,1024]{1,0:T(8,128)(2,1)S(1)}, u32[]{:S(2)}, u32[]{:S(2)}) collective-permute-start(bf16[128,1024]{1,0:T(8,128)(2,1)} %shard_map.96.qd0), channel_id=1, source_target_pairs={{0,24},{8,0},{16,8},{24,16},{1,25},{9,1},{17,9},{25,17},{2,26},{10... | collective-permute-start | bytes 786440 | tf_op jit(solution)/shard_map/ppermute | solution.py:501
  48.8 24.4 %collective-permute-start.12 = (bf16[2,2048,128]{2,1,0:T(8,128)(2,1)}, bf16[2,2048,128]{2,1,0:T(8,128)(2,1)}, u32[]{:S(2)}, u32[]{:S(2)}) collective-permute-start(bf16[2,2048,128]{2,1,0:T(8,128)(2,1)} %get-tuple-element.59), channel_id=1, source_target_pairs={{0,2},{2,0},{1,3},{3,1},{4,6},{6,4},{5,7},{7,5},{8,10},{10,8},{9,1... | collective-permute-start | bytes 3145736 | tf_op jit(solution)/shard_map/ppermute | solution.py:448
  54.1 4.5 %collective-permute-start.10 = (f32[4,2048]{1,0:T(4,128)S(1)}, f32[4,2048]{1,0:T(4,128)S(1)}, u32[]{:S(2)}, u32[]{:S(2)}) collective-permute-start(f32[4,2048]{1,0:T(4,128)S(1)} %shard_map.98.st0), channel_id=1, source_target_pairs={{0,16},{8,24},{16,0},{24,8},{1,17},{9,25},{17,1},{25,9},{2,18},{10... | collective-permute-start | bytes 98312 | tf_op jit(solution)/shard_map/ppermute | solution.py:521
  57.1 3.2 %collective-permute-start.11 = (f32[4,2048]{1,0:T(4,128)S(1)}, f32[4,2048]{1,0:T(4,128)S(1)}, u32[]{:S(2)}, u32[]{:S(2)}) collective-permute-start(f32[4,2048]{1,0:T(4,128)S(1)} %shard_map.98.st0), channel_id=1, source_target_pairs={{0,24},{8,0},{16,8},{24,16},{1,25},{9,1},{17,9},{25,17},{2,26},{10... | collective-permute-start | bytes 98312 | tf_op jit(solution)/shard_map/ppermute | solution.py:521
  57.9 4.0 %collective-permute-start.9 = (f32[4,2048]{1,0:T(4,128)S(1)}, f32[4,2048]{1,0:T(4,128)S(1)}, u32[]{:S(2)}, u32[]{:S(2)}) collective-permute-start(f32[4,2048]{1,0:T(4,128)S(1)} %shard_map.98.st0), channel_id=1, source_target_pairs={{0,8},{8,16},{16,24},{24,0},{1,9},{9,17},{17,25},{25,1},{2,10},{10... | collective-permute-start | bytes 98312 | tf_op jit(solution)/shard_map/ppermute | solution.py:521
  65.6 18.4 %copy-start.4 = (bf16[128,512]{1,0:T(8,128)(2,1)S(1)}, bf16[128,512]{1,0:T(8,128)(2,1)}, u32[]{:S(2)}) copy-start(bf16[128,512]{1,0:T(8,128)(2,1)} %get-tuple-element.62) | copy-start | bytes 393220
  65.6 19.9 %copy-start.3 = (bf16[128,512]{1,0:T(8,128)(2,1)S(1)}, bf16[128,512]{1,0:T(8,128)(2,1)}, u32[]{:S(2)}) copy-start(bf16[128,512]{1,0:T(8,128)(2,1)} %get-tuple-element.63) | copy-start | bytes 393220
  65.6 19.8 %copy-start.2 = (bf16[128,512]{1,0:T(8,128)(2,1)S(1)}, bf16[128,512]{1,0:T(8,128)(2,1)}, u32[]{:S(2)}) copy-start(bf16[128,512]{1,0:T(8,128)(2,1)} %get-tuple-element.64) | copy-start | bytes 393220
  65.6 26.6 %copy-start.1 = (bf16[128,512]{1,0:T(8,128)(2,1)S(1)}, bf16[128,512]{1,0:T(8,128)(2,1)}, u32[]{:S(2)}) copy-start(bf16[128,512]{1,0:T(8,128)(2,1)} %get-tuple-element.61.dq0) | copy-start | bytes 393220
  73.2 36.4 %all-to-all-start.1 = ((bf16[16,128,256]{2,1,0:T(8,128)(2,1)}), bf16[16,128,256]{2,1,0:T(8,128)(2,1)S(1)}, u32[]{:S(2)}, u32[]{:S(2)}) async-start(bf16[16,128,256]{2,1,0:T(8,128)(2,1)} %get-tuple-element.60), calls=%async_computation.1 | async-start | bytes 2097152 | tf_op jit(solution)/shard_map/all_to_all | solution.py:525
  84.0 3.9 %collective-permute-start.13 = (bf16[128,512]{1,0:T(8,128)(2,1)S(1)}, bf16[128,512]{1,0:T(8,128)(2,1)S(1)}, u32[]{:S(2)}, u32[]{:S(2)}) collective-permute-start(bf16[128,512]{1,0:T(8,128)(2,1)S(1)} %copy-done.4), channel_id=1, source_target_pairs={{0,24},{8,0},{16,8},{24,16},{1,25},{9,1},{17,9},{25,17},{2,26},{10... | collective-permute-start | bytes 393224 | tf_op jit(solution)/shard_map/ppermute | solution.py:526
  85.5 5.4 %collective-permute-start.14 = (bf16[128,512]{1,0:T(8,128)(2,1)S(1)}, bf16[128,512]{1,0:T(8,128)(2,1)S(1)}, u32[]{:S(2)}, u32[]{:S(2)}) collective-permute-start(bf16[128,512]{1,0:T(8,128)(2,1)S(1)} %copy-done.3), channel_id=1, source_target_pairs={{0,16},{8,24},{16,0},{24,8},{1,17},{9,25},{17,1},{25,9},{2,18},{10... | collective-permute-start | bytes 393224 | tf_op jit(solution)/shard_map/ppermute | solution.py:526
  85.5 6.8 %collective-permute-start.15 = (bf16[128,512]{1,0:T(8,128)(2,1)S(1)}, bf16[128,512]{1,0:T(8,128)(2,1)S(1)}, u32[]{:S(2)}, u32[]{:S(2)}) collective-permute-start(bf16[128,512]{1,0:T(8,128)(2,1)S(1)} %copy-done.2), channel_id=1, source_target_pairs={{0,8},{8,16},{16,24},{24,0},{1,9},{9,17},{17,25},{25,1},{2,10},{10... | collective-permute-start | bytes 393224 | tf_op jit(solution)/shard_map/ppermute | solution.py:526
  95.0 4.9 %collective-permute-start.16 = (bf16[128,1024]{1,0:T(8,128)(2,1)S(1)}, bf16[128,1024]{1,0:T(8,128)(2,1)S(1)}, u32[]{:S(2)}, u32[]{:S(2)}) collective-permute-start(bf16[128,1024]{1,0:T(8,128)(2,1)S(1)} %get-tuple-element.66), channel_id=1, source_target_pairs={{0,1},{1,0},{2,3},{3,2},{4,5},{5,4},{6,7},{7,6},{8,9},{9,8},{10,11... | collective-permute-start | bytes 786440 | tf_op jit(solution)/shard_map/ppermute | solution.py:445
  103.5 1.6 %collective-permute-start.17 = (bf16[128,1024]{1,0:T(8,128)(2,1)S(1)}, bf16[128,1024]{1,0:T(8,128)(2,1)S(1)}, u32[]{:S(2)}, u32[]{:S(2)}) collective-permute-start(bf16[128,1024]{1,0:T(8,128)(2,1)S(1)} %get-tuple-element.71), channel_id=1, source_target_pairs={{0,1},{1,0},{2,3},{3,2},{4,5},{5,4},{6,7},{7,6},{8,9},{9,8},{10,11... | collective-permute-start | bytes 786440 | tf_op jit(solution)/shard_map/ppermute | solution.py:445
  104.0 11.0 %collective-permute-start.19 = (bf16[128,1024]{1,0:T(8,128)(2,1)}, bf16[128,1024]{1,0:T(8,128)(2,1)}, u32[]{:S(2)}, u32[]{:S(2)}) collective-permute-start(bf16[128,1024]{1,0:T(8,128)(2,1)} %add_convert_fusion.2), channel_id=1, source_target_pairs={{0,2},{2,0},{1,3},{3,1},{4,6},{6,4},{5,7},{7,5},{8,10},{10,8},{9,1... | collective-permute-start | bytes 786440 | tf_op jit(solution)/shard_map/ppermute | solution.py:448
  111.0 5.5 %collective-permute-start.18 = (bf16[128,256]{1,0:T(8,128)(2,1)S(1)}, bf16[128,256]{1,0:T(8,128)(2,1)S(1)}, u32[]{:S(2)}, u32[]{:S(2)}) collective-permute-start(bf16[128,256]{1,0:T(8,128)(2,1)S(1)} %get-tuple-element.73.dkv), channel_id=1, source_target_pairs={{0,2},{2,0},{1,3},{3,1},{4,6},{6,4},{5,7},{7,5},{8,10},{10,8},{9,1... | collective-permute-start | bytes 196616 | tf_op jit(solution)/shard_map/ppermute | solution.py:448
  117.3 5.0 %collective-permute-start.20 = (bf16[128,1024]{1,0:T(8,128)(2,1)S(1)}, bf16[128,1024]{1,0:T(8,128)(2,1)S(1)}, u32[]{:S(2)}, u32[]{:S(2)}) collective-permute-start(bf16[128,1024]{1,0:T(8,128)(2,1)S(1)} %shard_map.105), channel_id=1, source_target_pairs={{0,1},{1,0},{2,3},{3,2},{4,5},{5,4},{6,7},{7,6},{8,9},{9,8},{10,11... | collective-permute-start | bytes 786440 | tf_op jit(solution)/shard_map/ppermute | solution.py:445

commit v7 on v6

--- a/solution.py
+++ b/solution.py
@@ -47,7 +47,7 @@
 
 def near_kernel(
     place, x0, x1, g0, g1, wq, wk, wv, wo,
-    x_half, g_half, far_q, far_k, far_v, far_o,
+    x_half, g_half, far_q, far_kv, far_o,
     near_q, near_k, near_v, near_o, g_buf, sems,
 ):
     xl, core = place[3], place[4]
@@ -56,7 +56,7 @@
     copies = []
     for rows, targets in (
         (near, (near_q, near_k, near_v, near_o)),
-        (far, (far_q, far_k, far_v, far_o)),
+        (far, (far_q, far_kv.at[:, :HEAD], far_kv.at[:, HEAD:], far_o)),
     ):
         for source, target in zip((wq, wk, wv, wo), targets):
             part = source.at[:, rows] if source is wo else source.at[rows, :]
@@ -83,7 +83,7 @@
     return [pl.ds(pl.multiple_of(c * 1024, 1024), 1024) for c in (core, 1 - core)]
 
 
-def far_inputs_kernel(place, x2, x3, wq, wk, wv, x_half, kv, q, kv_buf, q_buf, sems):
+def far_inputs_kernel(place, x2, x3, wq, wkv, x_half, kv, q, kv_buf, q_buf, sems):
     own, other = core_halves(place[4])
 
     def product(weight, low, high):
@@ -93,7 +93,7 @@
             + matmul(x3[...], weight[other, :])
         ).astype(BF16)
 
-    pair = jnp.concatenate([product(wk, 0, 128), product(wv, 128, 256)], axis=1)
+    pair = product(wkv, 0, 256)
     for i in range(4):
         kv_buf[i] = pair
     copies = [
@@ -455,10 +455,11 @@
     held = [
         shape(PAIR, ROWS), shape(PAIR, HEAD), shape(PAIR, HEAD), shape(ROWS, PAIR)
     ]
-    x_half, g_half, far_q, far_k, far_v, far_o = whole_call(
+    x_half, g_half, far_q, far_kv, far_o = whole_call(
         near_kernel,
         (place, inputs, x1, out_grad, g1, w_query, key_weight, value_weight, w_output),
-        [shape(BLOCK, 768, kind=F32), shape(BLOCK, ROWS, kind=F32)] + held,
+        [shape(BLOCK, 768, kind=F32), shape(BLOCK, ROWS, kind=F32)]
+        + [held[0], shape(PAIR, 2 * HEAD), held[3]],
         [pltpu.VMEM(h.shape, BF16) for h in held]
         + [pltpu.VMEM((BLOCK, ROWS), F32), pltpu.SemaphoreType.DMA((9,))],
         hbm=(5, 6, 7, 8),
@@ -470,7 +471,7 @@
     x3 = to_core(x2)
     kv_own, q_own = whole_call(
         far_inputs_kernel,
-        (place, x2, x3, far_q, far_k, far_v, x_half),
+        (place, x2, x3, far_q, far_kv, x_half),
         [shape(16, BLOCK, 2 * HEAD), shape(BLOCK, ROWS)],
         [
             pltpu.VMEM((4, BLOCK, 2 * HEAD), BF16),
@@ -500,7 +501,7 @@
     kv = lax.all_to_all(kv_own, ("z", "xh"), 0, 0, tiled=True).reshape(16 * BLOCK, 2 * HEAD)
     blocks = [qd_own] + [lax.ppermute(qd_own, "y", shifted(4, s)) for s in (1, 2, 3)]
 
-    *rows, far_kv = whole_call(
+    *rows, sent_kv = whole_call(
         stack_kernel,
         (place, times2d, *blocks, key_weight, value_weight),
         [shape(4 * ROWS, HEAD)] * 2
@@ -516,7 +517,7 @@
         hbm_outs=(3,),
         traffic=2 << 20,
     )
-    got_kv = to_xl(far_kv)
+    got_kv = to_xl(sent_kv)
     own_stats = stats(place, kv, rows)
     gathered = [own_stats] + [lax.ppermute(own_stats, "y", shifted(4, s)) for s in (1, 2, 3)]
     dkv, *dqs = grads(place, kv, rows, gathered)

time: 124 us -> 124 us (level)
  no operation moved by 1% of the time
where the time goes in v7:
time: 124 us; the launch traced here: 123 us
  waiting for transfers between devices  45.7 us (37%)
  starting transfers between devices  45.5 us (37%)
  Pallas kernels  28.5 us (23%)
  other arithmetic  1.6 us (1%)
    pallas_call x12, Pallas kernels, whole_call(): pl.pallas_call(kernel, in_specs=in_specs, out_specs=[pl.BlockSpec(memory_...  28.5 us
    ppermute x7, starting transfers between devices, to_core(): return lax.ppermute(value, 'core', swap)  13.3 us
    ppermute x5, waiting for transfers between devices, to_xl(): return lax.ppermute(value, 'xl', swap)  11.7 us
    ppermute x3, waiting for transfers between devices, local(): lax.ppermute(qd_own, 'y', shifted(4, s))  10.8 us
    all_to_all x1, starting transfers between devices, local(): dkv_parts = lax.all_to_all(dkv, ('z', 'xh'), 0, 0, tiled=True)  10.8 us
    all_to_all x1, starting transfers between devices, local(): lax.all_to_all(kv_own, ('z', 'xh'), 0, 0, tiled=True)  9.03 us
    ppermute x7, waiting for transfers between devices, to_core(): return lax.ppermute(value, 'core', swap)  6.19 us
    ppermute x3, waiting for transfers between devices, local(): lax.ppermute(dqs[s], 'y', shifted(4, -s))  6.12 us
  transfers between devices with their start and end apart: 23, of which 18 were waited for; matrix products, arithmetic and copies ran while one was open for 1% of the time, Pallas kernels for 22%

profile of v7, /device:TPU:1, one launch (start us, length us, event | category | flops | bytes accessed | tf_op | source)
XLA Modules:
  0.0 123.1 jit_solution(14774358158238044256)
XLA Ops:
  0.6 3.3 %collective-permute-start.1 = (bf16[128,1024]{1,0:T(8,128)(2,1)}, bf16[128,1024]{1,0:T(8,128)(2,1)S(1)}, u32[]{:S(2)}, u32[]{:S(2)}) collective-permute-start(bf16[128,1024]{1,0:T(8,128)(2,1)} %x0.1), channel_id=1, source_target_pairs={{0,1},{1,0},{2,3},{3,2},{4,5},{5,4},{6,7},{7,6},{8,9},{9,8},{10,11... | collective-permute-start | bytes 786440 | tf_op jit(solution)/shard_map/ppermute | solution.py:445
  4.1 1.2 collective-permute-done.1.x1
  5.7 0.9 copy-done
  6.7 5.2 %shard_map.94 = (f32[128,768]{1,0:T(8,128)S(1)}, f32[128,512]{1,0:T(8,128)}, bf16[2048,512]{1,0:T(8,128)(2,1)S(1)}, bf16[2048,256]{1,0:T(8,128)(2,1)S(1)}, bf16[512,2048]{1,0:T(8,128)(2,1)S(1)}) custom-call(s32[5]{0:T(128)S(1)} %stack.23.place, bf16[128,1024]{1,0:T(8,128)(2,1)S(1)} %copy-done, bf16[128,1024]{1,0:T(8,128)(2,1)S(1)} %collective-permute-done.1.x1, ...), custom_call_target="tpu_custom_call" | custom-call | flops 671088640 | bytes 10485760 | tf_op jit(solution)/shard_map/pallas_call | solution.py:136
  11.9 1.1 collective-permute-start.3
  13.0 1.2 collective-permute-done.3.x3
  14.2 2.1 %shard_map.95 = (bf16[16,128,256]{2,1,0:T(8,128)(2,1)}, bf16[128,512]{1,0:T(8,128)(2,1)}) custom-call(s32[5]{0:T(128)S(1)} %stack.23.place, bf16[128,1024]{1,0:T(8,128)(2,1)S(1)} %collective-permute-done.x2, bf16[128,1024]{1,0:T(8,128)(2,1)S(1)} %collective-permute-done.3.x3, bf16[2048,512]{1,0:T(8,128)(2,1)S(1)} %get-tuple-element.44.wq, ...), custom_call_target="tpu_custom_call" | custom-call | flops 402653184 | bytes 4194304 | tf_op jit(solution)/shard_map/pallas_call | solution.py:136
  16.2 9.0 %all-to-all-start = ((bf16[16,128,256]{2,1,0:T(8,128)(2,1)}), bf16[16,128,256]{2,1,0:T(8,128)(2,1)S(1)}, u32[]{:S(2)}, u32[]{:S(2)}) async-start(bf16[16,128,256]{2,1,0:T(8,128)(2,1)} %get-tuple-element.47), calls=%async_computation | async-start | bytes 2097152 | tf_op jit(solution)/shard_map/all_to_all | solution.py:501
  25.3 0.7 collective-permute-start.5
  26.0 1.2 collective-permute-done.5.g3
  27.2 2.9 %shard_map.96.qd0 = bf16[128,1024]{1,0:T(8,128)(2,1)} custom-call(s32[5]{0:T(128)S(1)} %stack.23.place, bf16[128,1024]{1,0:T(8,128)(2,1)S(1)} %collective-permute-done.4.g2, bf16[128,1024]{1,0:T(8,128)(2,1)S(1)} %collective-permute-done.5.g3, bf16[512,2048]{1,0:T(8,128)(2,1)S(1)} %get-tuple-element.50.wo, f32[128,512]{1,0:T(8,128)} %get-tuple-element.51.g_half, ...), custom_call_target="tpu_custom_call" | custom-call | flops 10000000000 | bytes 3145728 | tf_op jit(solution)/shard_map/pallas_call | solution.py:136
  30.0 1.4 %collective-permute-start.6 = (bf16[128,1024]{1,0:T(8,128)(2,1)}, bf16[128,1024]{1,0:T(8,128)(2,1)S(1)}, u32[]{:S(2)}, u32[]{:S(2)}) collective-permute-start(bf16[128,1024]{1,0:T(8,128)(2,1)} %shard_map.96.qd0), channel_id=1, source_target_pairs={{0,8},{8,16},{16,24},{24,0},{1,9},{9,17},{17,25},{25,1},{2,10},{10... | collective-permute-start | bytes 786440 | tf_op jit(solution)/shard_map/ppermute | solution.py:502
  31.4 2.6 %collective-permute-start.7 = (bf16[128,1024]{1,0:T(8,128)(2,1)}, bf16[128,1024]{1,0:T(8,128)(2,1)S(1)}, u32[]{:S(2)}, u32[]{:S(2)}) collective-permute-start(bf16[128,1024]{1,0:T(8,128)(2,1)} %shard_map.96.qd0), channel_id=1, source_target_pairs={{0,16},{8,24},{16,0},{24,8},{1,17},{9,25},{17,1},{25,9},{2,18},{10... | collective-permute-start | bytes 786440 | tf_op jit(solution)/shard_map/ppermute | solution.py:502
  34.0 1.1 collective-permute-start.8
  35.1 4.1 %collective-permute-done.6.qd1 = bf16[128,1024]{1,0:T(8,128)(2,1)S(1)} collective-permute-done((bf16[128,1024]{1,0:T(8,128)(2,1)}, bf16[128,1024]{1,0:T(8,128)(2,1)S(1)}, u32[]{:S(2)}, u32[]{:S(2)}) %collective-permute-start.6) | collective-permute-done | bytes 262176 | tf_op jit(solution)/shard_map/ppermute | solution.py:502
  39.2 6.7 %collective-permute-done.7.qd2 = bf16[128,1024]{1,0:T(8,128)(2,1)S(1)} collective-permute-done((bf16[128,1024]{1,0:T(8,128)(2,1)}, bf16[128,1024]{1,0:T(8,128)(2,1)S(1)}, u32[]{:S(2)}, u32[]{:S(2)}) %collective-permute-start.7) | collective-permute-done | bytes 262176 | tf_op jit(solution)/shard_map/ppermute | solution.py:502
  45.9 2.9 %shard_map.97 = (bf16[2048,128]{1,0:T(8,128)(2,1)S(1)}, bf16[2048,128]{1,0:T(8,128)(2,1)S(1)}, f32[384,512]{1,0:T(8,128)S(1)}, bf16[2,2048,128]{2,1,0:T(8,128)(2,1)}) custom-call(s32[5]{0:T(128)S(1)} %stack.23.place, s32[64,128]{1,0:T(8,128)} %bitcast.9, bf16[128,1024]{1,0:T(8,128)(2,1)} %shard_map.96.qd0, bf16[128,1024]{1,0:T(8,128)(2,1)S(1)} %collective-permute-done.6.qd1, ...), custom_call_target="tpu_custom_call" | custom-call | bytes 2097152 | tf_op jit(solution)/shard_map/pallas_call | solution.py:136
  48.8 0.4 collective-permute-start.12
  49.2 3.2 %all-to-all-done = bf16[16,128,256]{2,1,0:T(8,128)(2,1)S(1)} async-done(((bf16[16,128,256]{2,1,0:T(8,128)(2,1)}), bf16[16,128,256]{2,1,0:T(8,128)(2,1)S(1)}, u32[]{:S(2)}, u32[]{:S(2)}) %all-to-all-start) | async-done | bytes 1048608 | tf_op jit(solution)/shard_map/all_to_all | solution.py:501
  52.4 1.7 %shard_map.98.st0 = f32[4,2048]{1,0:T(4,128)S(1)} custom-call(s32[5]{0:T(128)S(1)} %stack.23.place, bf16[2048,256]{1,0:T(8,128)(2,1)S(1)} %bitcast.7, bf16[2048,128]{1,0:T(8,128)(2,1)S(1)} %get-tuple-element.53.q_rows, bf16[2048,128]{1,0:T(8,128)(2,1)S(1)} %get-tuple-element.54.g_rows, f32[384,512]{1,0:T(8,128)S(1)} %get-tuple-element.55.bias), custom_call_target="tpu_custom_call" | custom-call | flops 2147483648 | bytes 2097152 | tf_op jit(solution)/shard_map/pallas_call | solution.py:136
  54.1 3.0 %collective-permute-start.10 = (f32[4,2048]{1,0:T(4,128)S(1)}, f32[4,2048]{1,0:T(4,128)S(1)}, u32[]{:S(2)}, u32[]{:S(2)}) collective-permute-start(f32[4,2048]{1,0:T(4,128)S(1)} %shard_map.98.st0), channel_id=1, source_target_pairs={{0,16},{8,24},{16,0},{24,8},{1,17},{9,25},{17,1},{25,9},{2,18},{10... | collective-permute-start | bytes 98312 | tf_op jit(solution)/shard_map/ppermute | solution.py:522
  57.1 0.8 collective-permute-start.11
  57.9 0.7 collective-permute-start.9
  58.5 1.7 %collective-permute-done.11.st3 = f32[4,2048]{1,0:T(4,128)S(1)} collective-permute-done((f32[4,2048]{1,0:T(4,128)S(1)}, f32[4,2048]{1,0:T(4,128)S(1)}, u32[]{:S(2)}, u32[]{:S(2)}) %collective-permute-start.11) | collective-permute-done | bytes 32800 | tf_op jit(solution)/shard_map/ppermute | solution.py:522
  60.2 1.6 %collective-permute-done.9.st1 = f32[4,2048]{1,0:T(4,128)S(1)} collective-permute-done((f32[4,2048]{1,0:T(4,128)S(1)}, f32[4,2048]{1,0:T(4,128)S(1)}, u32[]{:S(2)}, u32[]{:S(2)}) %collective-permute-start.9) | collective-permute-done | bytes 32800 | tf_op jit(solution)/shard_map/ppermute | solution.py:522
  61.9 3.8 %shard_map.99 = (bf16[16,128,256]{2,1,0:T(8,128)(2,1)}, bf16[128,512]{1,0:T(8,128)(2,1)}, bf16[128,512]{1,0:T(8,128)(2,1)}, bf16[128,512]{1,0:T(8,128)(2,1)}, bf16[128,512]{1,0:T(8,128)(2,1)}) custom-call(s32[5]{0:T(128)S(1)} %stack.23.place, bf16[2048,256]{1,0:T(8,128)(2,1)S(1)} %bitcast.8, bf16[2048,128]{1,0:T(8,128)(2,1)S(1)} %get-tuple-element.53.q_rows, ...), custom_call_target="tpu_custom_call" | custom-call | flops 5368709120 | bytes 4194304 | tf_op jit(solution)/shard_map/pallas_call | solution.py:136
  65.7 7.6 %collective-permute-done.12.got_kv = bf16[2,2048,128]{2,1,0:T(8,128)(2,1)} collective-permute-done((bf16[2,2048,128]{2,1,0:T(8,128)(2,1)}, bf16[2,2048,128]{2,1,0:T(8,128)(2,1)}, u32[]{:S(2)}, u32[]{:S(2)}) %collective-permute-start.12) | collective-permute-done | bytes 1048608 | tf_op jit(solution)/shard_map/ppermute | solution.py:448
  73.2 10.8 %all-to-all-start.1 = ((bf16[16,128,256]{2,1,0:T(8,128)(2,1)}), bf16[16,128,256]{2,1,0:T(8,128)(2,1)S(1)}, u32[]{:S(2)}, u32[]{:S(2)}) async-start(bf16[16,128,256]{2,1,0:T(8,128)(2,1)} %get-tuple-element.58), calls=%async_computation.1 | async-start | bytes 2097152 | tf_op jit(solution)/shard_map/all_to_all | solution.py:526
  84.0 1.5 %collective-permute-start.13 = (bf16[128,512]{1,0:T(8,128)(2,1)S(1)}, bf16[128,512]{1,0:T(8,128)(2,1)S(1)}, u32[]{:S(2)}, u32[]{:S(2)}) collective-permute-start(bf16[128,512]{1,0:T(8,128)(2,1)S(1)} %copy-done.4), channel_id=1, source_target_pairs={{0,24},{8,0},{16,8},{24,16},{1,25},{9,1},{17,9},{25,17},{2,26},{10... | collective-permute-start | bytes 393224 | tf_op jit(solution)/shard_map/ppermute | solution.py:527
  85.5 0.7 collective-permute-start.15
  86.2 1.7 %collective-permute-done.13.dq1 = bf16[128,512]{1,0:T(8,128)(2,1)S(1)} collective-permute-done((bf16[128,512]{1,0:T(8,128)(2,1)S(1)}, bf16[128,512]{1,0:T(8,128)(2,1)S(1)}, u32[]{:S(2)}, u32[]{:S(2)}) %collective-permute-start.13) | collective-permute-done | bytes 131104 | tf_op jit(solution)/shard_map/ppermute | solution.py:527
  87.9 3.0 %collective-permute-done.14.dq2 = bf16[128,512]{1,0:T(8,128)(2,1)S(1)} collective-permute-done((bf16[128,512]{1,0:T(8,128)(2,1)S(1)}, bf16[128,512]{1,0:T(8,128)(2,1)S(1)}, u32[]{:S(2)}, u32[]{:S(2)}) %collective-permute-start.14) | collective-permute-done | bytes 131104 | tf_op jit(solution)/shard_map/ppermute | solution.py:527
  90.9 1.4 %collective-permute-done.15.dq3 = bf16[128,512]{1,0:T(8,128)(2,1)S(1)} collective-permute-done((bf16[128,512]{1,0:T(8,128)(2,1)S(1)}, bf16[128,512]{1,0:T(8,128)(2,1)S(1)}, u32[]{:S(2)}, u32[]{:S(2)}) %collective-permute-start.15) | collective-permute-done | bytes 131104 | tf_op jit(solution)/shard_map/ppermute | solution.py:527
  92.3 2.8 %shard_map.100 = (bf16[128,1024]{1,0:T(8,128)(2,1)S(1)}, bf16[128,1024]{1,0:T(8,128)(2,1)S(1)}, bf16[128,512]{1,0:T(8,128)(2,1)S(1)}) custom-call(s32[5]{0:T(128)S(1)} %stack.23.place, bf16[128,512]{1,0:T(8,128)(2,1)S(1)} %copy-done.1, bf16[128,512]{1,0:T(8,128)(2,1)S(1)} %collective-permute-done.13.dq1, bf16[128,512]{1,0:T(8,128)(2,1)S(1)} %collective-permute-done.14.dq2, ...), custom_call_target="tpu_custom_call" | custom-call | flops 268435456 | bytes 2097152 | tf_op jit(solution)/shard_map/pallas_call | solution.py:136
  95.1 3.8 %collective-permute-start.16 = (bf16[128,1024]{1,0:T(8,128)(2,1)S(1)}, bf16[128,1024]{1,0:T(8,128)(2,1)S(1)}, u32[]{:S(2)}, u32[]{:S(2)}) collective-permute-start(bf16[128,1024]{1,0:T(8,128)(2,1)S(1)} %get-tuple-element.64), channel_id=1, source_target_pairs={{0,1},{1,0},{2,3},{3,2},{4,5},{5,4},{6,7},{7,6},{8,9},{9,8},{10,11... | collective-permute-start | bytes 786440 | tf_op jit(solution)/shard_map/ppermute | solution.py:445
  98.8 1.2 collective-permute-done.16
  100.0 0.8 add_convert_fusion.2
  100.7 2.8 %shard_map.101 = (bf16[128,1024]{1,0:T(8,128)(2,1)S(1)}, bf16[128,1024]{1,0:T(8,128)(2,1)S(1)}, bf16[2,2048,256]{2,1,0:T(8,128)(2,1)S(1)}) custom-call(s32[5]{0:T(128)S(1)} %stack.23.place, bf16[128,512]{1,0:T(8,128)(2,1)S(1)} %get-tuple-element.66.total, bf16[4096,512]{1,0:T(8,128)(2,1)} %wq.5, bf16[4096,128]{1,0:T(8,128)(2,1)} %wk.5, ...), custom_call_target="tpu_custom_call" | custom-call | flops 268435456 | bytes 4194304 | tf_op jit(solution)/shard_map/pallas_call | solution.py:136
  103.5 0.5 collective-permute-start.17
  104.3 0.8 collective-permute-done.17
  105.2 4.4 %all-to-all-done.1.parts = bf16[16,128,256]{2,1,0:T(8,128)(2,1)S(1)} async-done(((bf16[16,128,256]{2,1,0:T(8,128)(2,1)}), bf16[16,128,256]{2,1,0:T(8,128)(2,1)S(1)}, u32[]{:S(2)}, u32[]{:S(2)}) %all-to-all-start.1) | async-done | bytes 1048608 | tf_op jit(solution)/shard_map/all_to_all | solution.py:526
  109.6 1.3 %shard_map.102 = (bf16[128,128]{1,0:T(8,128)(2,1)}, bf16[128,128]{1,0:T(8,128)(2,1)}, bf16[128,256]{1,0:T(8,128)(2,1)S(1)}) custom-call(s32[5]{0:T(128)S(1)} %stack.23.place, bf16[16,128,256]{2,1,0:T(8,128)(2,1)S(1)} %all-to-all-done.1.parts), custom_call_target="tpu_custom_call" | custom-call | bytes 2097152 | tf_op jit(solution)/shard_map/pallas_call | solution.py:136
  111.0 4.1 %collective-permute-done.19.far_queries = bf16[128,1024]{1,0:T(8,128)(2,1)} collective-permute-done((bf16[128,1024]{1,0:T(8,128)(2,1)}, bf16[128,1024]{1,0:T(8,128)(2,1)}, u32[]{:S(2)}, u32[]{:S(2)}) %collective-permute-start.19) | collective-permute-done | bytes 262176 | tf_op jit(solution)/shard_map/ppermute | solution.py:448
  115.1 1.4 %shard_map.103 = (f32[128,1024]{1,0:T(8,128)S(1)}, f32[128,1024]{1,0:T(8,128)S(1)}) custom-call(s32[5]{0:T(128)S(1)} %stack.23.place, bf16[128,256]{1,0:T(8,128)(2,1)S(1)} %get-tuple-element.71.dkv, bf16[2,2048,256]{2,1,0:T(8,128)(2,1)S(1)} %get-tuple-element.72.weights, bf16[128,1024]{1,0:T(8,128)(2,1)S(1)} %add_convert_fusion.1.queries, ...), custom_call_target="tpu_custom_call" | custom-call | flops 134217728 | bytes 2097152 | tf_op jit(solution)/shard_map/pallas_call | solution.py:136
  116.5 0.9 shard_map.105
  117.4 3.8 %collective-permute-start.20 = (bf16[128,1024]{1,0:T(8,128)(2,1)S(1)}, bf16[128,1024]{1,0:T(8,128)(2,1)S(1)}, u32[]{:S(2)}, u32[]{:S(2)}) collective-permute-start(bf16[128,1024]{1,0:T(8,128)(2,1)S(1)} %shard_map.105), channel_id=1, source_target_pairs={{0,1},{1,0},{2,3},{3,2},{4,5},{5,4},{6,7},{7,6},{8,9},{9,8},{10,11... | collective-permute-start | bytes 786440 | tf_op jit(solution)/shard_map/ppermute | solution.py:445
  121.2 0.8 shard_map.104
  122.4 0.8 add_convert_fusion
  (24 shorter events, 1.3 us)
Async XLA Ops:
  0.6 4.7 %collective-permute-start.1 = (bf16[128,1024]{1,0:T(8,128)(2,1)}, bf16[128,1024]{1,0:T(8,128)(2,1)S(1)}, u32[]{:S(2)}, u32[]{:S(2)}) collective-permute-start(bf16[128,1024]{1,0:T(8,128)(2,1)} %x0.1), channel_id=1, source_target_pairs={{0,1},{1,0},{2,3},{3,2},{4,5},{5,4},{6,7},{7,6},{8,9},{9,8},{10,11... | collective-permute-start | bytes 786440 | tf_op jit(solution)/shard_map/ppermute | solution.py:445
  4.0 1.7 %collective-permute-start.2 = (bf16[128,1024]{1,0:T(8,128)(2,1)}, bf16[128,1024]{1,0:T(8,128)(2,1)S(1)}, u32[]{:S(2)}, u32[]{:S(2)}) collective-permute-start(bf16[128,1024]{1,0:T(8,128)(2,1)} %g0.1), channel_id=1, source_target_pairs={{0,1},{1,0},{2,3},{3,2},{4,5},{5,4},{6,7},{7,6},{8,9},{9,8},{10,11... | collective-permute-start | bytes 786440 | tf_op jit(solution)/shard_map/ppermute | solution.py:445
  4.1 7.8 %collective-permute-start = (bf16[128,1024]{1,0:T(8,128)(2,1)}, bf16[128,1024]{1,0:T(8,128)(2,1)S(1)}, u32[]{:S(2)}, u32[]{:S(2)}) collective-permute-start(bf16[128,1024]{1,0:T(8,128)(2,1)} %x0.1), channel_id=1, source_target_pairs={{0,2},{2,0},{1,3},{3,1},{4,6},{6,4},{5,7},{7,5},{8,10},{10,8},{9,1... | collective-permute-start | bytes 786440 | tf_op jit(solution)/shard_map/ppermute | solution.py:448
  5.7 0.9 copy-start
  11.9 2.3 %collective-permute-start.3 = (bf16[128,1024]{1,0:T(8,128)(2,1)S(1)}, bf16[128,1024]{1,0:T(8,128)(2,1)S(1)}, u32[]{:S(2)}, u32[]{:S(2)}) collective-permute-start(bf16[128,1024]{1,0:T(8,128)(2,1)S(1)} %collective-permute-done.x2), channel_id=1, source_target_pairs={{0,1},{1,0},{2,3},{3,2},{4,5},{5,4},{6,7},{7,6},{8,9},{9,8},{10,11... | collective-permute-start | bytes 786440 | tf_op jit(solution)/shard_map/ppermute | solution.py:445
  13.0 12.3 %collective-permute-start.4 = (bf16[128,1024]{1,0:T(8,128)(2,1)}, bf16[128,1024]{1,0:T(8,128)(2,1)S(1)}, u32[]{:S(2)}, u32[]{:S(2)}) collective-permute-start(bf16[128,1024]{1,0:T(8,128)(2,1)} %g0.1), channel_id=1, source_target_pairs={{0,2},{2,0},{1,3},{3,1},{4,6},{6,4},{5,7},{7,5},{8,10},{10,8},{9,1... | collective-permute-start | bytes 786440 | tf_op jit(solution)/shard_map/ppermute | solution.py:448
  16.2 36.2 %all-to-all-start = ((bf16[16,128,256]{2,1,0:T(8,128)(2,1)}), bf16[16,128,256]{2,1,0:T(8,128)(2,1)S(1)}, u32[]{:S(2)}, u32[]{:S(2)}) async-start(bf16[16,128,256]{2,1,0:T(8,128)(2,1)} %get-tuple-element.47), calls=%async_computation | async-start | bytes 2097152 | tf_op jit(solution)/shard_map/all_to_all | solution.py:501
  25.3 1.9 %collective-permute-start.5 = (bf16[128,1024]{1,0:T(8,128)(2,1)S(1)}, bf16[128,1024]{1,0:T(8,128)(2,1)S(1)}, u32[]{:S(2)}, u32[]{:S(2)}) collective-permute-start(bf16[128,1024]{1,0:T(8,128)(2,1)S(1)} %collective-permute-done.4.g2), channel_id=1, source_target_pairs={{0,1},{1,0},{2,3},{3,2},{4,5},{5,4},{6,7},{7,6},{8,9},{9,8},{10,11... | collective-permute-start | bytes 786440 | tf_op jit(solution)/shard_map/ppermute | solution.py:445
  30.0 9.2 %collective-permute-start.6 = (bf16[128,1024]{1,0:T(8,128)(2,1)}, bf16[128,1024]{1,0:T(8,128)(2,1)S(1)}, u32[]{:S(2)}, u32[]{:S(2)}) collective-permute-start(bf16[128,1024]{1,0:T(8,128)(2,1)} %shard_map.96.qd0), channel_id=1, source_target_pairs={{0,8},{8,16},{16,24},{24,0},{1,9},{9,17},{17,25},{25,1},{2,10},{10... | collective-permute-start | bytes 786440 | tf_op jit(solution)/shard_map/ppermute | solution.py:502
  31.4 14.5 %collective-permute-start.7 = (bf16[128,1024]{1,0:T(8,128)(2,1)}, bf16[128,1024]{1,0:T(8,128)(2,1)S(1)}, u32[]{:S(2)}, u32[]{:S(2)}) collective-permute-start(bf16[128,1024]{1,0:T(8,128)(2,1)} %shard_map.96.qd0), channel_id=1, source_target_pairs={{0,16},{8,24},{16,0},{24,8},{1,17},{9,25},{17,1},{25,9},{2,18},{10... | collective-permute-start | bytes 786440 | tf_op jit(solution)/shard_map/ppermute | solution.py:502
  34.0 11.9 %collective-permute-start.8 = (bf16[128,1024]{1,0:T(8,128)(2,1)}, bf16[128,1024]{1,0:T(8,128)(2,1)S(1)}, u32[]{:S(2)}, u32[]{:S(2)}) collective-permute-start(bf16[128,1024]{1,0:T(8,128)(2,1)} %shard_map.96.qd0), channel_id=1, source_target_pairs={{0,24},{8,0},{16,8},{24,16},{1,25},{9,1},{17,9},{25,17},{2,26},{10... | collective-permute-start | bytes 786440 | tf_op jit(solution)/shard_map/ppermute | solution.py:502
  48.8 24.4 %collective-permute-start.12 = (bf16[2,2048,128]{2,1,0:T(8,128)(2,1)}, bf16[2,2048,128]{2,1,0:T(8,128)(2,1)}, u32[]{:S(2)}, u32[]{:S(2)}) collective-permute-start(bf16[2,2048,128]{2,1,0:T(8,128)(2,1)} %get-tuple-element.57), channel_id=1, source_target_pairs={{0,2},{2,0},{1,3},{3,1},{4,6},{6,4},{5,7},{7,5},{8,10},{10,8},{9,1... | collective-permute-start | bytes 3145736 | tf_op jit(solution)/shard_map/ppermute | solution.py:448
  54.1 4.4 %collective-permute-start.10 = (f32[4,2048]{1,0:T(4,128)S(1)}, f32[4,2048]{1,0:T(4,128)S(1)}, u32[]{:S(2)}, u32[]{:S(2)}) collective-permute-start(f32[4,2048]{1,0:T(4,128)S(1)} %shard_map.98.st0), channel_id=1, source_target_pairs={{0,16},{8,24},{16,0},{24,8},{1,17},{9,25},{17,1},{25,9},{2,18},{10... | collective-permute-start | bytes 98312 | tf_op jit(solution)/shard_map/ppermute | solution.py:522
  57.1 3.2 %collective-permute-start.11 = (f32[4,2048]{1,0:T(4,128)S(1)}, f32[4,2048]{1,0:T(4,128)S(1)}, u32[]{:S(2)}, u32[]{:S(2)}) collective-permute-start(f32[4,2048]{1,0:T(4,128)S(1)} %shard_map.98.st0), channel_id=1, source_target_pairs={{0,24},{8,0},{16,8},{24,16},{1,25},{9,1},{17,9},{25,17},{2,26},{10... | collective-permute-start | bytes 98312 | tf_op jit(solution)/shard_map/ppermute | solution.py:522
  57.9 4.0 %collective-permute-start.9 = (f32[4,2048]{1,0:T(4,128)S(1)}, f32[4,2048]{1,0:T(4,128)S(1)}, u32[]{:S(2)}, u32[]{:S(2)}) collective-permute-start(f32[4,2048]{1,0:T(4,128)S(1)} %shard_map.98.st0), channel_id=1, source_target_pairs={{0,8},{8,16},{16,24},{24,0},{1,9},{9,17},{17,25},{25,1},{2,10},{10... | collective-permute-start | bytes 98312 | tf_op jit(solution)/shard_map/ppermute | solution.py:522
  65.6 18.4 %copy-start.4 = (bf16[128,512]{1,0:T(8,128)(2,1)S(1)}, bf16[128,512]{1,0:T(8,128)(2,1)}, u32[]{:S(2)}) copy-start(bf16[128,512]{1,0:T(8,128)(2,1)} %get-tuple-element.60) | copy-start | bytes 393220
  65.6 19.8 %copy-start.3 = (bf16[128,512]{1,0:T(8,128)(2,1)S(1)}, bf16[128,512]{1,0:T(8,128)(2,1)}, u32[]{:S(2)}) copy-start(bf16[128,512]{1,0:T(8,128)(2,1)} %get-tuple-element.61) | copy-start | bytes 393220
  65.6 19.8 %copy-start.2 = (bf16[128,512]{1,0:T(8,128)(2,1)S(1)}, bf16[128,512]{1,0:T(8,128)(2,1)}, u32[]{:S(2)}) copy-start(bf16[128,512]{1,0:T(8,128)(2,1)} %get-tuple-element.62) | copy-start | bytes 393220
  65.7 26.6 %copy-start.1 = (bf16[128,512]{1,0:T(8,128)(2,1)S(1)}, bf16[128,512]{1,0:T(8,128)(2,1)}, u32[]{:S(2)}) copy-start(bf16[128,512]{1,0:T(8,128)(2,1)} %get-tuple-element.59.dq0) | copy-start | bytes 393220
  73.2 36.4 %all-to-all-start.1 = ((bf16[16,128,256]{2,1,0:T(8,128)(2,1)}), bf16[16,128,256]{2,1,0:T(8,128)(2,1)S(1)}, u32[]{:S(2)}, u32[]{:S(2)}) async-start(bf16[16,128,256]{2,1,0:T(8,128)(2,1)} %get-tuple-element.58), calls=%async_computation.1 | async-start | bytes 2097152 | tf_op jit(solution)/shard_map/all_to_all | solution.py:526
  84.0 3.9 %collective-permute-start.13 = (bf16[128,512]{1,0:T(8,128)(2,1)S(1)}, bf16[128,512]{1,0:T(8,128)(2,1)S(1)}, u32[]{:S(2)}, u32[]{:S(2)}) collective-permute-start(bf16[128,512]{1,0:T(8,128)(2,1)S(1)} %copy-done.4), channel_id=1, source_target_pairs={{0,24},{8,0},{16,8},{24,16},{1,25},{9,1},{17,9},{25,17},{2,26},{10... | collective-permute-start | bytes 393224 | tf_op jit(solution)/shard_map/ppermute | solution.py:527
  85.5 5.4 %collective-permute-start.14 = (bf16[128,512]{1,0:T(8,128)(2,1)S(1)}, bf16[128,512]{1,0:T(8,128)(2,1)S(1)}, u32[]{:S(2)}, u32[]{:S(2)}) collective-permute-start(bf16[128,512]{1,0:T(8,128)(2,1)S(1)} %copy-done.3), channel_id=1, source_target_pairs={{0,16},{8,24},{16,0},{24,8},{1,17},{9,25},{17,1},{25,9},{2,18},{10... | collective-permute-start | bytes 393224 | tf_op jit(solution)/shard_map/ppermute | solution.py:527
  85.5 6.8 %collective-permute-start.15 = (bf16[128,512]{1,0:T(8,128)(2,1)S(1)}, bf16[128,512]{1,0:T(8,128)(2,1)S(1)}, u32[]{:S(2)}, u32[]{:S(2)}) collective-permute-start(bf16[128,512]{1,0:T(8,128)(2,1)S(1)} %copy-done.2), channel_id=1, source_target_pairs={{0,8},{8,16},{16,24},{24,0},{1,9},{9,17},{17,25},{25,1},{2,10},{10... | collective-permute-start | bytes 393224 | tf_op jit(solution)/shard_map/ppermute | solution.py:527
  95.1 4.9 %collective-permute-start.16 = (bf16[128,1024]{1,0:T(8,128)(2,1)S(1)}, bf16[128,1024]{1,0:T(8,128)(2,1)S(1)}, u32[]{:S(2)}, u32[]{:S(2)}) collective-permute-start(bf16[128,1024]{1,0:T(8,128)(2,1)S(1)} %get-tuple-element.64), channel_id=1, source_target_pairs={{0,1},{1,0},{2,3},{3,2},{4,5},{5,4},{6,7},{7,6},{8,9},{9,8},{10,11... | collective-permute-start | bytes 786440 | tf_op jit(solution)/shard_map/ppermute | solution.py:445
  103.5 1.6 %collective-permute-start.17 = (bf16[128,1024]{1,0:T(8,128)(2,1)S(1)}, bf16[128,1024]{1,0:T(8,128)(2,1)S(1)}, u32[]{:S(2)}, u32[]{:S(2)}) collective-permute-start(bf16[128,1024]{1,0:T(8,128)(2,1)S(1)} %get-tuple-element.69), channel_id=1, source_target_pairs={{0,1},{1,0},{2,3},{3,2},{4,5},{5,4},{6,7},{7,6},{8,9},{9,8},{10,11... | collective-permute-start | bytes 786440 | tf_op jit(solution)/shard_map/ppermute | solution.py:445
  104.0 11.0 %collective-permute-start.19 = (bf16[128,1024]{1,0:T(8,128)(2,1)}, bf16[128,1024]{1,0:T(8,128)(2,1)}, u32[]{:S(2)}, u32[]{:S(2)}) collective-permute-start(bf16[128,1024]{1,0:T(8,128)(2,1)} %add_convert_fusion.2), channel_id=1, source_target_pairs={{0,2},{2,0},{1,3},{3,1},{4,6},{6,4},{5,7},{7,5},{8,10},{10,8},{9,1... | collective-permute-start | bytes 786440 | tf_op jit(solution)/shard_map/ppermute | solution.py:448
  111.0 5.5 %collective-permute-start.18 = (bf16[128,256]{1,0:T(8,128)(2,1)S(1)}, bf16[128,256]{1,0:T(8,128)(2,1)S(1)}, u32[]{:S(2)}, u32[]{:S(2)}) collective-permute-start(bf16[128,256]{1,0:T(8,128)(2,1)S(1)} %get-tuple-element.71.dkv), channel_id=1, source_target_pairs={{0,2},{2,0},{1,3},{3,1},{4,6},{6,4},{5,7},{7,5},{8,10},{10,8},{9,1... | collective-permute-start | bytes 196616 | tf_op jit(solution)/shard_map/ppermute | solution.py:448
  117.4 5.0 %collective-permute-start.20 = (bf16[128,1024]{1,0:T(8,128)(2,1)S(1)}, bf16[128,1024]{1,0:T(8,128)(2,1)S(1)}, u32[]{:S(2)}, u32[]{:S(2)}) collective-permute-start(bf16[128,1024]{1,0:T(8,128)(2,1)S(1)} %shard_map.105), channel_id=1, source_target_pairs={{0,1},{1,0},{2,3},{3,2},{4,5},{5,4},{6,7},{7,6},{8,9},{9,8},{10,11... | collective-permute-start | bytes 786440 | tf_op jit(solution)/shard_map/ppermute | solution.py:445
